TPU v7x, 128 devices: a whole 4x4x4 slice. The times are simulated.
128 devices in a mesh: pair: 32 (over x, z, y_hi), win: 4 (over y_lo, core).
Axes of the slice: x: 4, y: 4 (y_hi: 2, y_lo: 2; y = y_hi * 2 + y_lo), z: 4, core: 2. Of those that a mesh axis runs over, the one named last changes fastest.
Arguments:
- spectra: bfloat16 [32, 2, 384, 8192], P(None, None, 'win', 'pair'), may hold values from -6 to 6
- channel_order: int32 [32, 256], P('pair'), may hold values from 0 to 255, each once within a row
- partners: int32 [4, 32], replicated, may hold values from 0 to 31, as said below
Outputs:
- stacks: float32 [32, 256, 4, 16, 256], P('pair', 'win')
Inputs may be any that keep to these rules, and one draw needn't show every extreme that they name: For every round r and block b, partners[r, b] differs from b and partners[r, partners[r, b]] = b; no two rounds match the same two blocks. `channel_order`: each row lists every slot once.
All inputs are finite; a program needn't handle non-finite values.
Results may differ from a plain program's by a relative error of at most 0.004.
Values may be sent and summed in bfloat16 or wider, within the bound.
No kernel may reach another device: no remote copies, remote signals or barrier semaphores. Data moves between devices by JAX's collectives and lax.ppermute only.
A program may use at most 128 MiB of HBM per device.

v0:
```python
import math

import jax
import jax.numpy as jnp
from jax import lax
from jax.sharding import PartitionSpec as P

LAGS = 16
ROUNDS = 4


def whiten(spectra):
    values = spectra.astype(jnp.float32)
    band_power = values[:, 0] * values[:, 0] + values[:, 1] * values[:, 1]
    num_bins = band_power.shape[0]
    padded = jnp.pad(band_power, ((2, 2), (0, 0), (0, 0)))
    band_total = (
        padded[0:num_bins]
        + padded[1 : num_bins + 1]
        + padded[2 : num_bins + 2]
        + padded[3 : num_bins + 3]
        + padded[4 : num_bins + 4]
    )
    bin_index = jnp.arange(num_bins, dtype=jnp.int32)
    counts = (jnp.minimum(bin_index + 2, num_bins - 1) - jnp.maximum(bin_index - 2, 0) + 1).astype(
        jnp.float32
    )
    band_mean = band_total / counts[:, None, None]
    inv_scale = 1.0 / jnp.maximum(jnp.sqrt(band_mean), 0.5)
    return (values * inv_scale[:, None]).astype(jnp.bfloat16)


def make_table(num_bins, num_lags, window_total):
    bin_freq = jnp.arange(num_bins, dtype=jnp.float32)[:, None]
    lag_index = (jnp.arange(num_lags, dtype=jnp.int32) - num_lags // 2).astype(jnp.float32)[None, :]
    phase_angle = math.pi * bin_freq * lag_index / num_bins
    norm_factor = 1.0 / math.sqrt(window_total * num_bins)
    return jnp.concatenate([jnp.cos(phase_angle), -jnp.sin(phase_angle)], 0) * norm_factor


def prepare(mate_block):
    num_bins, _, num_windows, num_cols = mate_block.shape
    right_real = mate_block.reshape(num_bins, 2 * num_windows, num_cols)
    right_turned = jnp.concatenate([mate_block[:, 1], -mate_block[:, 0]], axis=1)
    return (right_real, right_turned)


def correlate(own_block, mate_pair, lag_table, row_count):
    num_bins, _, num_windows, _ = own_block.shape
    left_rows = own_block.reshape(num_bins, 2 * num_windows, row_count)
    cross_real = jnp.einsum(
        "fki,fkj->fij", left_rows, mate_pair[0], preferred_element_type=jnp.float32
    )
    cross_imag = jnp.einsum(
        "fki,fkj->fij", left_rows, mate_pair[1], preferred_element_type=jnp.float32
    )
    stacked = jnp.concatenate([cross_real, cross_imag], 0)
    return jnp.einsum("gl,gij->ilj", lag_table, stacked, precision=lax.Precision.HIGHEST)


def local(spectra, channel_order, partners):
    whitened = whiten(spectra)
    own_block = jnp.take(whitened, channel_order[0], axis=3)
    num_blocks = lax.axis_size("pair")
    win_count = lax.axis_size("win")
    window_total = spectra.shape[2] * win_count
    lag_table = make_table(spectra.shape[0], LAGS, window_total)
    own_pieces = own_block.reshape(num_blocks, -1)
    share_rows = own_block.shape[3] // win_count
    turned = lax.all_to_all(own_pieces, "pair", split_axis=0, concat_axis=0, tiled=True)
    results = []
    for turn_index in range(ROUNDS):
        arranged = jnp.take(turned, partners[turn_index], axis=0)
        received = lax.all_to_all(arranged, "pair", split_axis=0, concat_axis=0, tiled=True)
        mate_pair = prepare(received.reshape(own_block.shape))

        def term_rows(first_row, row_count, mate_pair=mate_pair):
            return correlate(own_block, mate_pair, lag_table, row_count)

        results.append(
            lax.psum_scatter(
                term_rows(jnp.int32(0), share_rows * lax.axis_size("win")),
                "win",
                scatter_dimension=0,
                tiled=True,
            )
        )
    stacks = jnp.stack(results, 1)
    return stacks[None]


def solution(mesh):
    return jax.shard_map(
        local,
        mesh=mesh,
        in_specs=(P(None, None, "win", "pair"), P("pair", None), P()),
        out_specs=P("pair", "win", None, None, None),
        check_vma=False,
    )
```

profile of v0, /device:TPU:16, one launch (start us, length us, event | category | flops | bytes accessed | tf_op | source)
XLA Modules:
  0.0 740.2 jit_solution(11196014802949244184)
XLA Ops:
  6.5 7.6 %copy.60 = bf16[32,2,96,256]{2,0,3,1:T(8,128)(2,1)} copy(bf16[32,2,96,256]{3,2,1,0:T(8,128)(2,1)} %param.5) | data formatting | bytes 6291456 | tf_op args[0]
  25.1 5.2 gather_fusion
  30.3 5.8 copy.61
  46.5 5.4 reshape.209
  52.0 11.4 %all-to-all-start = ((bf16[32,2,24576]{2,1,0:T(2,128)(2,1)}), bf16[32,2,24576]{2,1,0:T(2,128)(2,1)S(1)}, u32[]{:S(2)}, u32[]{:S(2)}) async-start(bf16[32,2,24576]{2,1,0:T(2,128)(2,1)} %reshape.209), calls=%async_computation | async-start | bytes 6291456 | tf_op jit(solution)/shard_map/all_to_all | solution.py:70
  63.4 42.0 %all-to-all-done = bf16[32,2,24576]{2,1,0:T(2,128)(2,1)S(1)} async-done(((bf16[32,2,24576]{2,1,0:T(2,128)(2,1)}), bf16[32,2,24576]{2,1,0:T(2,128)(2,1)S(1)}, u32[]{:S(2)}, u32[]{:S(2)}) %all-to-all-start) | async-done | bytes 3145760 | tf_op jit(solution)/shard_map/all_to_all | solution.py:70
  105.4 12.5 %reshape.210 = bf16[32,1,49152]{2,1,0:T(2,128)(2,1)} reshape(bf16[32,2,24576]{2,1,0:T(2,128)(2,1)S(1)} %all-to-all-done) | data formatting | bytes 6291456
  117.9 6.2 copy.115
  128.4 4.3 gather_fusion.2
  132.7 6.1 select_bitcast_fusion.2
  138.8 5.8 reduce.12
  144.6 5.4 reshape.217
  150.0 7.1 all-to-all-start.1
  161.8 37.8 %all-to-all-done.1 = bf16[32,2,24576]{2,1,0:T(2,128)(2,1)} async-done(((bf16[32,2,24576]{2,1,0:T(2,128)(2,1)}), bf16[32,2,24576]{2,1,0:T(2,128)(2,1)}, u32[]{:S(2)}, u32[]{:S(2)}) %all-to-all-start.1) | async-done | bytes 3145760 | tf_op jit(solution)/shard_map/all_to_all | solution.py:74
  199.5 18.9 %reshape.218 = bf16[32,1,49152]{2,1,0:T(2,128)(2,1)} reshape(bf16[32,2,24576]{2,1,0:T(2,128)(2,1)} %all-to-all-done.1) | data formatting | bytes 6291456
  218.4 20.0 %reduce = bf16[32,49152]{1,0:T(8,128)(2,1)} reduce(bf16[32,1,49152]{2,1,0:T(2,128)(2,1)} %reshape.218, bf16[]{:T(256)} %constant.55), dimensions={1}, to_apply=%all_to_all.33.reduce_sub_computation | reduce | bytes 6291458 | tf_op jit(solution)/shard_map/all_to_all | solution.py:74
  244.3 4.6 fusion.16
  249.0 4.8 pad_maximum_fusion
  253.7 16.5 %fusion.32 = f32[256,16,256]{2,1,0:T(8,128)} fusion(f32[64,16,1]{0,1,2:T(8,128)S(1)} %fusion.52, f32[64,256,256]{2,1,0:T(8,128)S(1)} %pad_maximum_fusion), kind=kOutput, calls=%fused_computation.57 | convolution fusion | flops 805306368 | bytes 20975616 | tf_op jit(solution)/shard_map/gl,gij->ilj/dot_general | solution.py:58
  270.3 5.7 reduce.11
  276.0 5.4 reshape.215
  281.4 7.2 all-to-all-start.2
  288.9 4.4 gather_fusion.3
  293.3 4.3 gather_fusion.4
  297.6 34.4 %all-to-all-done.2 = bf16[32,2,24576]{2,1,0:T(2,128)(2,1)} async-done(((bf16[32,2,24576]{2,1,0:T(2,128)(2,1)}), bf16[32,2,24576]{2,1,0:T(2,128)(2,1)}, u32[]{:S(2)}, u32[]{:S(2)}) %all-to-all-start.2) | async-done | bytes 3145760 | tf_op jit(solution)/shard_map/all_to_all | solution.py:74
  331.9 19.0 %reshape.216 = bf16[32,1,49152]{2,1,0:T(2,128)(2,1)} reshape(bf16[32,2,24576]{2,1,0:T(2,128)(2,1)} %all-to-all-done.2) | data formatting | bytes 6291456
  350.9 18.3 %reduce.2 = bf16[32,49152]{1,0:T(8,128)(2,1)S(1)} reduce(bf16[32,1,49152]{2,1,0:T(2,128)(2,1)} %reshape.216, bf16[]{:T(256)} %constant.55), dimensions={1}, to_apply=%all_to_all.35.reduce_sub_computation | reduce | bytes 6291458 | tf_op jit(solution)/shard_map/all_to_all | solution.py:74
  373.2 4.6 fusion.64
  377.9 4.8 pad_maximum_fusion.1
  382.7 16.8 %fusion.35 = f32[256,16,256]{2,1,0:T(8,128)} fusion(f32[64,16,1]{0,1,2:T(8,128)S(1)} %fusion.52, f32[64,256,256]{2,1,0:T(8,128)S(1)} %pad_maximum_fusion.1), kind=kOutput, calls=%fused_computation.58 | convolution fusion | flops 805306368 | bytes 20975616 | tf_op jit(solution)/shard_map/gl,gij->ilj/dot_general | solution.py:58
  399.6 6.2 select_bitcast_fusion
  405.9 5.7 reduce.10
  411.5 5.5 reshape.213
  417.0 57.5 %all_to_all.45 = bf16[32,2,24576]{2,1,0:T(2,128)(2,1)} all-to-all(bf16[32,2,24576]{2,1,0:T(2,128)(2,1)} %reshape.213), channel_id=1, replica_groups=mesh['pair'=32,'win'=4] {'pair'}, dimensions={0} | all-to-all | bytes 6291456 | tf_op jit(solution)/shard_map/all_to_all | solution.py:74
  474.5 19.0 %reshape.214 = bf16[32,1,49152]{2,1,0:T(2,128)(2,1)} reshape(bf16[32,2,24576]{2,1,0:T(2,128)(2,1)} %all_to_all.45) | data formatting | bytes 6291456
  493.5 20.0 %reduce.4 = bf16[32,49152]{1,0:T(8,128)(2,1)} reduce(bf16[32,1,49152]{2,1,0:T(2,128)(2,1)} %reshape.214, bf16[]{:T(256)} %constant.55), dimensions={1}, to_apply=%all_to_all.37.reduce_sub_computation | reduce | bytes 6291458 | tf_op jit(solution)/shard_map/all_to_all | solution.py:74
  517.7 4.7 fusion.65
  522.4 4.8 pad_maximum_fusion.2
  527.2 16.4 %fusion.38 = f32[256,16,256]{2,1,0:T(8,128)} fusion(f32[64,16,1]{0,1,2:T(8,128)S(1)} %fusion.52, f32[64,256,256]{2,1,0:T(8,128)S(1)} %pad_maximum_fusion.2), kind=kOutput, calls=%fused_computation.59 | convolution fusion | flops 805306368 | bytes 20975616 | tf_op jit(solution)/shard_map/gl,gij->ilj/dot_general | solution.py:58
  543.7 5.7 reduce.9
  549.4 5.4 reshape.211
  554.8 53.9 %all_to_all.46 = bf16[32,2,24576]{2,1,0:T(2,128)(2,1)} all-to-all(bf16[32,2,24576]{2,1,0:T(2,128)(2,1)} %reshape.211), channel_id=1, replica_groups=mesh['pair'=32,'win'=4] {'pair'}, dimensions={0} | all-to-all | bytes 6291456 | tf_op jit(solution)/shard_map/all_to_all | solution.py:74
  608.7 18.9 %reshape.212 = bf16[32,1,49152]{2,1,0:T(2,128)(2,1)} reshape(bf16[32,2,24576]{2,1,0:T(2,128)(2,1)} %all_to_all.46) | data formatting | bytes 6291456
  627.6 20.0 %reduce.6 = bf16[32,49152]{1,0:T(8,128)(2,1)} reduce(bf16[32,1,49152]{2,1,0:T(2,128)(2,1)} %reshape.212, bf16[]{:T(256)} %constant.55), dimensions={1}, to_apply=%all_to_all.39.reduce_sub_computation | reduce | bytes 6291458 | tf_op jit(solution)/shard_map/all_to_all | solution.py:74
  651.9 4.6 fusion.66
  656.5 4.8 pad_maximum_fusion.3
  661.3 16.6 %fusion.41 = f32[256,16,256]{2,1,0:T(8,128)} fusion(f32[64,16,1]{0,1,2:T(8,128)S(1)} %fusion.52, f32[64,256,256]{2,1,0:T(8,128)S(1)} %pad_maximum_fusion.3), kind=kOutput, calls=%fused_computation.60 | convolution fusion | flops 805306368 | bytes 20975616 | tf_op jit(solution)/shard_map/gl,gij->ilj/dot_general | solution.py:58
  678.0 50.0 %reduce-scatter.11.cloned.1.call-done = f32[64,16,256]{2,1,0:T(8,128)} async-done(((f32[256,16,256]{2,1,0:T(8,128)}), f32[64,16,256]{2,1,0:T(8,128)}) %reduce-scatter.11.cloned.1.call-update) | async-done | bytes 1048592 | tf_op jit(solution)/shard_map/reduce_scatter | solution.py:81
  (66 shorter events, 54.2 us)
Async XLA Ops:
  18.6 3.5 copy-start.2
  22.1 3.0 copy-start.5
  36.1 3.4 copy-start.3
  52.0 11.4 %copy-start.4 = (s32[4,32]{1,0:T(4,128)S(1)}, s32[4,32]{1,0:T(4,128)}, u32[]{:S(2)}) copy-start(s32[4,32]{1,0:T(4,128)} %param.7) | copy-start | bytes 1540
  52.0 53.4 %all-to-all-start = ((bf16[32,2,24576]{2,1,0:T(2,128)(2,1)}), bf16[32,2,24576]{2,1,0:T(2,128)(2,1)S(1)}, u32[]{:S(2)}, u32[]{:S(2)}) async-start(bf16[32,2,24576]{2,1,0:T(2,128)(2,1)} %reshape.209), calls=%async_computation | async-start | bytes 6291456 | tf_op jit(solution)/shard_map/all_to_all | solution.py:70
  150.0 49.5 %all-to-all-start.1 = ((bf16[32,2,24576]{2,1,0:T(2,128)(2,1)}), bf16[32,2,24576]{2,1,0:T(2,128)(2,1)}, u32[]{:S(2)}, u32[]{:S(2)}) async-start(bf16[32,2,24576]{2,1,0:T(2,128)(2,1)} %reshape.217), calls=%async_computation.1 | async-start | bytes 6291456 | tf_op jit(solution)/shard_map/all_to_all | solution.py:74
  157.1 520.8 %reduce-scatter.5.cloned.1.call-start = ((), (), s32[]{:S(2)}) async-start(), calls=%async_computation.9 | async-start | bytes 5242880 | tf_op jit(solution)/shard_map/reduce_scatter | solution.py:81
  241.1 1.9 copy-start
  281.4 50.5 %all-to-all-start.2 = ((bf16[32,2,24576]{2,1,0:T(2,128)(2,1)}), bf16[32,2,24576]{2,1,0:T(2,128)(2,1)}, u32[]{:S(2)}, u32[]{:S(2)}) async-start(bf16[32,2,24576]{2,1,0:T(2,128)(2,1)} %reshape.215), calls=%async_computation.3 | async-start | bytes 6291456 | tf_op jit(solution)/shard_map/all_to_all | solution.py:74
  288.6 389.4 %reduce-scatter.7.cloned.1.call-start = ((), (), s32[]{:S(2)}) async-start(), calls=%async_computation.10 | async-start | bytes 5242880 | tf_op jit(solution)/shard_map/reduce_scatter | solution.py:81
  370.0 1.9 copy-start.1
  399.6 278.4 %reduce-scatter.9.cloned.1.call-start = ((), (), s32[]{:S(2)}) async-start(), calls=%async_computation.11 | async-start | bytes 5242880 | tf_op jit(solution)/shard_map/reduce_scatter | solution.py:81
  543.6 184.3 %reduce-scatter.11.cloned.1.call-start = ((), (), s32[]{:S(2)}) async-start(), calls=%async_computation.12 | async-start | bytes 5242880 | tf_op jit(solution)/shard_map/reduce_scatter | solution.py:81
Sparse Core Ops, SparseCore 0:
  270.4 82.3 reduce-scatter.4
  399.7 88.0 reduce-scatter.6
  543.8 83.6 reduce-scatter.8
  678.0 49.8 reduce-scatter.10
where the time goes:
time: 754 us; the launch traced here: 740 us
  local copies, waits for them, and re-layouts  177 us (23%)
  waiting for transfers between devices  164 us (22%)
  other arithmetic  157 us (21%)
  blocking collectives  111 us (15%)
  matrix products  90.2 us (12%)
  starting transfers between devices  26.4 us (4%)
  between operations  14 us (2%)
    unnamed x28, local copies, waits for them, and re-layouts  141 us
    all_to_all x10, other arithmetic, local(): lax.all_to_all(arranged, 'pair', split_axis=0, concat_axis=0, tiled=True)  114 us
    all_to_all x2, blocking collectives, local(): lax.all_to_all(arranged, 'pair', split_axis=0, concat_axis=0, tiled=True)  111 us
    all_to_all x2, waiting for transfers between devices, local(): lax.all_to_all(arranged, 'pair', split_axis=0, concat_axis=0, tiled=True)  72.1 us
    dot_general x4, matrix products, correlate(): jnp.einsum('gl,gij->ilj', lag_table, stacked, precision=lax.Precision.HIG...  66.3 us
    reduce_scatter x4, waiting for transfers between devices, local(): lax.psum_scatter(term_rows(jnp.int32(0), share_rows * lax.axis_size('win'...  50 us
    all_to_all x1, waiting for transfers between devices, local(): lax.all_to_all(own_pieces, 'pair', split_axis=0, concat_axis=0, tiled=True)  42 us
    concatenate x4, other arithmetic, correlate(): stacked = jnp.concatenate([cross_real, cross_imag], 0)  19.3 us
  transfers between devices with their start and end apart: 7, of which 4 were waited for; matrix products, arithmetic and copies ran while one was open for 35% of the time, Pallas kernels for 0%

commit v1 on v0

v1 whole, which is shorter than its diff:
```python
import functools
import math

import jax
import jax.numpy as jnp
from jax import lax
from jax.experimental import pallas as pl
from jax.experimental.pallas import tpu as pltpu
from jax.sharding import PartitionSpec as P

LAGS = 16
ROUNDS = 4
VMEM_BYTES = 56 * 1024 * 1024
QUARTER_ORDER = (0, 2, 1, 3)
bf16 = jnp.bfloat16
f32 = jnp.float32


def params(**more):
    return pltpu.CompilerParams(vmem_limit_bytes=VMEM_BYTES, **more)


def whiten_kernel(order_ref, spectra_ref, out_ref):
    num_bins, _, rows, cols = spectra_ref.shape
    slots = lax.broadcasted_iota(jnp.int32, (cols, cols), 0)
    pick = (slots == order_ref[...]).astype(f32).astype(bf16)
    values = spectra_ref[...].astype(f32)
    power = values[:, 0] * values[:, 0] + values[:, 1] * values[:, 1]
    parts = []
    for f in range(num_bins):
        lo, hi = max(f - 2, 0), min(f + 2, num_bins - 1)
        total = power[lo]
        for g in range(lo + 1, hi + 1):
            total = total + power[g]
        inv_scale = jnp.minimum(lax.rsqrt(total * (1.0 / (hi - lo + 1))), 2.0)
        parts.append((values[f] * inv_scale[None]).astype(bf16).reshape(2 * rows, cols))
    flat = jnp.concatenate(parts, 0)
    ordered = jnp.dot(flat, pick, preferred_element_type=f32).astype(bf16)
    out_ref[...] = ordered.reshape(num_bins, 2, rows, cols)


def whiten(spectra, channel_order):
    num_bins, _, num_windows, cols = spectra.shape
    rows = 16
    return pl.pallas_call(
        whiten_kernel,
        grid=(num_windows // rows,),
        out_shape=jax.ShapeDtypeStruct(spectra.shape, bf16),
        in_specs=[
            pl.BlockSpec((1, cols), lambda s: (0, 0)),
            pl.BlockSpec((num_bins, 2, rows, cols), lambda s: (0, 0, s, 0)),
        ],
        out_specs=pl.BlockSpec((num_bins, 2, rows, cols), lambda s: (0, 0, s, 0)),
        compiler_params=params(),
        name="whiten",
    )(channel_order, spectra)


def turn_kernel(own_ref, out_ref):
    bins, depth, cols = own_ref.shape
    half = depth // 2
    quarter = cols // 4
    for f in range(bins):
        block = own_ref[f].astype(f32)
        plain = block.T.astype(bf16)
        turned = jnp.concatenate([-block[half:], block[:half]], 0).T.astype(bf16)
        for place, source in enumerate(QUARTER_ORDER):
            rows = slice(source * quarter, (source + 1) * quarter)
            out_ref[f, place * quarter : (place + 1) * quarter, :] = plain[rows]
            out_ref[f, cols + place * quarter : cols + (place + 1) * quarter, :] = turned[rows]


def turn(own_rows):
    num_bins, depth, cols = own_rows.shape
    bins = 4
    return pl.pallas_call(
        turn_kernel,
        grid=(num_bins // bins,),
        out_shape=jax.ShapeDtypeStruct((num_bins, 2 * cols, depth), bf16),
        in_specs=[pl.BlockSpec((bins, depth, cols), lambda s: (s, 0, 0))],
        out_specs=pl.BlockSpec((bins, 2 * cols, depth), lambda s: (s, 0, 0)),
        compiler_params=params(),
        cost_estimate=pl.CostEstimate(flops=0, bytes_accessed=12_000_000, transcendentals=0),
        name="turn",
    )(own_rows)


def gather_kernel(index_ref, source_ref, out_ref, sems):
    count = out_ref.shape[0]
    copies = []
    for place in range(count):
        copy = pltpu.make_async_copy(
            source_ref.at[index_ref[place]], out_ref.at[place], sems.at[place]
        )
        copy.start()
        copies.append(copy)
    for copy in copies:
        copy.wait()


def gather(source, index):
    return pl.pallas_call(
        gather_kernel,
        out_shape=jax.ShapeDtypeStruct((index.shape[0],) + source.shape[1:], source.dtype),
        in_specs=[pl.BlockSpec(memory_space=pltpu.SMEM), pl.BlockSpec(memory_space=pl.ANY)],
        out_specs=pl.BlockSpec(memory_space=pl.ANY),
        scratch_shapes=[pltpu.SemaphoreType.DMA((index.shape[0],))],
        compiler_params=pltpu.CompilerParams(),
        name="gather",
    )(index, source)


def weighted(terms):
    total = None
    for weight, value in terms:
        if abs(weight) < 1e-12:
            continue
        term = value * weight
        total = term if total is None else total + term
    return total


def lag_sums(real, imag, norm):
    cosine = lambda f, t: math.cos(math.pi * f * t / 32) * norm
    sine = lambda f, t: -math.sin(math.pi * f * t / 32) * norm
    even, odd = {}, {}
    low = {0: real(0), 16: real(16)}
    diff = {0: low[0]}
    for f in range(1, 16):
        a, b = real(f), real(32 - f)
        low[f], diff[f] = a + b, a - b
    for t in (1, 3, 5, 7):
        even[t] = weighted([(cosine(f, t), diff[f]) for f in range(16)])
    minus = {f: low[f] - low[16 - f] for f in range(8)}
    for t in (2, 6):
        even[t] = weighted([(cosine(f, t), minus[f]) for f in range(8)])
    plus = {f: low[f] + low[16 - f] for f in range(8)}
    plus[8] = low[8]
    even[4] = weighted([(cosine(f, 4), plus[f] - plus[8 - f]) for f in range(4)])
    sums = {f: plus[f] + plus[8 - f] for f in range(4)}
    sums[4] = plus[4]
    even[8] = weighted([(cosine(f, 8), sums[f]) for f in range(5)])
    total = sums[0]
    for f in range(1, 5):
        total = total + sums[f]
    even[0] = total * norm

    add = {16: imag(16)}
    sub = {}
    for f in range(1, 16):
        a, b = imag(f), imag(32 - f)
        add[f], sub[f] = a + b, a - b
    for t in (1, 3, 5, 7):
        odd[t] = weighted([(sine(f, t), add[f]) for f in range(1, 17)])
    sums = {f: sub[f] + sub[16 - f] for f in range(1, 8)}
    sums[8] = sub[8]
    for t in (2, 6):
        odd[t] = weighted([(sine(f, t), sums[f]) for f in range(1, 9)])
    minus = {f: sub[f] - sub[16 - f] for f in range(1, 8)}
    odd[4] = weighted(
        [(sine(f, 4), minus[f] + minus[8 - f]) for f in range(1, 4)] + [(sine(4, 4), minus[4])]
    )
    odd[8] = weighted([(sine(f, 8), minus[f] - minus[8 - f]) for f in range(1, 4)])
    return even, odd


def correlate_kernel(norm, core_ref, own_ref, mate_ref, keep_ref, send_ref, cross):
    step = pl.program_id(0)
    bins = own_ref.shape[0]
    for f in range(bins):
        cross[step * bins + f] = jnp.dot(own_ref[f], mate_ref[f], preferred_element_type=f32)

    @pl.when(step == pl.num_programs(0) - 1)
    def _():
        lags, half, cols = keep_ref.shape
        core = core_ref[0]
        rows, lanes = 16, 128

        def part(out_ref, base):
            def body(chunk, carry):
                row = pl.multiple_of(chunk * rows, rows)
                for lane in range(0, cols, lanes):
                    where = pl.ds(pl.multiple_of(base + row, rows), rows)
                    turned = pl.ds(pl.multiple_of(2 * half + base + row, rows), rows)
                    even, odd = lag_sums(
                        lambda f: cross[f, where, lane : lane + lanes],
                        lambda f: cross[f, turned, lane : lane + lanes],
                        norm,
                    )
                    for lag in range(lags):
                        t = lag - LAGS // 2
                        if t == 0:
                            value = even[0]
                        elif t > 0:
                            value = even[t] + odd[t]
                        else:
                            value = even[-t] - odd[-t]
                        out_ref[lag, pl.ds(row, rows), lane : lane + lanes] = value.astype(
                            out_ref.dtype
                        )
                return carry

            lax.fori_loop(0, half // rows, body, 0)

        part(keep_ref, core * half)
        part(send_ref, (1 - core) * half)


def correlate(own_turned, mate, core, norm, lags):
    num_bins, double, depth = own_turned.shape
    cols = mate.shape[2]
    bins = 8
    half = double // 4
    return pl.pallas_call(
        functools.partial(correlate_kernel, norm),
        grid=(num_bins // bins,),
        out_shape=[
            jax.ShapeDtypeStruct((lags, half, cols), f32),
            jax.ShapeDtypeStruct((lags, half, cols), bf16),
        ],
        in_specs=[
            pl.BlockSpec(memory_space=pltpu.SMEM),
            pl.BlockSpec((bins, double, depth), lambda s: (s, 0, 0)),
            pl.BlockSpec((bins, depth, cols), lambda s: (s, 0, 0)),
        ],
        out_specs=[
            pl.BlockSpec((lags, half, cols), lambda s: (0, 0, 0)),
            pl.BlockSpec((lags, half, cols), lambda s: (0, 0, 0)),
        ],
        scratch_shapes=[pltpu.VMEM((num_bins, double, cols), f32)],
        compiler_params=params(),
        cost_estimate=pl.CostEstimate(
            flops=2 * num_bins * double * depth * cols, bytes_accessed=20_000_000, transcendentals=0
        ),
        name="correlate",
    )(core, own_turned, mate)


def final_kernel(*refs):
    *in_refs, out_ref = refs
    rows = 8
    for turn_index in range(len(in_refs) // 2):
        mine, theirs = in_refs[2 * turn_index], in_refs[2 * turn_index + 1]

        def body(chunk, carry):
            where = pl.ds(pl.multiple_of(chunk * 2 * rows, 2 * rows), 2 * rows)
            value = mine[:, where, :] + theirs[:, where, :].astype(f32)
            out_ref[where, turn_index] = jnp.swapaxes(value, 0, 1)
            return carry

        lax.fori_loop(0, out_ref.shape[0] // (2 * rows), body, 0)


def final(pairs):
    lags, rows, cols = pairs[0][0].shape
    flat = [array for pair in pairs for array in pair]
    vmem = pl.BlockSpec(memory_space=pltpu.VMEM)
    return pl.pallas_call(
        final_kernel,
        out_shape=jax.ShapeDtypeStruct((rows, len(pairs), lags, cols), f32),
        in_specs=[vmem] * len(flat),
        out_specs=vmem,
        compiler_params=params(),
        name="final",
    )(*flat)


def local(spectra, channel_order, partners):
    num_bins, _, num_windows, cols = spectra.shape
    win_count = lax.axis_size("win")
    place = lax.axis_index("win")
    core = (place % 2).astype(jnp.int32)
    chip = (place // 2).astype(jnp.int32)
    other_core = [(i, i ^ 1) for i in range(win_count)]
    other_chip = [(i, i ^ 2) for i in range(win_count)]
    norm = 1.0 / math.sqrt(num_windows * win_count * num_bins)

    own = whiten(spectra, channel_order).reshape(num_bins, 2 * num_windows, cols)
    own_turned = turn(own)
    shares = lax.all_to_all(own, "pair", split_axis=0, concat_axis=0, tiled=True)
    pairs = []
    for turn_index in range(ROUNDS):
        arranged = gather(shares, partners[turn_index])
        mate = lax.all_to_all(arranged, "pair", split_axis=0, concat_axis=0, tiled=True)
        keep, send = correlate(own_turned, mate, core[None], norm, LAGS)
        total = keep + lax.ppermute(send, "win", other_core).astype(f32)
        quarter = cols // 4
        mine = lax.dynamic_slice_in_dim(total, chip * quarter, quarter, 1)
        others = lax.dynamic_slice_in_dim(total, (1 - chip) * quarter, quarter, 1).astype(bf16)
        pairs.append((mine, lax.ppermute(others, "win", other_chip)))
    return final(pairs)[None]


def solution(mesh):
    return jax.shard_map(
        local,
        mesh=mesh,
        in_specs=(P(None, None, "win", "pair"), P("pair", None), P()),
        out_specs=P("pair", "win", None, None, None),
        check_vma=False,
    )
```

time: 754 us -> 608 us (0.81); the launches traced: 740 us -> 607 us
  Pallas kernels: 0 us -> 460 us
  local copies, waits for them, and re-layouts: 177 us -> 12 us
  other arithmetic: 157 us -> 3.92 us
  blocking collectives: 111 us -> 0 us
  matrix products: 90.2 us -> 0 us
  waiting for transfers between devices: 164 us -> 77.2 us
  starting transfers between devices: 26.4 us -> 53.4 us
  between operations: 14 us -> 0.23 us
    pallas_call x0 -> x11, Pallas kernels: none -> 460 us  [the longest x4 389 us: gather(): pl.pallas_call(gather_kernel, out_shape=jax.ShapeDtypeStruct((index.shape...]
    unnamed x28 -> x24, local copies, waits for them, and re-layouts: 141 us -> 6.8 us
    all_to_all x10 -> x0, other arithmetic: 114 us -> none  [local(): lax.all_to_all(arranged, 'pair', split_axis=0, concat_axis=0, tiled=True)]
    all_to_all x2 -> x0, blocking collectives: 111 us -> none  [local(): lax.all_to_all(arranged, 'pair', split_axis=0, concat_axis=0, tiled=True)]
    dot_general x12 -> x0, matrix products: 90.2 us -> none  [the longest x4 66.3 us: correlate(): jnp.einsum('gl,gij->ilj', lag_table, stacked, precision=lax.Precision.HIG...]
    all_to_all x2 -> x4, waiting for transfers between devices: 72.1 us -> 0.01 us  [local(): lax.all_to_all(arranged, 'pair', split_axis=0, concat_axis=0, tiled=True)]
    reduce_scatter x4 -> x0, waiting for transfers between devices: 50 us -> none  [local(): lax.psum_scatter(term_rows(jnp.int32(0), share_rows * lax.axis_size('win'...]
    ppermute x0 -> x8, waiting for transfers between devices: none -> 35.6 us  [the longest x4 35.6 us: local(): pairs.append((mine, lax.ppermute(others, 'win', other_chip)))]
  transfers between devices with their start and end apart: 7 -> 13, of which waited for: 4 -> 5; matrix products, arithmetic and copies ran while one was open for 35% -> 2% of each run, Pallas kernels for 0% -> 58%
where the time goes in v1:
time: 608 us; the launch traced here: 607 us
  Pallas kernels  460 us (76%)
  waiting for transfers between devices  77.2 us (13%)
  starting transfers between devices  53.4 us (9%)
  local copies, waits for them, and re-layouts  12 us (2%)
    pallas_call x4, Pallas kernels, gather(): pl.pallas_call(gather_kernel, out_shape=jax.ShapeDtypeStruct((index.shape...  389 us
    pallas_call x4, Pallas kernels, correlate(): pl.pallas_call(functools.partial(correlate_kernel, norm), grid=(num_bins...  50.2 us
    all_to_all x1, waiting for transfers between devices, local(): lax.all_to_all(own, 'pair', split_axis=0, concat_axis=0, tiled=True)  41.7 us
    all_to_all x4, starting transfers between devices, local(): lax.all_to_all(arranged, 'pair', split_axis=0, concat_axis=0, tiled=True)  36.5 us
    ppermute x4, waiting for transfers between devices, local(): pairs.append((mine, lax.ppermute(others, 'win', other_chip)))  35.6 us
  transfers between devices with their start and end apart: 13, of which 5 were waited for; matrix products, arithmetic and copies ran while one was open for 2% of the time, Pallas kernels for 58%

profile of v1, /device:TPU:16, one launch (start us, length us, event | category | flops | bytes accessed | tf_op | source)
XLA Modules:
  0.0 606.8 jit_solution(15971398958207939489)
XLA Ops:
  0.0 6.2 %whiten.1 = bf16[32,2,96,256]{3,2,1,0:T(8,128)(2,1)} custom-call(s32[1,256]{1,0:T(1,128)} %order_ref.1, bf16[32,2,96,256]{3,2,1,0:T(8,128)(2,1)} %spectra_ref.1), custom_call_target="tpu_custom_call" | custom-call | tf_op jit(solution)/shard_map/whiten/pallas_call | solution.py:45
  6.2 11.0 %all-to-all-start = ((bf16[32,192,256]{2,1,0:T(8,128)(2,1)}), bf16[32,192,256]{2,1,0:T(8,128)(2,1)S(1)}, u32[]{:S(2)}, u32[]{:S(2)}) async-start(bf16[32,192,256]{2,1,0:T(8,128)(2,1)} %bitcast.11), calls=%async_computation | async-start | bytes 6291456 | tf_op jit(solution)/shard_map/all_to_all | solution.py:280
  17.3 0.6 slice_bitcast_fusion
  17.8 41.7 %all-to-all-done.source_ref = bf16[32,192,256]{2,1,0:T(8,128)(2,1)S(1)} async-done(((bf16[32,192,256]{2,1,0:T(8,128)(2,1)}), bf16[32,192,256]{2,1,0:T(8,128)(2,1)S(1)}, u32[]{:S(2)}, u32[]{:S(2)}) %all-to-all-start) | async-done | bytes 3145760 | tf_op jit(solution)/shard_map/all_to_all | solution.py:280
  59.5 1.6 copy-done
  61.2 97.3 %gather.7 = bf16[32,192,256]{2,1,0:T(8,128)(2,1)} custom-call(s32[32]{0:T(128)} %get-tuple-element.21.index_ref, bf16[32,192,256]{2,1,0:T(8,128)(2,1)} %copy-done), custom_call_target="tpu_custom_call" | custom-call | tf_op jit(solution)/shard_map/gather/pallas_call | solution.py:102
  158.5 7.0 %all-to-all-start.4 = ((bf16[32,192,256]{2,1,0:T(8,128)(2,1)}), bf16[32,192,256]{2,1,0:T(8,128)(2,1)S(1)}, u32[]{:S(2)}, u32[]{:S(2)}) async-start(bf16[32,192,256]{2,1,0:T(8,128)(2,1)} %gather.7), calls=%async_computation.4 | async-start | bytes 6291456 | tf_op jit(solution)/shard_map/all_to_all | solution.py:284
  165.5 97.3 %gather.6 = bf16[32,192,256]{2,1,0:T(8,128)(2,1)} custom-call(s32[32]{0:T(128)} %get-tuple-element.24.index_ref, bf16[32,192,256]{2,1,0:T(8,128)(2,1)} %copy-done), custom_call_target="tpu_custom_call" | custom-call | tf_op jit(solution)/shard_map/gather/pallas_call | solution.py:102
  262.8 0.0 all-to-all-done.4.mate_ref
  262.9 1.6 copy-done.2
  264.5 9.8 %all-to-all-start.3 = ((bf16[32,192,256]{2,1,0:T(8,128)(2,1)}), bf16[32,192,256]{2,1,0:T(8,128)(2,1)}, u32[]{:S(2)}, u32[]{:S(2)}) async-start(bf16[32,192,256]{2,1,0:T(8,128)(2,1)} %gather.6), calls=%async_computation.3 | async-start | bytes 6291456 | tf_op jit(solution)/shard_map/all_to_all | solution.py:284
  274.3 97.3 %gather.5 = bf16[32,192,256]{2,1,0:T(8,128)(2,1)} custom-call(s32[32]{0:T(128)} %get-tuple-element.22.index_ref, bf16[32,192,256]{2,1,0:T(8,128)(2,1)} %copy-done), custom_call_target="tpu_custom_call" | custom-call | tf_op jit(solution)/shard_map/gather/pallas_call | solution.py:102
  371.7 0.0 all-to-all-done.3.mate_ref
  371.7 9.8 %all-to-all-start.2 = ((bf16[32,192,256]{2,1,0:T(8,128)(2,1)}), bf16[32,192,256]{2,1,0:T(8,128)(2,1)S(1)}, u32[]{:S(2)}, u32[]{:S(2)}) async-start(bf16[32,192,256]{2,1,0:T(8,128)(2,1)} %gather.5), calls=%async_computation.2 | async-start | bytes 6291456 | tf_op jit(solution)/shard_map/all_to_all | solution.py:284
  381.5 97.3 %gather.4 = bf16[32,192,256]{2,1,0:T(8,128)(2,1)} custom-call(s32[32]{0:T(128)} %get-tuple-element.23.index_ref, bf16[32,192,256]{2,1,0:T(8,128)(2,1)} %copy-done), custom_call_target="tpu_custom_call" | custom-call | tf_op jit(solution)/shard_map/gather/pallas_call | solution.py:102
  478.9 1.7 copy-done.1
  480.5 9.8 %all-to-all-start.1 = ((bf16[32,192,256]{2,1,0:T(8,128)(2,1)}), bf16[32,192,256]{2,1,0:T(8,128)(2,1)}, u32[]{:S(2)}, u32[]{:S(2)}) async-start(bf16[32,192,256]{2,1,0:T(8,128)(2,1)} %gather.4), calls=%async_computation.1 | async-start | bytes 6291456 | tf_op jit(solution)/shard_map/all_to_all | solution.py:284
  490.4 8.3 %turn.1.own_ref = bf16[32,512,192]{2,1,0:T(8,128)(2,1)} custom-call(bf16[32,192,256]{2,1,0:T(8,128)(2,1)} %bitcast.12), custom_call_target="tpu_custom_call" | custom-call | bytes 12000000 | tf_op jit(solution)/shard_map/turn/pallas_call | solution.py:76
  498.7 12.6 %correlate.7 = (f32[16,128,256]{2,1,0:T(8,128)}, bf16[16,128,256]{2,1,0:T(8,128)(2,1)}) custom-call(s32[1]{0:T(128)} %bitcast.core_ref, bf16[32,512,192]{2,1,0:T(8,128)(2,1)} %turn.1.own_ref, bf16[32,192,256]{2,1,0:T(8,128)(2,1)} %copy-done.2), custom_call_target="tpu_custom_call" | custom-call | flops 1610612736 | bytes 20000000 | tf_op jit(solution)/shard_map/correlate/pallas_call | solution.py:214
  511.3 12.5 %correlate.6 = (f32[16,128,256]{2,1,0:T(8,128)}, bf16[16,128,256]{2,1,0:T(8,128)(2,1)}) custom-call(s32[1]{0:T(128)} %bitcast.core_ref, bf16[32,512,192]{2,1,0:T(8,128)(2,1)} %turn.1.own_ref, bf16[32,192,256]{2,1,0:T(8,128)(2,1)} %all-to-all-done.3.mate_ref), custom_call_target="tpu_custom_call" | custom-call | flops 1610612736 | bytes 20000000 | tf_op jit(solution)/shard_map/correlate/pallas_call | solution.py:214
  523.8 0.5 collective-permute-start.4
  524.3 12.5 %correlate.5 = (f32[16,128,256]{2,1,0:T(8,128)}, bf16[16,128,256]{2,1,0:T(8,128)(2,1)}) custom-call(s32[1]{0:T(128)} %bitcast.core_ref, bf16[32,512,192]{2,1,0:T(8,128)(2,1)} %turn.1.own_ref, bf16[32,192,256]{2,1,0:T(8,128)(2,1)} %copy-done.1), custom_call_target="tpu_custom_call" | custom-call | flops 1610612736 | bytes 20000000 | tf_op jit(solution)/shard_map/correlate/pallas_call | solution.py:214
  536.8 0.0 collective-permute-start.2
  536.8 12.7 %correlate.4 = (f32[16,128,256]{2,1,0:T(8,128)}, bf16[16,128,256]{2,1,0:T(8,128)(2,1)}) custom-call(s32[1]{0:T(128)} %bitcast.core_ref, bf16[32,512,192]{2,1,0:T(8,128)(2,1)} %turn.1.own_ref, bf16[32,192,256]{2,1,0:T(8,128)(2,1)} %all-to-all-done.1.mate_ref), custom_call_target="tpu_custom_call" | custom-call | flops 1610612736 | bytes 20000000 | tf_op jit(solution)/shard_map/correlate/pallas_call | solution.py:214
  549.4 0.5 collective-permute-start
  549.9 1.7 convert_add_fusion
  551.6 0.1 dynamic-slice_convert_fusion
  551.6 2.6 collective-permute-start.7
  554.2 0.3 convert_add_fusion.1
  554.5 0.1 dynamic-slice_convert_fusion.1
  554.6 0.2 collective-permute-start.5
  554.8 1.0 copy-done.5
  555.8 1.7 convert_add_fusion.2
  557.5 0.1 dynamic-slice_convert_fusion.2
  557.6 1.0 collective-permute-start.3
  558.6 0.2 convert_add_fusion.3
  558.9 0.1 dynamic-slice_convert_fusion.3
  558.9 1.2 collective-permute-start.1
  560.1 1.1 constant_dynamic-slice_fusion.refs_6_
  561.2 1.1 constant_dynamic-slice_fusion.1.refs_4_
  562.3 1.1 constant_dynamic-slice_fusion.2.refs_2_
  563.4 1.1 constant_dynamic-slice_fusion.3.refs_0_
  564.5 2.5 collective-permute-done.7.refs_7_
  566.9 11.2 %collective-permute-done.5.refs_5_ = bf16[16,64,256]{2,1,0:T(8,128)(2,1)S(1)} collective-permute-done((bf16[16,64,256]{2,1,0:T(8,128)(2,1)S(1)}, bf16[16,64,256]{2,1,0:T(8,128)(2,1)S(1)}, u32[]{:S(2)}, u32[]{:S(2)}) %collective-permute-start.5) | collective-permute-done | bytes 524320 | tf_op jit(solution)/shard_map/ppermute | solution.py:290
  578.2 11.2 %collective-permute-done.3.refs_3_ = bf16[16,64,256]{2,1,0:T(8,128)(2,1)S(1)} collective-permute-done((bf16[16,64,256]{2,1,0:T(8,128)(2,1)S(1)}, bf16[16,64,256]{2,1,0:T(8,128)(2,1)S(1)}, u32[]{:S(2)}, u32[]{:S(2)}) %collective-permute-start.3) | collective-permute-done | bytes 524320 | tf_op jit(solution)/shard_map/ppermute | solution.py:290
  589.4 10.6 %collective-permute-done.1.refs_1_ = bf16[16,64,256]{2,1,0:T(8,128)(2,1)S(1)} collective-permute-done((bf16[16,64,256]{2,1,0:T(8,128)(2,1)S(1)}, bf16[16,64,256]{2,1,0:T(8,128)(2,1)S(1)}, u32[]{:S(2)}, u32[]{:S(2)}) %collective-permute-start.1) | collective-permute-done | bytes 524320 | tf_op jit(solution)/shard_map/ppermute | solution.py:290
  600.1 0.8 copy-done.10
  600.9 5.9 final.1
  (26 shorter events, 0.1 us)
Async XLA Ops:
  6.2 11.0 %copy-start.11 = (s32[4,32]{1,0:T(4,128)S(1)}, s32[4,32]{1,0:T(4,128)}, u32[]{:S(2)}) copy-start(s32[4,32]{1,0:T(4,128)} %param.5) | copy-start | bytes 1540
  6.2 53.3 %all-to-all-start = ((bf16[32,192,256]{2,1,0:T(8,128)(2,1)}), bf16[32,192,256]{2,1,0:T(8,128)(2,1)S(1)}, u32[]{:S(2)}, u32[]{:S(2)}) async-start(bf16[32,192,256]{2,1,0:T(8,128)(2,1)} %bitcast.11), calls=%async_computation | async-start | bytes 6291456 | tf_op jit(solution)/shard_map/all_to_all | solution.py:280
  59.5 1.7 copy-start
  158.5 104.3 %all-to-all-start.4 = ((bf16[32,192,256]{2,1,0:T(8,128)(2,1)}), bf16[32,192,256]{2,1,0:T(8,128)(2,1)S(1)}, u32[]{:S(2)}, u32[]{:S(2)}) async-start(bf16[32,192,256]{2,1,0:T(8,128)(2,1)} %gather.7), calls=%async_computation.4 | async-start | bytes 6291456 | tf_op jit(solution)/shard_map/all_to_all | solution.py:284
  262.9 1.6 copy-start.2
  264.5 107.2 %all-to-all-start.3 = ((bf16[32,192,256]{2,1,0:T(8,128)(2,1)}), bf16[32,192,256]{2,1,0:T(8,128)(2,1)}, u32[]{:S(2)}, u32[]{:S(2)}) async-start(bf16[32,192,256]{2,1,0:T(8,128)(2,1)} %gather.6), calls=%async_computation.3 | async-start | bytes 6291456 | tf_op jit(solution)/shard_map/all_to_all | solution.py:284
  371.7 107.2 %all-to-all-start.2 = ((bf16[32,192,256]{2,1,0:T(8,128)(2,1)}), bf16[32,192,256]{2,1,0:T(8,128)(2,1)S(1)}, u32[]{:S(2)}, u32[]{:S(2)}) async-start(bf16[32,192,256]{2,1,0:T(8,128)(2,1)} %gather.5), calls=%async_computation.2 | async-start | bytes 6291456 | tf_op jit(solution)/shard_map/all_to_all | solution.py:284
  478.9 1.7 copy-start.1
  480.5 56.2 %all-to-all-start.1 = ((bf16[32,192,256]{2,1,0:T(8,128)(2,1)}), bf16[32,192,256]{2,1,0:T(8,128)(2,1)}, u32[]{:S(2)}, u32[]{:S(2)}) async-start(bf16[32,192,256]{2,1,0:T(8,128)(2,1)} %gather.4), calls=%async_computation.1 | async-start | bytes 6291456 | tf_op jit(solution)/shard_map/all_to_all | solution.py:284
  511.3 38.6 %collective-permute-start.6 = (bf16[16,128,256]{2,1,0:T(8,128)(2,1)}, bf16[16,128,256]{2,1,0:T(8,128)(2,1)}, u32[]{:S(2)}, u32[]{:S(2)}) collective-permute-start(bf16[16,128,256]{2,1,0:T(8,128)(2,1)} %get-tuple-element.20), channel_id=1, source_target_pairs={{0,1},{1,0},{2,3},{3,2},{4,5},{5,4},{6,7},{7,6},{8,9},{9,8},{10,11... | collective-permute-start | bytes 3145736 | tf_op jit(solution)/shard_map/ppermute | solution.py:286
  523.8 30.5 %collective-permute-start.4 = (bf16[16,128,256]{2,1,0:T(8,128)(2,1)}, bf16[16,128,256]{2,1,0:T(8,128)(2,1)S(1)}, u32[]{:S(2)}, u32[]{:S(2)}) collective-permute-start(bf16[16,128,256]{2,1,0:T(8,128)(2,1)} %get-tuple-element.18), channel_id=1, source_target_pairs={{0,1},{1,0},{2,3},{3,2},{4,5},{5,4},{6,7},{7,6},{8,9},{9,8},{10,11... | collective-permute-start | bytes 3145736 | tf_op jit(solution)/shard_map/ppermute | solution.py:286
  536.8 13.2 %copy-start.4 = (f32[16,128,256]{2,1,0:T(8,128)S(1)}, f32[16,128,256]{2,1,0:T(8,128)}, u32[]{:S(2)}) copy-start(f32[16,128,256]{2,1,0:T(8,128)} %get-tuple-element.19) | copy-start | bytes 6291460
  536.8 18.0 %collective-permute-start.2 = (bf16[16,128,256]{2,1,0:T(8,128)(2,1)}, bf16[16,128,256]{2,1,0:T(8,128)(2,1)}, u32[]{:S(2)}, u32[]{:S(2)}) collective-permute-start(bf16[16,128,256]{2,1,0:T(8,128)(2,1)} %get-tuple-element.16), channel_id=1, source_target_pairs={{0,1},{1,0},{2,3},{3,2},{4,5},{5,4},{6,7},{7,6},{8,9},{9,8},{10,11... | collective-permute-start | bytes 3145736 | tf_op jit(solution)/shard_map/ppermute | solution.py:286
  549.4 9.2 %collective-permute-start = (bf16[16,128,256]{2,1,0:T(8,128)(2,1)}, bf16[16,128,256]{2,1,0:T(8,128)(2,1)S(1)}, u32[]{:S(2)}, u32[]{:S(2)}) collective-permute-start(bf16[16,128,256]{2,1,0:T(8,128)(2,1)} %get-tuple-element.14), channel_id=1, source_target_pairs={{0,1},{1,0},{2,3},{3,2},{4,5},{5,4},{6,7},{7,6},{8,9},{9,8},{10,11... | collective-permute-start | bytes 3145736 | tf_op jit(solution)/shard_map/ppermute | solution.py:286
  549.9 4.3 copy-start.3
  551.6 15.3 %collective-permute-start.7 = (bf16[16,64,256]{2,1,0:T(8,128)(2,1)S(1)}, bf16[16,64,256]{2,1,0:T(8,128)(2,1)S(1)}, u32[]{:S(2)}, u32[]{:S(2)}) collective-permute-start(bf16[16,64,256]{2,1,0:T(8,128)(2,1)S(1)} %dynamic-slice_convert_fusion), channel_id=1, source_target_pairs={{0,2},{1,3},{2,0},{3,1},{4,6},{5,7},{6,4},{7,5},{8,10},{9,11},{10,... | collective-permute-start | bytes 1572872 | tf_op jit(solution)/shard_map/ppermute | solution.py:290
  554.2 1.6 copy-start.5
  554.6 23.5 %collective-permute-start.5 = (bf16[16,64,256]{2,1,0:T(8,128)(2,1)S(1)}, bf16[16,64,256]{2,1,0:T(8,128)(2,1)S(1)}, u32[]{:S(2)}, u32[]{:S(2)}) collective-permute-start(bf16[16,64,256]{2,1,0:T(8,128)(2,1)S(1)} %dynamic-slice_convert_fusion.1), channel_id=1, source_target_pairs={{0,2},{1,3},{2,0},{3,1},{4,6},{5,7},{6,4},{7,5},{8,10},{9,11},{10,... | collective-permute-start | bytes 1572872 | tf_op jit(solution)/shard_map/ppermute | solution.py:290
  555.8 2.8 copy-start.6
  557.6 31.8 %collective-permute-start.3 = (bf16[16,64,256]{2,1,0:T(8,128)(2,1)S(1)}, bf16[16,64,256]{2,1,0:T(8,128)(2,1)S(1)}, u32[]{:S(2)}, u32[]{:S(2)}) collective-permute-start(bf16[16,64,256]{2,1,0:T(8,128)(2,1)S(1)} %dynamic-slice_convert_fusion.2), channel_id=1, source_target_pairs={{0,2},{1,3},{2,0},{3,1},{4,6},{5,7},{6,4},{7,5},{8,10},{9,11},{10,... | collective-permute-start | bytes 1572872 | tf_op jit(solution)/shard_map/ppermute | solution.py:290
  558.9 41.1 %collective-permute-start.1 = (bf16[16,64,256]{2,1,0:T(8,128)(2,1)S(1)}, bf16[16,64,256]{2,1,0:T(8,128)(2,1)S(1)}, u32[]{:S(2)}, u32[]{:S(2)}) collective-permute-start(bf16[16,64,256]{2,1,0:T(8,128)(2,1)S(1)} %dynamic-slice_convert_fusion.3), channel_id=1, source_target_pairs={{0,2},{1,3},{2,0},{3,1},{4,6},{5,7},{6,4},{7,5},{8,10},{9,11},{10,... | collective-permute-start | bytes 1572872 | tf_op jit(solution)/shard_map/ppermute | solution.py:290
  566.9 33.1 %copy-start.7 = (bf16[16,64,256]{2,1,0:T(8,128)(2,1)}, bf16[16,64,256]{2,1,0:T(8,128)(2,1)S(1)}, u32[]{:S(2)}) copy-start(bf16[16,64,256]{2,1,0:T(8,128)(2,1)S(1)} %collective-permute-done.7.refs_7_) | copy-start | bytes 1572868
  578.2 21.9 %copy-start.8 = (bf16[16,64,256]{2,1,0:T(8,128)(2,1)}, bf16[16,64,256]{2,1,0:T(8,128)(2,1)S(1)}, u32[]{:S(2)}) copy-start(bf16[16,64,256]{2,1,0:T(8,128)(2,1)S(1)} %collective-permute-done.5.refs_5_) | copy-start | bytes 1572868
  589.4 10.6 %copy-start.9 = (bf16[16,64,256]{2,1,0:T(8,128)(2,1)}, bf16[16,64,256]{2,1,0:T(8,128)(2,1)S(1)}, u32[]{:S(2)}) copy-start(bf16[16,64,256]{2,1,0:T(8,128)(2,1)S(1)} %collective-permute-done.3.refs_3_) | copy-start | bytes 1572868
  600.1 0.8 copy-start.10

commit v2 on v1

--- a/solution.py
+++ b/solution.py
@@ -85,27 +85,32 @@
     )(own_rows)
 
 
-def gather_kernel(index_ref, source_ref, out_ref, sems):
-    count = out_ref.shape[0]
+def gather_kernel(index_ref, source_ref, *refs):
+    *out_refs, sems = refs
     copies = []
-    for place in range(count):
-        copy = pltpu.make_async_copy(
-            source_ref.at[index_ref[place]], out_ref.at[place], sems.at[place]
-        )
-        copy.start()
-        copies.append(copy)
+    for group, out_ref in enumerate(out_refs):
+        for place in range(out_ref.shape[0]):
+            copy = pltpu.make_async_copy(
+                source_ref.at[index_ref[group, place]], out_ref.at[place], sems.at[group, place]
+            )
+            copy.start()
+            copies.append(copy)
     for copy in copies:
         copy.wait()
 
 
 def gather(source, index):
+    groups, places = index.shape
     return pl.pallas_call(
         gather_kernel,
-        out_shape=jax.ShapeDtypeStruct((index.shape[0],) + source.shape[1:], source.dtype),
-        in_specs=[pl.BlockSpec(memory_space=pltpu.SMEM), pl.BlockSpec(memory_space=pl.ANY)],
-        out_specs=pl.BlockSpec(memory_space=pl.ANY),
-        scratch_shapes=[pltpu.SemaphoreType.DMA((index.shape[0],))],
-        compiler_params=pltpu.CompilerParams(),
+        out_shape=[jax.ShapeDtypeStruct((places,) + source.shape[1:], source.dtype)] * groups,
+        in_specs=[
+            pl.BlockSpec(memory_space=pltpu.SMEM),
+            pl.BlockSpec(memory_space=pltpu.VMEM),
+        ],
+        out_specs=[pl.BlockSpec(memory_space=pl.ANY)] * groups,
+        scratch_shapes=[pltpu.SemaphoreType.DMA(index.shape)],
+        compiler_params=params(),
         name="gather",
     )(index, source)
 
@@ -278,13 +283,18 @@
     own = whiten(spectra, channel_order).reshape(num_bins, 2 * num_windows, cols)
     own_turned = turn(own)
     shares = lax.all_to_all(own, "pair", split_axis=0, concat_axis=0, tiled=True)
+    arranged = gather(shares, partners)
     pairs = []
+    kept = []
     for turn_index in range(ROUNDS):
-        arranged = gather(shares, partners[turn_index])
-        mate = lax.all_to_all(arranged, "pair", split_axis=0, concat_axis=0, tiled=True)
-        keep, send = correlate(own_turned, mate, core[None], norm, LAGS)
+        operand = arranged[turn_index]
+        if turn_index >= 2:
+            operand, kept[turn_index - 2] = lax.optimization_barrier((operand, kept[turn_index - 2]))
+        mate = lax.all_to_all(operand, "pair", split_axis=0, concat_axis=0, tiled=True)
+        kept.append(correlate(own_turned, mate, core[None], norm, LAGS))
+    quarter = cols // 4
+    for keep, send in kept:
         total = keep + lax.ppermute(send, "win", other_core).astype(f32)
-        quarter = cols // 4
         mine = lax.dynamic_slice_in_dim(total, chip * quarter, quarter, 1)
         others = lax.dynamic_slice_in_dim(total, (1 - chip) * quarter, quarter, 1).astype(bf16)
         pairs.append((mine, lax.ppermute(others, "win", other_chip)))

time: 608 us -> 333 us (0.55)
  Pallas kernels: 460 us -> 78.6 us
  blocking collectives: 0 us -> 95.6 us
  waiting for transfers between devices: 77.2 us -> 110 us
  starting transfers between devices: 53.4 us -> 29.8 us
    pallas_call x4 -> x1, Pallas kernels: 389 us -> 7.61 us  [gather(): pl.pallas_call(gather_kernel, out_shape=[jax.ShapeDtypeStruct((places,) +...]
    all_to_all x0 -> x2, blocking collectives: none -> 95.6 us  [the longest x1 50 us: local(): lax.all_to_all(own, 'pair', split_axis=0, concat_axis=0, tiled=True)]
    all_to_all x5 -> x3, waiting for transfers between devices: 41.7 us -> 73.7 us  [local(): lax.all_to_all(operand, 'pair', split_axis=0, concat_axis=0, tiled=True)]
    all_to_all x5 -> x3, starting transfers between devices: 47.5 us -> 23.3 us  [local(): lax.all_to_all(operand, 'pair', split_axis=0, concat_axis=0, tiled=True)]
  transfers between devices with their start and end apart: 13 -> 11, of which waited for: 5 -> 7; matrix products, arithmetic and copies ran while one was open for 2% -> 3% of each run, Pallas kernels for 58% -> 18%
where the time goes in v2:
time: 333 us; the launch traced here: 330 us
  waiting for transfers between devices  110 us (33%)
  blocking collectives  95.6 us (29%)
  Pallas kernels  78.6 us (24%)
  starting transfers between devices  29.8 us (9%)
  local copies, waits for them, and re-layouts  10.4 us (3%)
  other arithmetic  6.25 us (2%)
    all_to_all x3, waiting for transfers between devices, local(): lax.all_to_all(operand, 'pair', split_axis=0, concat_axis=0, tiled=True)  73.7 us
    pallas_call x4, Pallas kernels, correlate(): pl.pallas_call(functools.partial(correlate_kernel, norm), grid=(num_bins...  50.5 us
    all_to_all x1, blocking collectives, local(): lax.all_to_all(own, 'pair', split_axis=0, concat_axis=0, tiled=True)  50 us
    all_to_all x1, blocking collectives, local(): lax.all_to_all(operand, 'pair', split_axis=0, concat_axis=0, tiled=True)  45.7 us
    ppermute x4, waiting for transfers between devices, local(): pairs.append((mine, lax.ppermute(others, 'win', other_chip)))  35.8 us
    all_to_all x3, starting transfers between devices, local(): lax.all_to_all(operand, 'pair', split_axis=0, concat_axis=0, tiled=True)  23.3 us
    pallas_call x1, Pallas kernels, turn(): pl.pallas_call(turn_kernel, grid=(num_bins // bins,), out_shape=jax.Shape...  8.31 us
    pallas_call x1, Pallas kernels, gather(): pl.pallas_call(gather_kernel, out_shape=[jax.ShapeDtypeStruct((places,) +...  7.61 us
  transfers between devices with their start and end apart: 11, of which 7 were waited for; matrix products, arithmetic and copies ran while one was open for 3% of the time, Pallas kernels for 18%

profile of v2, /device:TPU:16, one launch (start us, length us, event | category | flops | bytes accessed | tf_op | source)
XLA Modules:
  0.0 330.3 jit_solution(406370782554361060)
XLA Ops:
  0.0 6.2 %whiten.1 = bf16[32,2,96,256]{3,2,1,0:T(8,128)(2,1)} custom-call(s32[1,256]{1,0:T(1,128)} %order_ref.1, bf16[32,2,96,256]{3,2,1,0:T(8,128)(2,1)} %spectra_ref.1), custom_call_target="tpu_custom_call" | custom-call | tf_op jit(solution)/shard_map/whiten/pallas_call | solution.py:45
  6.2 50.0 %all_to_all.25.source_ref = bf16[32,192,256]{2,1,0:T(8,128)(2,1)} all-to-all(bf16[32,192,256]{2,1,0:T(8,128)(2,1)} %bitcast.3), channel_id=1, replica_groups=mesh['pair'=32,'win'=4] {'pair'}, dimensions={0} | all-to-all | bytes 6291456 | tf_op jit(solution)/shard_map/all_to_all | solution.py:285
  56.2 7.6 %gather.1 = (bf16[32,192,256]{2,1,0:T(8,128)(2,1)}, bf16[32,192,256]{2,1,0:T(8,128)(2,1)}, bf16[32,192,256]{2,1,0:T(8,128)(2,1)}, bf16[32,192,256]{2,1,0:T(8,128)(2,1)}) custom-call(s32[4,32]{1,0:T(4,128)} %index_ref.1, bf16[32,192,256]{2,1,0:T(8,128)(2,1)} %all_to_all.25.source_ref), custom_call_target="tpu_custom_call" | custom-call | tf_op jit(solution)/shard_map/gather/pallas_call | solution.py:104
  63.8 45.7 %all_to_all.26.mate_ref = bf16[32,192,256]{2,1,0:T(8,128)(2,1)} all-to-all(bf16[32,192,256]{2,1,0:T(8,128)(2,1)} %get-tuple-element.30), channel_id=1, replica_groups=mesh['pair'=32,'win'=4] {'pair'}, dimensions={0} | all-to-all | bytes 6291456 | tf_op jit(solution)/shard_map/all_to_all | solution.py:293
  109.5 6.6 %all-to-all-start.1 = ((bf16[32,192,256]{2,1,0:T(8,128)(2,1)}), bf16[32,192,256]{2,1,0:T(8,128)(2,1)S(1)}, u32[]{:S(2)}, u32[]{:S(2)}) async-start(bf16[32,192,256]{2,1,0:T(8,128)(2,1)} %get-tuple-element.24), calls=%async_computation.1 | async-start | bytes 6291456 | tf_op jit(solution)/shard_map/all_to_all | solution.py:293
  116.1 8.3 %turn.1.own_ref = bf16[32,512,192]{2,1,0:T(8,128)(2,1)} custom-call(bf16[32,192,256]{2,1,0:T(8,128)(2,1)} %bitcast.4), custom_call_target="tpu_custom_call" | custom-call | bytes 12000000 | tf_op jit(solution)/shard_map/turn/pallas_call | solution.py:76
  124.4 12.6 %correlate.5 = (f32[16,128,256]{2,1,0:T(8,128)}, bf16[16,128,256]{2,1,0:T(8,128)(2,1)}) custom-call(s32[1]{0:T(128)} %bitcast.1.core_ref, bf16[32,512,192]{2,1,0:T(8,128)(2,1)} %turn.1.own_ref, bf16[32,192,256]{2,1,0:T(8,128)(2,1)} %all_to_all.26.mate_ref), custom_call_target="tpu_custom_call" | custom-call | flops 1610612736 | bytes 20000000 | tf_op jit(solution)/shard_map/correlate/pallas_call | solution.py:219
  137.0 18.6 %all-to-all-done.1.mate_ref = bf16[32,192,256]{2,1,0:T(8,128)(2,1)S(1)} async-done(((bf16[32,192,256]{2,1,0:T(8,128)(2,1)}), bf16[32,192,256]{2,1,0:T(8,128)(2,1)S(1)}, u32[]{:S(2)}, u32[]{:S(2)}) %all-to-all-start.1) | async-done | bytes 3145760 | tf_op jit(solution)/shard_map/all_to_all | solution.py:293
  155.6 1.7 copy-done.2
  157.2 9.6 %all-to-all-start.4 = ((bf16[32,192,256]{2,1,0:T(8,128)(2,1)}), bf16[32,192,256]{2,1,0:T(8,128)(2,1)S(1)}, u32[]{:S(2)}, u32[]{:S(2)}) async-start(bf16[32,192,256]{2,1,0:T(8,128)(2,1)} %get-tuple-element.38), calls=%async_computation.4 | async-start | bytes 6291456 | tf_op jit(solution)/shard_map/all_to_all | solution.py:293
  166.8 12.5 %correlate.4 = (f32[16,128,256]{2,1,0:T(8,128)}, bf16[16,128,256]{2,1,0:T(8,128)(2,1)}) custom-call(s32[1]{0:T(128)} %bitcast.1.core_ref, bf16[32,512,192]{2,1,0:T(8,128)(2,1)} %turn.1.own_ref, bf16[32,192,256]{2,1,0:T(8,128)(2,1)} %copy-done.2), custom_call_target="tpu_custom_call" | custom-call | flops 1610612736 | bytes 20000000 | tf_op jit(solution)/shard_map/correlate/pallas_call | solution.py:219
  179.3 29.9 %all-to-all-done.4.mate_ref = bf16[32,192,256]{2,1,0:T(8,128)(2,1)S(1)} async-done(((bf16[32,192,256]{2,1,0:T(8,128)(2,1)}), bf16[32,192,256]{2,1,0:T(8,128)(2,1)S(1)}, u32[]{:S(2)}, u32[]{:S(2)}) %all-to-all-start.4) | async-done | bytes 3145760 | tf_op jit(solution)/shard_map/all_to_all | solution.py:293
  209.2 1.7 copy-done.1
  210.8 7.1 %all-to-all-start.3 = ((bf16[32,192,256]{2,1,0:T(8,128)(2,1)}), bf16[32,192,256]{2,1,0:T(8,128)(2,1)S(1)}, u32[]{:S(2)}, u32[]{:S(2)}) async-start(bf16[32,192,256]{2,1,0:T(8,128)(2,1)} %get-tuple-element.35), calls=%async_computation.3 | async-start | bytes 6291456 | tf_op jit(solution)/shard_map/all_to_all | solution.py:293
  217.9 0.1 collective-permute-start.2
  218.0 0.5 collective-permute-start
  218.5 12.6 %correlate.7 = (f32[16,128,256]{2,1,0:T(8,128)}, bf16[16,128,256]{2,1,0:T(8,128)(2,1)}) custom-call(s32[1]{0:T(128)} %bitcast.1.core_ref, bf16[32,512,192]{2,1,0:T(8,128)(2,1)} %turn.1.own_ref, bf16[32,192,256]{2,1,0:T(8,128)(2,1)} %copy-done.1), custom_call_target="tpu_custom_call" | custom-call | flops 1610612736 | bytes 20000000 | tf_op jit(solution)/shard_map/correlate/pallas_call | solution.py:219
  231.1 0.1 collective-permute-start.6
  231.2 0.0 collective-permute-done.2
  231.2 2.8 convert_add_fusion.2
  234.1 25.2 %all-to-all-done.3.mate_ref = bf16[32,192,256]{2,1,0:T(8,128)(2,1)S(1)} async-done(((bf16[32,192,256]{2,1,0:T(8,128)(2,1)}), bf16[32,192,256]{2,1,0:T(8,128)(2,1)S(1)}, u32[]{:S(2)}, u32[]{:S(2)}) %all-to-all-start.3) | async-done | bytes 3145760 | tf_op jit(solution)/shard_map/all_to_all | solution.py:293
  259.3 1.7 copy-done
  261.0 12.9 %correlate.6 = (f32[16,128,256]{2,1,0:T(8,128)}, bf16[16,128,256]{2,1,0:T(8,128)(2,1)}) custom-call(s32[1]{0:T(128)} %bitcast.1.core_ref, bf16[32,512,192]{2,1,0:T(8,128)(2,1)} %turn.1.own_ref, bf16[32,192,256]{2,1,0:T(8,128)(2,1)} %copy-done), custom_call_target="tpu_custom_call" | custom-call | flops 1610612736 | bytes 20000000 | tf_op jit(solution)/shard_map/correlate/pallas_call | solution.py:219
  273.8 0.0 collective-permute-start.4
  273.8 0.1 dynamic-slice_convert_fusion.2
  273.9 3.4 %collective-permute-start.3 = (bf16[16,64,256]{2,1,0:T(8,128)(2,1)S(1)}, bf16[16,64,256]{2,1,0:T(8,128)(2,1)S(1)}, u32[]{:S(2)}, u32[]{:S(2)}) collective-permute-start(bf16[16,64,256]{2,1,0:T(8,128)(2,1)S(1)} %dynamic-slice_convert_fusion.2), channel_id=1, source_target_pairs={{0,2},{1,3},{2,0},{3,1},{4,6},{5,7},{6,4},{7,5},{8,10},{9,11},{10,... | collective-permute-start | bytes 1572872 | tf_op jit(solution)/shard_map/ppermute | solution.py:300
  277.3 0.0 collective-permute-done
  277.3 1.5 convert_add_fusion.3
  278.8 0.1 dynamic-slice_convert_fusion.3
  278.9 0.2 collective-permute-start.1
  279.1 0.0 collective-permute-done.6
  279.1 1.7 convert_add_fusion
  280.8 0.1 dynamic-slice_convert_fusion
  280.9 2.0 collective-permute-start.7
  282.9 0.0 collective-permute-done.4
  282.9 0.2 convert_add_fusion.1
  283.1 0.1 dynamic-slice_convert_fusion.1
  283.2 0.2 collective-permute-start.5
  283.4 1.1 constant_dynamic-slice_fusion.2.refs_2_
  284.5 1.1 constant_dynamic-slice_fusion.3.refs_0_
  285.6 1.1 constant_dynamic-slice_fusion.refs_6_
  286.7 1.1 constant_dynamic-slice_fusion.1.refs_4_
  287.8 2.3 collective-permute-done.3.refs_3_
  290.1 11.2 %collective-permute-done.1.refs_1_ = bf16[16,64,256]{2,1,0:T(8,128)(2,1)S(1)} collective-permute-done((bf16[16,64,256]{2,1,0:T(8,128)(2,1)S(1)}, bf16[16,64,256]{2,1,0:T(8,128)(2,1)S(1)}, u32[]{:S(2)}, u32[]{:S(2)}) %collective-permute-start.1) | collective-permute-done | bytes 524320 | tf_op jit(solution)/shard_map/ppermute | solution.py:300
  301.3 11.2 %collective-permute-done.7.refs_7_ = bf16[16,64,256]{2,1,0:T(8,128)(2,1)S(1)} collective-permute-done((bf16[16,64,256]{2,1,0:T(8,128)(2,1)S(1)}, bf16[16,64,256]{2,1,0:T(8,128)(2,1)S(1)}, u32[]{:S(2)}, u32[]{:S(2)}) %collective-permute-start.7) | collective-permute-done | bytes 524320 | tf_op jit(solution)/shard_map/ppermute | solution.py:300
  312.6 11.0 %collective-permute-done.5.refs_5_ = bf16[16,64,256]{2,1,0:T(8,128)(2,1)S(1)} collective-permute-done((bf16[16,64,256]{2,1,0:T(8,128)(2,1)S(1)}, bf16[16,64,256]{2,1,0:T(8,128)(2,1)S(1)}, u32[]{:S(2)}, u32[]{:S(2)}) %collective-permute-start.5) | collective-permute-done | bytes 524320 | tf_op jit(solution)/shard_map/ppermute | solution.py:300
  323.6 0.8 copy-done.11
  324.4 5.9 %final.1 = f32[64,4,16,256]{3,2,1,0:T(8,128)} custom-call(f32[16,64,256]{2,1,0:T(8,128)} %constant_dynamic-slice_fusion.3.refs_0_, bf16[16,64,256]{2,1,0:T(8,128)(2,1)} %copy-done.9, f32[16,64,256]{2,1,0:T(8,128)} %constant_dynamic-slice_fusion.2.refs_2_, bf16[16,64,256]{2,1,0:T(8,128)(2,1)} %copy-done.8, ...), custom_call_target="tpu_custom_call" | custom-call | tf_op jit(solution)/shard_map/final/pallas_call | solution.py:263
  (20 shorter events, 0.0 us)
Async XLA Ops:
  109.5 46.1 %all-to-all-start.1 = ((bf16[32,192,256]{2,1,0:T(8,128)(2,1)}), bf16[32,192,256]{2,1,0:T(8,128)(2,1)S(1)}, u32[]{:S(2)}, u32[]{:S(2)}) async-start(bf16[32,192,256]{2,1,0:T(8,128)(2,1)} %get-tuple-element.24), calls=%async_computation.1 | async-start | bytes 6291456 | tf_op jit(solution)/shard_map/all_to_all | solution.py:293
  155.6 1.7 copy-start.2
  157.2 51.9 %all-to-all-start.4 = ((bf16[32,192,256]{2,1,0:T(8,128)(2,1)}), bf16[32,192,256]{2,1,0:T(8,128)(2,1)S(1)}, u32[]{:S(2)}, u32[]{:S(2)}) async-start(bf16[32,192,256]{2,1,0:T(8,128)(2,1)} %get-tuple-element.38), calls=%async_computation.4 | async-start | bytes 6291456 | tf_op jit(solution)/shard_map/all_to_all | solution.py:293
  209.2 1.7 copy-start.1
  210.8 48.5 %all-to-all-start.3 = ((bf16[32,192,256]{2,1,0:T(8,128)(2,1)}), bf16[32,192,256]{2,1,0:T(8,128)(2,1)S(1)}, u32[]{:S(2)}, u32[]{:S(2)}) async-start(bf16[32,192,256]{2,1,0:T(8,128)(2,1)} %get-tuple-element.35), calls=%async_computation.3 | async-start | bytes 6291456 | tf_op jit(solution)/shard_map/all_to_all | solution.py:293
  217.9 13.3 %collective-permute-start.2 = (bf16[16,128,256]{2,1,0:T(8,128)(2,1)}, bf16[16,128,256]{2,1,0:T(8,128)(2,1)}, u32[]{:S(2)}, u32[]{:S(2)}) collective-permute-start(bf16[16,128,256]{2,1,0:T(8,128)(2,1)} %get-tuple-element.34), channel_id=1, source_target_pairs={{0,1},{1,0},{2,3},{3,2},{4,5},{5,4},{6,7},{7,6},{8,9},{9,8},{10,11... | collective-permute-start | bytes 3145736 | tf_op jit(solution)/shard_map/ppermute | solution.py:297
  218.0 59.3 %collective-permute-start = (bf16[16,128,256]{2,1,0:T(8,128)(2,1)}, bf16[16,128,256]{2,1,0:T(8,128)(2,1)}, u32[]{:S(2)}, u32[]{:S(2)}) collective-permute-start(bf16[16,128,256]{2,1,0:T(8,128)(2,1)} %get-tuple-element.28), channel_id=1, source_target_pairs={{0,1},{1,0},{2,3},{3,2},{4,5},{5,4},{6,7},{7,6},{8,9},{9,8},{10,11... | collective-permute-start | bytes 3145736 | tf_op jit(solution)/shard_map/ppermute | solution.py:297
  218.5 12.7 %copy-start.5 = (f32[16,128,256]{2,1,0:T(8,128)S(1)}, f32[16,128,256]{2,1,0:T(8,128)}, u32[]{:S(2)}) copy-start(f32[16,128,256]{2,1,0:T(8,128)} %get-tuple-element.33) | copy-start | bytes 6291460
  231.1 48.0 %collective-permute-start.6 = (bf16[16,128,256]{2,1,0:T(8,128)(2,1)}, bf16[16,128,256]{2,1,0:T(8,128)(2,1)}, u32[]{:S(2)}, u32[]{:S(2)}) collective-permute-start(bf16[16,128,256]{2,1,0:T(8,128)(2,1)} %get-tuple-element.40), channel_id=1, source_target_pairs={{0,1},{1,0},{2,3},{3,2},{4,5},{5,4},{6,7},{7,6},{8,9},{9,8},{10,11... | collective-permute-start | bytes 3145736 | tf_op jit(solution)/shard_map/ppermute | solution.py:297
  259.3 1.7 copy-start
  260.9 12.9 %copy-start.3 = (f32[16,128,256]{2,1,0:T(8,128)S(1)}, f32[16,128,256]{2,1,0:T(8,128)}, u32[]{:S(2)}) copy-start(f32[16,128,256]{2,1,0:T(8,128)} %convert_add_fusion.2) | copy-start | bytes 6291460
  260.9 16.4 %copy-start.4 = (f32[16,128,256]{2,1,0:T(8,128)S(1)}, f32[16,128,256]{2,1,0:T(8,128)}, u32[]{:S(2)}) copy-start(f32[16,128,256]{2,1,0:T(8,128)} %get-tuple-element.27) | copy-start | bytes 6291460
  273.8 9.0 %collective-permute-start.4 = (bf16[16,128,256]{2,1,0:T(8,128)(2,1)}, bf16[16,128,256]{2,1,0:T(8,128)(2,1)S(1)}, u32[]{:S(2)}, u32[]{:S(2)}) collective-permute-start(bf16[16,128,256]{2,1,0:T(8,128)(2,1)} %get-tuple-element.37), channel_id=1, source_target_pairs={{0,1},{1,0},{2,3},{3,2},{4,5},{5,4},{6,7},{7,6},{8,9},{9,8},{10,11... | collective-permute-start | bytes 3145736 | tf_op jit(solution)/shard_map/ppermute | solution.py:297
  273.9 5.2 %copy-start.6 = (f32[16,128,256]{2,1,0:T(8,128)S(1)}, f32[16,128,256]{2,1,0:T(8,128)}, u32[]{:S(2)}) copy-start(f32[16,128,256]{2,1,0:T(8,128)} %get-tuple-element.39) | copy-start | bytes 6291460
  273.9 16.2 %collective-permute-start.3 = (bf16[16,64,256]{2,1,0:T(8,128)(2,1)S(1)}, bf16[16,64,256]{2,1,0:T(8,128)(2,1)S(1)}, u32[]{:S(2)}, u32[]{:S(2)}) collective-permute-start(bf16[16,64,256]{2,1,0:T(8,128)(2,1)S(1)} %dynamic-slice_convert_fusion.2), channel_id=1, source_target_pairs={{0,2},{1,3},{2,0},{3,1},{4,6},{5,7},{6,4},{7,5},{8,10},{9,11},{10,... | collective-permute-start | bytes 1572872 | tf_op jit(solution)/shard_map/ppermute | solution.py:300
  278.9 22.4 %collective-permute-start.1 = (bf16[16,64,256]{2,1,0:T(8,128)(2,1)S(1)}, bf16[16,64,256]{2,1,0:T(8,128)(2,1)S(1)}, u32[]{:S(2)}, u32[]{:S(2)}) collective-permute-start(bf16[16,64,256]{2,1,0:T(8,128)(2,1)S(1)} %dynamic-slice_convert_fusion.3), channel_id=1, source_target_pairs={{0,2},{1,3},{2,0},{3,1},{4,6},{5,7},{6,4},{7,5},{8,10},{9,11},{10,... | collective-permute-start | bytes 1572872 | tf_op jit(solution)/shard_map/ppermute | solution.py:300
  279.1 3.7 %copy-start.7 = (f32[16,128,256]{2,1,0:T(8,128)S(1)}, f32[16,128,256]{2,1,0:T(8,128)}, u32[]{:S(2)}) copy-start(f32[16,128,256]{2,1,0:T(8,128)} %get-tuple-element.36) | copy-start | bytes 6291460
  280.9 31.6 %collective-permute-start.7 = (bf16[16,64,256]{2,1,0:T(8,128)(2,1)S(1)}, bf16[16,64,256]{2,1,0:T(8,128)(2,1)S(1)}, u32[]{:S(2)}, u32[]{:S(2)}) collective-permute-start(bf16[16,64,256]{2,1,0:T(8,128)(2,1)S(1)} %dynamic-slice_convert_fusion), channel_id=1, source_target_pairs={{0,2},{1,3},{2,0},{3,1},{4,6},{5,7},{6,4},{7,5},{8,10},{9,11},{10,... | collective-permute-start | bytes 1572872 | tf_op jit(solution)/shard_map/ppermute | solution.py:300
  283.2 40.4 %collective-permute-start.5 = (bf16[16,64,256]{2,1,0:T(8,128)(2,1)S(1)}, bf16[16,64,256]{2,1,0:T(8,128)(2,1)S(1)}, u32[]{:S(2)}, u32[]{:S(2)}) collective-permute-start(bf16[16,64,256]{2,1,0:T(8,128)(2,1)S(1)} %dynamic-slice_convert_fusion.1), channel_id=1, source_target_pairs={{0,2},{1,3},{2,0},{3,1},{4,6},{5,7},{6,4},{7,5},{8,10},{9,11},{10,... | collective-permute-start | bytes 1572872 | tf_op jit(solution)/shard_map/ppermute | solution.py:300
  290.1 33.5 %copy-start.8 = (bf16[16,64,256]{2,1,0:T(8,128)(2,1)}, bf16[16,64,256]{2,1,0:T(8,128)(2,1)S(1)}, u32[]{:S(2)}) copy-start(bf16[16,64,256]{2,1,0:T(8,128)(2,1)S(1)} %collective-permute-done.3.refs_3_) | copy-start | bytes 1572868
  301.3 22.3 %copy-start.9 = (bf16[16,64,256]{2,1,0:T(8,128)(2,1)}, bf16[16,64,256]{2,1,0:T(8,128)(2,1)S(1)}, u32[]{:S(2)}) copy-start(bf16[16,64,256]{2,1,0:T(8,128)(2,1)S(1)} %collective-permute-done.1.refs_1_) | copy-start | bytes 1572868
  312.6 11.1 %copy-start.10 = (bf16[16,64,256]{2,1,0:T(8,128)(2,1)}, bf16[16,64,256]{2,1,0:T(8,128)(2,1)S(1)}, u32[]{:S(2)}) copy-start(bf16[16,64,256]{2,1,0:T(8,128)(2,1)S(1)} %collective-permute-done.7.refs_7_) | copy-start | bytes 1572868
  323.6 0.8 copy-start.11

commit v3 on v2

--- a/solution.py
+++ b/solution.py
@@ -241,64 +241,201 @@
     )(core, own_turned, mate)
 
 
-def final_kernel(*refs):
-    *in_refs, out_ref = refs
-    rows = 8
-    for turn_index in range(len(in_refs) // 2):
-        mine, theirs = in_refs[2 * turn_index], in_refs[2 * turn_index + 1]
-
-        def body(chunk, carry):
-            where = pl.ds(pl.multiple_of(chunk * 2 * rows, 2 * rows), 2 * rows)
-            value = mine[:, where, :] + theirs[:, where, :].astype(f32)
-            out_ref[where, turn_index] = jnp.swapaxes(value, 0, 1)
+def plan_kernel(partners_ref, mate_ref, back_ref, flip_ref):
+    rounds, blocks = partners_ref.shape
+    for task in range(rounds // 2):
+        first, second = 2 * task, 2 * task + 1
+
+        def clear(block, carry):
+            flip_ref[task, block] = -1
             return carry
 
-        lax.fori_loop(0, out_ref.shape[0] // (2 * rows), body, 0)
-
-
-def final(pairs):
+        def walk(block):
+            partner = partners_ref[first, block]
+            flip_ref[task, block] = 0
+            flip_ref[task, partner] = 1
+            mate_ref[task, block] = partner
+            back_ref[task, partner] = block
+            following = partners_ref[second, partner]
+            mate_ref[task, partner] = following
+            back_ref[task, following] = partner
+            return following
+
+        def start(block, carry):
+            lax.while_loop(lambda block: flip_ref[task, block] < 0, walk, block)
+            return carry
+
+        lax.fori_loop(0, blocks, clear, 0)
+        lax.fori_loop(0, blocks, start, 0)
+
+
+def plan(partners):
+    rounds, blocks = partners.shape
+    smem = pl.BlockSpec(memory_space=pltpu.SMEM)
+    table = jax.ShapeDtypeStruct((rounds // 2, blocks), jnp.int32)
+    return pl.pallas_call(
+        plan_kernel,
+        out_shape=[table] * 3,
+        in_specs=[smem],
+        out_specs=[smem] * 3,
+        compiler_params=params(),
+        name="plan",
+    )(partners)
+
+
+def core_sum_kernel(place_ref, keep_ref, recv_ref, own_ref, other_ref, send_ref):
+    chip = place_ref[1]
+    lags, rows, cols = own_ref.shape
+    half = cols // 2
+    own_rows = pl.ds(pl.multiple_of(chip * rows, rows), rows)
+    other_rows = pl.ds(pl.multiple_of((1 - chip) * rows, rows), rows)
+    own_cols = pl.ds(pl.multiple_of(chip * half, half), half)
+    other_cols = pl.ds(pl.multiple_of((1 - chip) * half, half), half)
+    for lag in range(lags):
+        own_ref[lag] = keep_ref[lag, own_rows, :] + recv_ref[lag, own_rows, :].astype(f32)
+        send_ref[lag] = (
+            keep_ref[lag, other_rows, :] + recv_ref[lag, other_rows, :].astype(f32)
+        ).astype(bf16)
+        if lag > 0:
+            other_ref[lag - 1] = keep_ref[lag, other_rows, own_cols] + recv_ref[
+                lag, other_rows, own_cols
+            ].astype(f32)
+            lane = (lag - 1) % 2 * half
+            send_ref[lags + (lag - 1) // 2, :, lane : lane + half] = (
+                keep_ref[lag, own_rows, other_cols]
+                + recv_ref[lag, own_rows, other_cols].astype(f32)
+            ).astype(bf16)
+
+
+def core_sum(place, keep, recv):
+    lags, rows, cols = keep.shape
+    vmem = pl.BlockSpec(memory_space=pltpu.VMEM)
+    return pl.pallas_call(
+        core_sum_kernel,
+        out_shape=[
+            jax.ShapeDtypeStruct((lags, rows // 2, cols), f32),
+            jax.ShapeDtypeStruct((lags - 1, rows // 2, cols // 2), f32),
+            jax.ShapeDtypeStruct((lags + (lags - 1) // 2, rows // 2, cols), bf16),
+        ],
+        in_specs=[pl.BlockSpec(memory_space=pltpu.SMEM), vmem, vmem],
+        out_specs=[vmem] * 3,
+        compiler_params=params(),
+        cost_estimate=pl.CostEstimate(flops=0, bytes_accessed=8_000_000, transcendentals=0),
+        name="core_sum",
+    )(place, keep, recv)
+
+
+def chip_sum_kernel(place_ref, own_ref, other_ref, recv_ref, mine_ref, keep_ref, send_ref):
+    core, chip = place_ref[0], place_ref[1]
+    lags, rows, cols = own_ref.shape
+    half = cols // 2
+    own_cols = pl.ds(pl.multiple_of(chip * half, half), half)
+    for lag in range(lags - 1):
+        mine_ref[lag] = own_ref[lag] + recv_ref[lag].astype(f32)
+    for back in range(lags - 1):
+        lag = lags - 1 - back
+        lane = (lag - 1) % 2 * half
+        own = own_ref[lag, :, own_cols] + recv_ref[lag, :, own_cols].astype(f32)
+        other = other_ref[lag - 1] + recv_ref[
+            lags + (lag - 1) // 2, :, lane : lane + half
+        ].astype(f32)
+        low = jnp.where(chip == 0, own, other)
+        high = jnp.where(chip == 0, other, own)
+        turned = jnp.concatenate([low, high], 0).T
+        keep_ref[back] = jnp.where(core == 0, turned[:rows], turned[rows:]).astype(bf16)
+        send_ref[back] = jnp.where(core == 0, turned[rows:], turned[:rows]).astype(bf16)
+
+
+def chip_sum(place, own, other, recv):
+    lags, rows, cols = own.shape
+    vmem = pl.BlockSpec(memory_space=pltpu.VMEM)
+    back = jax.ShapeDtypeStruct((lags - 1, rows, 2 * rows), bf16)
+    return pl.pallas_call(
+        chip_sum_kernel,
+        out_shape=[jax.ShapeDtypeStruct((lags - 1, rows, cols), f32), back, back],
+        in_specs=[pl.BlockSpec(memory_space=pltpu.SMEM), vmem, vmem, vmem],
+        out_specs=[vmem] * 3,
+        compiler_params=params(),
+        cost_estimate=pl.CostEstimate(flops=0, bytes_accessed=10_000_000, transcendentals=0),
+        name="chip_sum",
+    )(place, own, other, recv)
+
+
+def final_kernel(tasks, place_ref, flip_ref, *refs):
+    out_ref = refs[-1]
+    core, block = place_ref[0], place_ref[2]
+    for task in range(tasks):
+        mine_ref, back_ref = refs[2 * task], refs[2 * task + 1]
+        flip = flip_ref[task, block]
+        lags = mine_ref.shape[0]
+        out_ref[:, 2 * task + flip] = jnp.swapaxes(mine_ref[...], 0, 1)
+        near = back_ref[:lags].astype(f32)
+        far = back_ref[lags:].astype(f32)
+        first = jnp.where(core == 0, near, far)
+        second = jnp.where(core == 0, far, near)
+        lanes = first.shape[2]
+        lane = lax.broadcasted_iota(jnp.int32, first.shape, 2)
+        quarter = lanes // 2
+        low = jnp.where(lane < quarter, first, pltpu.roll(second, quarter, 2))
+        high = jnp.where(lane < quarter, pltpu.roll(first, quarter, 2), second)
+        out_ref[:, 2 * task + 1 - flip, :, :lanes] = jnp.swapaxes(low, 0, 1)
+        out_ref[:, 2 * task + 1 - flip, :, lanes:] = jnp.swapaxes(high, 0, 1)
+
+
+def final(place, flip, pairs):
     lags, rows, cols = pairs[0][0].shape
     flat = [array for pair in pairs for array in pair]
-    vmem = pl.BlockSpec(memory_space=pltpu.VMEM)
-    return pl.pallas_call(
-        final_kernel,
-        out_shape=jax.ShapeDtypeStruct((rows, len(pairs), lags, cols), f32),
-        in_specs=[vmem] * len(flat),
-        out_specs=vmem,
+    smem = pl.BlockSpec(memory_space=pltpu.SMEM)
+    step = 16
+    specs = [pl.BlockSpec((array.shape[0], step, array.shape[2]), lambda s: (0, s, 0)) for array in flat]
+    return pl.pallas_call(
+        functools.partial(final_kernel, len(pairs)),
+        grid=(rows // step,),
+        out_shape=jax.ShapeDtypeStruct((rows, 2 * len(pairs), lags, cols), f32),
+        in_specs=[smem, smem] + specs,
+        out_specs=pl.BlockSpec((step, 2 * len(pairs), lags, cols), lambda s: (s, 0, 0, 0)),
         compiler_params=params(),
         name="final",
-    )(*flat)
+    )(place, flip, *flat)
+
+
+def exchange(array):
+    return lax.all_to_all(array, "pair", split_axis=0, concat_axis=0, tiled=True)
 
 
 def local(spectra, channel_order, partners):
     num_bins, _, num_windows, cols = spectra.shape
     win_count = lax.axis_size("win")
-    place = lax.axis_index("win")
-    core = (place % 2).astype(jnp.int32)
-    chip = (place // 2).astype(jnp.int32)
+    win = lax.axis_index("win")
+    place = jnp.stack([win % 2, win // 2, lax.axis_index("pair")]).astype(jnp.int32)
     other_core = [(i, i ^ 1) for i in range(win_count)]
     other_chip = [(i, i ^ 2) for i in range(win_count)]
     norm = 1.0 / math.sqrt(num_windows * win_count * num_bins)
+    tasks = ROUNDS // 2
 
     own = whiten(spectra, channel_order).reshape(num_bins, 2 * num_windows, cols)
     own_turned = turn(own)
-    shares = lax.all_to_all(own, "pair", split_axis=0, concat_axis=0, tiled=True)
-    arranged = gather(shares, partners)
+    mate_of, back_of, flip = plan(partners)
+    shares = exchange(own)
+    arranged = list(gather(shares, mate_of))
+    arranged[0], own_turned = lax.optimization_barrier((arranged[0], own_turned))
+    mates = [exchange(arranged[task]) for task in range(tasks)]
     pairs = []
-    kept = []
-    for turn_index in range(ROUNDS):
-        operand = arranged[turn_index]
-        if turn_index >= 2:
-            operand, kept[turn_index - 2] = lax.optimization_barrier((operand, kept[turn_index - 2]))
-        mate = lax.all_to_all(operand, "pair", split_axis=0, concat_axis=0, tiled=True)
-        kept.append(correlate(own_turned, mate, core[None], norm, LAGS))
-    quarter = cols // 4
-    for keep, send in kept:
-        total = keep + lax.ppermute(send, "win", other_core).astype(f32)
-        mine = lax.dynamic_slice_in_dim(total, chip * quarter, quarter, 1)
-        others = lax.dynamic_slice_in_dim(total, (1 - chip) * quarter, quarter, 1).astype(bf16)
-        pairs.append((mine, lax.ppermute(others, "win", other_chip)))
-    return final(pairs)[None]
+    for task in range(tasks):
+        keep, send = correlate(own_turned, mates[task], place, norm, LAGS + 1)
+        own_sum, other_sum, chip_send = core_sum(
+            place, keep, lax.ppermute(send, "win", other_core)
+        )
+        if task + 1 < tasks:
+            mates[task + 1], chip_send = lax.optimization_barrier((mates[task + 1], chip_send))
+        mine, back_keep, back_send = chip_sum(
+            place, own_sum, other_sum, lax.ppermute(chip_send, "win", other_chip)
+        )
+        back_recv = lax.ppermute(back_send, "win", other_core)
+        spread = exchange(jnp.concatenate([back_keep, back_recv], 0))
+        (returned,) = gather(spread, back_of[task : task + 1])
+        pairs.append((mine, exchange(returned)))
+    return final(place, flip, pairs)[None]
 
 
 def solution(mesh):

time: 333 us -> 288 us (0.86)
  blocking collectives: 95.6 us -> 62.9 us
  waiting for transfers between devices: 110 us -> 89 us
  starting transfers between devices: 29.8 us -> 47.7 us
  Pallas kernels: 78.6 us -> 70.9 us
    all_to_all x2, blocking collectives: 95.6 us -> 62.9 us  [exchange(): lax.all_to_all(array, 'pair', split_axis=0, concat_axis=0, tiled=True)]
    pallas_call x4 -> x2, Pallas kernels: 50.5 us -> 25.3 us  [correlate(): pl.pallas_call(functools.partial(correlate_kernel, norm), grid=(num_bins...]
    all_to_all x3 -> x5, starting transfers between devices: 23.3 us -> 42.5 us  [exchange(): lax.all_to_all(array, 'pair', split_axis=0, concat_axis=0, tiled=True)]
    ppermute x8 -> x6, waiting for transfers between devices: 35.8 us -> 19.3 us  [the longest x2 12.5 us: local(): lax.ppermute(chip_send, 'win', other_chip)]
    pallas_call x1 -> x6, Pallas kernels: 5.91 us -> 21.7 us  [the longest x2 7.28 us: core_sum(): pl.pallas_call(core_sum_kernel, out_shape=[jax.ShapeDtypeStruct((lags, ro...]
    add x4 -> x0, other arithmetic: 6.25 us -> none  [local(): total = keep + lax.ppermute(send, 'win', other_core).astype(f32)]
    dynamic_slice x4 -> x0, local copies, waits for them, and re-layouts: 4.32 us -> none  [local(): mine = lax.dynamic_slice_in_dim(total, chip * quarter, quarter, 1)]
    all_to_all x3 -> x5, waiting for transfers between devices: 73.7 us -> 69.7 us  [exchange(): lax.all_to_all(array, 'pair', split_axis=0, concat_axis=0, tiled=True)]
  transfers between devices with their start and end apart: 11 -> 11, of which waited for: 7 -> 11; matrix products, arithmetic and copies ran while one was open for 3% -> 2% of each run, Pallas kernels for 18% -> 15%
where the time goes in v3:
time: 288 us; the launch traced here: 283 us
  waiting for transfers between devices  89 us (31%)
  Pallas kernels  70.9 us (25%)
  blocking collectives  62.9 us (22%)
  starting transfers between devices  47.7 us (17%)
  local copies, waits for them, and re-layouts  7.7 us (3%)
  other arithmetic  4.23 us (1%)
    all_to_all x5, waiting for transfers between devices, exchange(): lax.all_to_all(array, 'pair', split_axis=0, concat_axis=0, tiled=True)  69.7 us
    all_to_all x2, blocking collectives, exchange(): lax.all_to_all(array, 'pair', split_axis=0, concat_axis=0, tiled=True)  62.9 us
    all_to_all x5, starting transfers between devices, exchange(): lax.all_to_all(array, 'pair', split_axis=0, concat_axis=0, tiled=True)  42.5 us
    pallas_call x2, Pallas kernels, correlate(): pl.pallas_call(functools.partial(correlate_kernel, norm), grid=(num_bins...  25.3 us
    ppermute x2, waiting for transfers between devices, local(): lax.ppermute(chip_send, 'win', other_chip)  12.5 us
    pallas_call x3, Pallas kernels, gather(): pl.pallas_call(gather_kernel, out_shape=[jax.ShapeDtypeStruct((places,) +...  9.35 us
    pallas_call x1, Pallas kernels, turn(): pl.pallas_call(turn_kernel, grid=(num_bins // bins,), out_shape=jax.Shape...  8.29 us
    pallas_call x2, Pallas kernels, core_sum(): pl.pallas_call(core_sum_kernel, out_shape=[jax.ShapeDtypeStruct((lags, ro...  7.28 us
  transfers between devices with their start and end apart: 11, of which 11 were waited for; matrix products, arithmetic and copies ran while one was open for 2% of the time, Pallas kernels for 15%

profile of v3, /device:TPU:16, one launch (start us, length us, event | category | flops | bytes accessed | tf_op | source)
XLA Modules:
  0.0 282.5 jit_solution(16532742143285959648)
XLA Ops:
  0.0 6.2 %whiten.1 = bf16[32,2,96,256]{3,2,1,0:T(8,128)(2,1)} custom-call(s32[1,256]{1,0:T(1,128)} %order_ref.1, bf16[32,2,96,256]{3,2,1,0:T(8,128)(2,1)} %spectra_ref.1), custom_call_target="tpu_custom_call" | custom-call | tf_op jit(solution)/shard_map/whiten/pallas_call | solution.py:45
  6.2 10.9 %all-to-all-start = ((bf16[32,192,256]{2,1,0:T(8,128)(2,1)}), bf16[32,192,256]{2,1,0:T(8,128)(2,1)S(1)}, u32[]{:S(2)}, u32[]{:S(2)}) async-start(bf16[32,192,256]{2,1,0:T(8,128)(2,1)} %bitcast.5), calls=%async_computation | async-start | bytes 6291456 | tf_op jit(solution)/shard_map/all_to_all | solution.py:403
  17.1 8.3 %turn.1.own_ref = bf16[32,512,192]{2,1,0:T(8,128)(2,1)} custom-call(bf16[32,192,256]{2,1,0:T(8,128)(2,1)} %bitcast.6), custom_call_target="tpu_custom_call" | custom-call | bytes 12000000 | tf_op jit(solution)/shard_map/turn/pallas_call | solution.py:76
  25.4 3.3 %plan.1 = (s32[2,32]{1,0:T(2,128)}, s32[2,32]{1,0:T(2,128)}, s32[2,32]{1,0:T(2,128)}) custom-call(s32[4,32]{1,0:T(4,128)} %partners_ref.1), custom_call_target="tpu_custom_call" | custom-call | tf_op jit(solution)/shard_map/plan/pallas_call | solution.py:276
  28.8 30.6 %all-to-all-done.source_ref = bf16[32,192,256]{2,1,0:T(8,128)(2,1)S(1)} async-done(((bf16[32,192,256]{2,1,0:T(8,128)(2,1)}), bf16[32,192,256]{2,1,0:T(8,128)(2,1)S(1)}, u32[]{:S(2)}, u32[]{:S(2)}) %all-to-all-start) | async-done | bytes 3145760 | tf_op jit(solution)/shard_map/all_to_all | solution.py:403
  59.4 1.7 copy-done
  61.0 5.1 %gather.3 = (bf16[32,192,256]{2,1,0:T(8,128)(2,1)}, bf16[32,192,256]{2,1,0:T(8,128)(2,1)}) custom-call(s32[2,32]{1,0:T(2,128)} %get-tuple-element.31.index_ref, bf16[32,192,256]{2,1,0:T(8,128)(2,1)} %copy-done), custom_call_target="tpu_custom_call" | custom-call | tf_op jit(solution)/shard_map/gather/pallas_call | solution.py:104
  66.1 46.2 %all_to_all.35.mate_ref = bf16[32,192,256]{2,1,0:T(8,128)(2,1)} all-to-all(bf16[32,192,256]{2,1,0:T(8,128)(2,1)} %get-tuple-element.34), channel_id=1, replica_groups=mesh['pair'=32,'win'=4] {'pair'}, dimensions={0} | all-to-all | bytes 6291456 | tf_op jit(solution)/shard_map/all_to_all | solution.py:403
  112.3 6.9 %all-to-all-start.2 = ((bf16[32,192,256]{2,1,0:T(8,128)(2,1)}), bf16[32,192,256]{2,1,0:T(8,128)(2,1)S(1)}, u32[]{:S(2)}, u32[]{:S(2)}) async-start(bf16[32,192,256]{2,1,0:T(8,128)(2,1)} %get-tuple-element.39), calls=%async_computation.2 | async-start | bytes 6291456 | tf_op jit(solution)/shard_map/all_to_all | solution.py:403
  119.3 0.7 pad_add_fusion.core_ref.place_ref
  119.9 12.6 %correlate.2 = (f32[17,128,256]{2,1,0:T(8,128)}, bf16[17,128,256]{2,1,0:T(8,128)(2,1)}) custom-call(s32[3]{0:T(128)} %pad_add_fusion.core_ref.place_ref, bf16[32,512,192]{2,1,0:T(8,128)(2,1)} %turn.1.own_ref, bf16[32,192,256]{2,1,0:T(8,128)(2,1)} %all_to_all.35.mate_ref), custom_call_target="tpu_custom_call" | custom-call | flops 1610612736 | bytes 20000000 | tf_op jit(solution)/shard_map/correlate/pallas_call | solution.py:219
  132.5 0.0 collective-permute-start
  132.5 3.0 %collective-permute-done.recv_ref = bf16[17,128,256]{2,1,0:T(8,128)(2,1)S(1)} collective-permute-done((bf16[17,128,256]{2,1,0:T(8,128)(2,1)}, bf16[17,128,256]{2,1,0:T(8,128)(2,1)S(1)}, u32[]{:S(2)}, u32[]{:S(2)}) %collective-permute-start) | collective-permute-done | bytes 1114144 | tf_op jit(solution)/shard_map/ppermute | solution.py:427
  135.5 1.0 copy-done.6
  136.5 3.6 %core_sum.2 = (f32[17,64,256]{2,1,0:T(8,128)}, f32[16,64,128]{2,1,0:T(8,128)}, bf16[25,64,256]{2,1,0:T(8,128)(2,1)}) custom-call(s32[3]{0:T(128)} %pad_add_fusion.core_ref.place_ref, f32[17,128,256]{2,1,0:T(8,128)} %get-tuple-element.35.keep_ref, bf16[17,128,256]{2,1,0:T(8,128)(2,1)} %copy-done.6), custom_call_target="tpu_custom_call" | custom-call | bytes 8000000 | tf_op jit(solution)/shard_map/core_sum/pallas_call | solution.py:313
  140.1 20.2 %all-to-all-done.2.mate_ref = bf16[32,192,256]{2,1,0:T(8,128)(2,1)S(1)} async-done(((bf16[32,192,256]{2,1,0:T(8,128)(2,1)}), bf16[32,192,256]{2,1,0:T(8,128)(2,1)S(1)}, u32[]{:S(2)}, u32[]{:S(2)}) %all-to-all-start.2) | async-done | bytes 3145760 | tf_op jit(solution)/shard_map/all_to_all | solution.py:403
  160.3 1.7 copy-done.1
  162.0 12.6 %correlate.3 = (f32[17,128,256]{2,1,0:T(8,128)}, bf16[17,128,256]{2,1,0:T(8,128)(2,1)}) custom-call(s32[3]{0:T(128)} %pad_add_fusion.core_ref.place_ref, bf16[32,512,192]{2,1,0:T(8,128)(2,1)} %turn.1.own_ref, bf16[32,192,256]{2,1,0:T(8,128)(2,1)} %copy-done.1), custom_call_target="tpu_custom_call" | custom-call | flops 1610612736 | bytes 20000000 | tf_op jit(solution)/shard_map/correlate/pallas_call | solution.py:219
  174.6 0.0 collective-permute-start.3
  174.6 2.6 collective-permute-start.1
  177.3 0.3 collective-permute-done.3.recv_ref
  177.6 1.0 copy-done.5
  178.6 3.6 %core_sum.3 = (f32[17,64,256]{2,1,0:T(8,128)}, f32[16,64,128]{2,1,0:T(8,128)}, bf16[25,64,256]{2,1,0:T(8,128)(2,1)}) custom-call(s32[3]{0:T(128)} %pad_add_fusion.core_ref.place_ref, f32[17,128,256]{2,1,0:T(8,128)} %get-tuple-element.47.keep_ref, bf16[17,128,256]{2,1,0:T(8,128)(2,1)} %copy-done.5), custom_call_target="tpu_custom_call" | custom-call | bytes 8000000 | tf_op jit(solution)/shard_map/core_sum/pallas_call | solution.py:313
  182.2 2.5 collective-permute-start.4
  184.7 11.6 %collective-permute-done.1.recv_ref = bf16[25,64,256]{2,1,0:T(8,128)(2,1)S(1)} collective-permute-done((bf16[25,64,256]{2,1,0:T(8,128)(2,1)S(1)}, bf16[25,64,256]{2,1,0:T(8,128)(2,1)S(1)}, u32[]{:S(2)}, u32[]{:S(2)}) %collective-permute-start.1) | collective-permute-done | bytes 819232 | tf_op jit(solution)/shard_map/ppermute | solution.py:432
  196.4 0.9 copy-done.8
  197.2 3.1 %chip_sum.2 = (f32[16,64,256]{2,1,0:T(8,128)}, bf16[16,64,128]{2,1,0:T(8,128)(2,1)}, bf16[16,64,128]{2,1,0:T(8,128)(2,1)}) custom-call(s32[3]{0:T(128)} %pad_add_fusion.core_ref.place_ref, f32[17,64,256]{2,1,0:T(8,128)} %get-tuple-element.37.own_ref, f32[16,64,128]{2,1,0:T(8,128)} %get-tuple-element.38.other_ref, bf16[25,64,256]{2,1,0:T(8,128)(2,1)} %copy-done.8), custom_call_target="tpu_custom_call" | custom-call | bytes 10000000 | tf_op jit(solution)/shard_map/chip_sum/pallas_call | solution.py:353
  200.3 0.0 collective-permute-start.2
  200.3 1.7 collective-permute-done.2
  202.1 1.8 pad_maximum_fusion
  203.9 8.8 %all-to-all-start.3 = ((bf16[32,64,128]{2,1,0:T(8,128)(2,1)}), bf16[32,64,128]{2,1,0:T(8,128)(2,1)S(1)}, u32[]{:S(2)}, u32[]{:S(2)}) async-start(bf16[32,64,128]{2,1,0:T(8,128)(2,1)} %pad_maximum_fusion), calls=%async_computation.3 | async-start | bytes 1048576 | tf_op jit(solution)/shard_map/all_to_all | solution.py:403
  212.7 0.9 collective-permute-done.4.recv_ref
  213.7 0.9 copy-done.7
  214.5 3.1 %chip_sum.3 = (f32[16,64,256]{2,1,0:T(8,128)}, bf16[16,64,128]{2,1,0:T(8,128)(2,1)}, bf16[16,64,128]{2,1,0:T(8,128)(2,1)}) custom-call(s32[3]{0:T(128)} %pad_add_fusion.core_ref.place_ref, f32[17,64,256]{2,1,0:T(8,128)} %get-tuple-element.49.own_ref, f32[16,64,128]{2,1,0:T(8,128)} %get-tuple-element.50.other_ref, bf16[25,64,256]{2,1,0:T(8,128)(2,1)} %copy-done.7), custom_call_target="tpu_custom_call" | custom-call | bytes 10000000 | tf_op jit(solution)/shard_map/chip_sum/pallas_call | solution.py:353
  217.6 0.0 collective-permute-start.5
  217.6 1.7 collective-permute-done.5
  219.3 1.8 pad_maximum_fusion.1
  221.1 2.8 all-to-all-done.3.source_ref
  223.9 9.4 %all-to-all-start.5 = ((bf16[32,64,128]{2,1,0:T(8,128)(2,1)}), bf16[32,64,128]{2,1,0:T(8,128)(2,1)S(1)}, u32[]{:S(2)}, u32[]{:S(2)}) async-start(bf16[32,64,128]{2,1,0:T(8,128)(2,1)} %pad_maximum_fusion.1), calls=%async_computation.5 | async-start | bytes 1048576 | tf_op jit(solution)/shard_map/all_to_all | solution.py:403
  233.4 0.6 fusion
  234.0 0.0 copy-done.2
  234.0 2.1 gather.4
  236.1 8.4 %all-to-all-done.5.source_ref = bf16[32,64,128]{2,1,0:T(8,128)(2,1)S(1)} async-done(((bf16[32,64,128]{2,1,0:T(8,128)(2,1)}), bf16[32,64,128]{2,1,0:T(8,128)(2,1)S(1)}, u32[]{:S(2)}, u32[]{:S(2)}) %all-to-all-start.5) | async-done | bytes 524320 | tf_op jit(solution)/shard_map/all_to_all | solution.py:403
  244.5 6.5 %all-to-all-start.4 = ((bf16[32,64,128]{2,1,0:T(8,128)(2,1)}), bf16[32,64,128]{2,1,0:T(8,128)(2,1)S(1)}, u32[]{:S(2)}, u32[]{:S(2)}) async-start(bf16[32,64,128]{2,1,0:T(8,128)(2,1)} %gather.4), calls=%async_computation.4 | async-start | bytes 1048576 | tf_op jit(solution)/shard_map/all_to_all | solution.py:403
  251.0 2.1 gather.5
  253.2 7.7 %all-to-all-done.4.refs_1_ = bf16[32,64,128]{2,1,0:T(8,128)(2,1)S(1)} async-done(((bf16[32,64,128]{2,1,0:T(8,128)(2,1)}), bf16[32,64,128]{2,1,0:T(8,128)(2,1)S(1)}, u32[]{:S(2)}, u32[]{:S(2)}) %all-to-all-start.4) | async-done | bytes 524320 | tf_op jit(solution)/shard_map/all_to_all | solution.py:403
  260.8 16.7 %all_to_all.36.refs_3_ = bf16[32,64,128]{2,1,0:T(8,128)(2,1)} all-to-all(bf16[32,64,128]{2,1,0:T(8,128)(2,1)} %gather.5), channel_id=1, replica_groups=mesh['pair'=32,'win'=4] {'pair'}, dimensions={0} | all-to-all | bytes 1048576 | tf_op jit(solution)/shard_map/all_to_all | solution.py:403
  277.6 5.0 %final.1 = f32[64,4,16,256]{3,2,1,0:T(8,128)} custom-call(s32[3]{0:T(128)} %pad_add_fusion.core_ref.place_ref, s32[2,32]{1,0:T(2,128)} %get-tuple-element.30.flip_ref, f32[16,64,256]{2,1,0:T(8,128)} %get-tuple-element.42.refs_0_, bf16[32,64,128]{2,1,0:T(8,128)(2,1)} %copy-done.4, f32[16,64,256]{2,1,0:T(8,128)} %get-tuple-element.52.refs_2_, ...), custom_call_target="tpu_custom_call" | custom-call | tf_op jit(solution)/shard_map/final/pallas_call | solution.py:391
  (15 shorter events, 0.0 us)
Async XLA Ops:
  6.2 53.1 %all-to-all-start = ((bf16[32,192,256]{2,1,0:T(8,128)(2,1)}), bf16[32,192,256]{2,1,0:T(8,128)(2,1)S(1)}, u32[]{:S(2)}, u32[]{:S(2)}) async-start(bf16[32,192,256]{2,1,0:T(8,128)(2,1)} %bitcast.5), calls=%async_computation | async-start | bytes 6291456 | tf_op jit(solution)/shard_map/all_to_all | solution.py:403
  59.4 1.7 copy-start
  112.3 48.0 %all-to-all-start.2 = ((bf16[32,192,256]{2,1,0:T(8,128)(2,1)}), bf16[32,192,256]{2,1,0:T(8,128)(2,1)S(1)}, u32[]{:S(2)}, u32[]{:S(2)}) async-start(bf16[32,192,256]{2,1,0:T(8,128)(2,1)} %get-tuple-element.39), calls=%async_computation.2 | async-start | bytes 6291456 | tf_op jit(solution)/shard_map/all_to_all | solution.py:403
  132.5 3.0 %collective-permute-start = (bf16[17,128,256]{2,1,0:T(8,128)(2,1)}, bf16[17,128,256]{2,1,0:T(8,128)(2,1)S(1)}, u32[]{:S(2)}, u32[]{:S(2)}) collective-permute-start(bf16[17,128,256]{2,1,0:T(8,128)(2,1)} %get-tuple-element.36), channel_id=1, source_target_pairs={{0,1},{1,0},{2,3},{3,2},{4,5},{5,4},{6,7},{7,6},{8,9},{9,8},{10,11... | collective-permute-start | bytes 3342344 | tf_op jit(solution)/shard_map/ppermute | solution.py:427
  135.5 1.0 copy-start.6
  160.3 1.7 copy-start.1
  162.0 12.7 %copy-start.10 = (bf16[25,64,256]{2,1,0:T(8,128)(2,1)S(1)}, bf16[25,64,256]{2,1,0:T(8,128)(2,1)}, u32[]{:S(2)}) copy-start(bf16[25,64,256]{2,1,0:T(8,128)(2,1)} %get-tuple-element.41) | copy-start | bytes 2457604
  174.6 3.0 %collective-permute-start.3 = (bf16[17,128,256]{2,1,0:T(8,128)(2,1)}, bf16[17,128,256]{2,1,0:T(8,128)(2,1)S(1)}, u32[]{:S(2)}, u32[]{:S(2)}) collective-permute-start(bf16[17,128,256]{2,1,0:T(8,128)(2,1)} %get-tuple-element.48), channel_id=1, source_target_pairs={{0,1},{1,0},{2,3},{3,2},{4,5},{5,4},{6,7},{7,6},{8,9},{9,8},{10,11... | collective-permute-start | bytes 3342344 | tf_op jit(solution)/shard_map/ppermute | solution.py:427
  174.6 21.7 %collective-permute-start.1 = (bf16[25,64,256]{2,1,0:T(8,128)(2,1)S(1)}, bf16[25,64,256]{2,1,0:T(8,128)(2,1)S(1)}, u32[]{:S(2)}, u32[]{:S(2)}) collective-permute-start(bf16[25,64,256]{2,1,0:T(8,128)(2,1)S(1)} %copy-done.10), channel_id=1, source_target_pairs={{0,2},{1,3},{2,0},{3,1},{4,6},{5,7},{6,4},{7,5},{8,10},{9,11},{10,... | collective-permute-start | bytes 2457608 | tf_op jit(solution)/shard_map/ppermute | solution.py:432
  177.6 1.0 copy-start.5
  182.2 31.4 %collective-permute-start.4 = (bf16[25,64,256]{2,1,0:T(8,128)(2,1)}, bf16[25,64,256]{2,1,0:T(8,128)(2,1)S(1)}, u32[]{:S(2)}, u32[]{:S(2)}) collective-permute-start(bf16[25,64,256]{2,1,0:T(8,128)(2,1)} %get-tuple-element.51), channel_id=1, source_target_pairs={{0,2},{1,3},{2,0},{3,1},{4,6},{5,7},{6,4},{7,5},{8,10},{9,11},{10,... | collective-permute-start | bytes 2457608 | tf_op jit(solution)/shard_map/ppermute | solution.py:432
  196.4 0.9 copy-start.8
  200.3 1.7 collective-permute-start.2
  202.1 31.3 %copy-start.9 = (s32[2,32]{1,0:T(2,128)S(1)}, s32[2,32]{1,0:T(2,128)}, u32[]{:S(2)}) copy-start(s32[2,32]{1,0:T(2,128)} %get-tuple-element.43) | copy-start | bytes 772
  203.9 20.1 %all-to-all-start.3 = ((bf16[32,64,128]{2,1,0:T(8,128)(2,1)}), bf16[32,64,128]{2,1,0:T(8,128)(2,1)S(1)}, u32[]{:S(2)}, u32[]{:S(2)}) async-start(bf16[32,64,128]{2,1,0:T(8,128)(2,1)} %pad_maximum_fusion), calls=%async_computation.3 | async-start | bytes 1048576 | tf_op jit(solution)/shard_map/all_to_all | solution.py:403
  213.6 0.9 copy-start.7
  217.6 1.7 collective-permute-start.5
  223.9 10.0 %copy-start.2 = (bf16[32,64,128]{2,1,0:T(8,128)(2,1)}, bf16[32,64,128]{2,1,0:T(8,128)(2,1)S(1)}, u32[]{:S(2)}) copy-start(bf16[32,64,128]{2,1,0:T(8,128)(2,1)S(1)} %all-to-all-done.3.source_ref) | copy-start | bytes 1572868
  223.9 20.6 %all-to-all-start.5 = ((bf16[32,64,128]{2,1,0:T(8,128)(2,1)}), bf16[32,64,128]{2,1,0:T(8,128)(2,1)S(1)}, u32[]{:S(2)}, u32[]{:S(2)}) async-start(bf16[32,64,128]{2,1,0:T(8,128)(2,1)} %pad_maximum_fusion.1), calls=%async_computation.5 | async-start | bytes 1048576 | tf_op jit(solution)/shard_map/all_to_all | solution.py:403
  244.5 6.5 %copy-start.3 = (bf16[32,64,128]{2,1,0:T(8,128)(2,1)}, bf16[32,64,128]{2,1,0:T(8,128)(2,1)S(1)}, u32[]{:S(2)}) copy-start(bf16[32,64,128]{2,1,0:T(8,128)(2,1)S(1)} %all-to-all-done.5.source_ref) | copy-start | bytes 1572868
  244.5 16.3 %all-to-all-start.4 = ((bf16[32,64,128]{2,1,0:T(8,128)(2,1)}), bf16[32,64,128]{2,1,0:T(8,128)(2,1)S(1)}, u32[]{:S(2)}, u32[]{:S(2)}) async-start(bf16[32,64,128]{2,1,0:T(8,128)(2,1)} %gather.4), calls=%async_computation.4 | async-start | bytes 1048576 | tf_op jit(solution)/shard_map/all_to_all | solution.py:403
  260.8 16.8 %copy-start.4 = (bf16[32,64,128]{2,1,0:T(8,128)(2,1)}, bf16[32,64,128]{2,1,0:T(8,128)(2,1)S(1)}, u32[]{:S(2)}) copy-start(bf16[32,64,128]{2,1,0:T(8,128)(2,1)S(1)} %all-to-all-done.4.refs_1_) | copy-start | bytes 1572868

commit v4 on v3

--- a/solution.py
+++ b/solution.py
@@ -283,28 +283,27 @@
     )(partners)
 
 
-def core_sum_kernel(place_ref, keep_ref, recv_ref, own_ref, other_ref, send_ref):
+def core_sum_kernel(place_ref, keep_ref, recv_ref, near_ref, far_ref, turn_ref, rest_ref):
     chip = place_ref[1]
-    lags, rows, cols = own_ref.shape
-    half = cols // 2
-    own_rows = pl.ds(pl.multiple_of(chip * rows, rows), rows)
-    other_rows = pl.ds(pl.multiple_of((1 - chip) * rows, rows), rows)
+    lags, rows, half = near_ref.shape
+    count = rows // 2
+    own_rows = pl.ds(pl.multiple_of(chip * count, count), count)
+    other_rows = pl.ds(pl.multiple_of((1 - chip) * count, count), count)
     own_cols = pl.ds(pl.multiple_of(chip * half, half), half)
     other_cols = pl.ds(pl.multiple_of((1 - chip) * half, half), half)
+
+    def total(lag, where, columns):
+        return keep_ref[lag, where, columns] + recv_ref[lag, where, columns].astype(f32)
+
+    everything = slice(None)
+    rest_ref[lags - 1] = total(0, other_rows, other_cols).astype(bf16)
     for lag in range(lags):
-        own_ref[lag] = keep_ref[lag, own_rows, :] + recv_ref[lag, own_rows, :].astype(f32)
-        send_ref[lag] = (
-            keep_ref[lag, other_rows, :] + recv_ref[lag, other_rows, :].astype(f32)
-        ).astype(bf16)
+        near_ref[lag] = total(lag, everything, own_cols)
         if lag > 0:
-            other_ref[lag - 1] = keep_ref[lag, other_rows, own_cols] + recv_ref[
-                lag, other_rows, own_cols
-            ].astype(f32)
-            lane = (lag - 1) % 2 * half
-            send_ref[lags + (lag - 1) // 2, :, lane : lane + half] = (
-                keep_ref[lag, own_rows, other_cols]
-                + recv_ref[lag, own_rows, other_cols].astype(f32)
-            ).astype(bf16)
+            turn_ref[lag - 1] = total(lag, everything, other_cols).astype(bf16)
+        if lag < lags - 1:
+            far_ref[lag] = total(lag, own_rows, other_cols)
+            rest_ref[lag] = total(lag, other_rows, own_cols).astype(bf16)
 
 
 def core_sum(place, keep, recv):
@@ -313,94 +312,170 @@
     return pl.pallas_call(
         core_sum_kernel,
         out_shape=[
-            jax.ShapeDtypeStruct((lags, rows // 2, cols), f32),
+            jax.ShapeDtypeStruct((lags, rows, cols // 2), f32),
             jax.ShapeDtypeStruct((lags - 1, rows // 2, cols // 2), f32),
-            jax.ShapeDtypeStruct((lags + (lags - 1) // 2, rows // 2, cols), bf16),
+            jax.ShapeDtypeStruct((lags - 1, rows, cols // 2), bf16),
+            jax.ShapeDtypeStruct((lags, rows // 2, cols // 2), bf16),
         ],
         in_specs=[pl.BlockSpec(memory_space=pltpu.SMEM), vmem, vmem],
-        out_specs=[vmem] * 3,
-        compiler_params=params(),
-        cost_estimate=pl.CostEstimate(flops=0, bytes_accessed=8_000_000, transcendentals=0),
+        out_specs=[vmem] * 4,
+        compiler_params=params(),
+        cost_estimate=pl.CostEstimate(flops=0, bytes_accessed=10_000_000, transcendentals=0),
         name="core_sum",
     )(place, keep, recv)
 
 
-def chip_sum_kernel(place_ref, own_ref, other_ref, recv_ref, mine_ref, keep_ref, send_ref):
-    core, chip = place_ref[0], place_ref[1]
-    lags, rows, cols = own_ref.shape
-    half = cols // 2
-    own_cols = pl.ds(pl.multiple_of(chip * half, half), half)
-    for lag in range(lags - 1):
-        mine_ref[lag] = own_ref[lag] + recv_ref[lag].astype(f32)
+def mirror_kernel(place_ref, near_ref, recv_ref, *refs):
+    *earlier_refs, back_ref = refs
+    core = place_ref[0]
+    lags, rows, _ = near_ref.shape
+    task = len(earlier_refs)
+    for index, earlier_ref in enumerate(earlier_refs):
+        back_ref[:, index] = earlier_ref[:, index]
     for back in range(lags - 1):
         lag = lags - 1 - back
-        lane = (lag - 1) % 2 * half
-        own = own_ref[lag, :, own_cols] + recv_ref[lag, :, own_cols].astype(f32)
-        other = other_ref[lag - 1] + recv_ref[
-            lags + (lag - 1) // 2, :, lane : lane + half
-        ].astype(f32)
-        low = jnp.where(chip == 0, own, other)
-        high = jnp.where(chip == 0, other, own)
-        turned = jnp.concatenate([low, high], 0).T
-        keep_ref[back] = jnp.where(core == 0, turned[:rows], turned[rows:]).astype(bf16)
-        send_ref[back] = jnp.where(core == 0, turned[rows:], turned[:rows]).astype(bf16)
-
-
-def chip_sum(place, own, other, recv):
-    lags, rows, cols = own.shape
+        turned = (near_ref[lag] + recv_ref[lag - 1].astype(f32)).T
+        low, high = turned[: rows // 2], turned[rows // 2 :]
+        back_ref[back, task] = jnp.where(core == 0, low, high).astype(bf16)
+        back_ref[lags - 1 + back, task] = jnp.where(core == 0, high, low).astype(bf16)
+
+
+def mirror(place, near, recv, earlier):
+    lags, rows, cols = near.shape
     vmem = pl.BlockSpec(memory_space=pltpu.VMEM)
-    back = jax.ShapeDtypeStruct((lags - 1, rows, 2 * rows), bf16)
-    return pl.pallas_call(
-        chip_sum_kernel,
-        out_shape=[jax.ShapeDtypeStruct((lags - 1, rows, cols), f32), back, back],
-        in_specs=[pl.BlockSpec(memory_space=pltpu.SMEM), vmem, vmem, vmem],
-        out_specs=[vmem] * 3,
-        compiler_params=params(),
-        cost_estimate=pl.CostEstimate(flops=0, bytes_accessed=10_000_000, transcendentals=0),
-        name="chip_sum",
-    )(place, own, other, recv)
-
-
-def final_kernel(tasks, place_ref, flip_ref, *refs):
+    return pl.pallas_call(
+        mirror_kernel,
+        out_shape=jax.ShapeDtypeStruct((2 * (lags - 1), len(earlier) + 1, cols // 2, rows), bf16),
+        in_specs=[pl.BlockSpec(memory_space=pltpu.SMEM), vmem, vmem] + [vmem] * len(earlier),
+        out_specs=vmem,
+        compiler_params=params(),
+        cost_estimate=pl.CostEstimate(flops=0, bytes_accessed=8_000_000, transcendentals=0),
+        name="mirror",
+    )(place, near, recv, *earlier)
+
+
+def own_rows_kernel(flip_ref, place_ref, near_ref, far_ref, turn_ref, rest_ref, *refs):
     out_ref = refs[-1]
-    core, block = place_ref[0], place_ref[2]
-    for task in range(tasks):
-        mine_ref, back_ref = refs[2 * task], refs[2 * task + 1]
-        flip = flip_ref[task, block]
-        lags = mine_ref.shape[0]
-        out_ref[:, 2 * task + flip] = jnp.swapaxes(mine_ref[...], 0, 1)
-        near = back_ref[:lags].astype(f32)
-        far = back_ref[lags:].astype(f32)
-        first = jnp.where(core == 0, near, far)
-        second = jnp.where(core == 0, far, near)
-        lanes = first.shape[2]
-        lane = lax.broadcasted_iota(jnp.int32, first.shape, 2)
-        quarter = lanes // 2
-        low = jnp.where(lane < quarter, first, pltpu.roll(second, quarter, 2))
-        high = jnp.where(lane < quarter, pltpu.roll(first, quarter, 2), second)
-        out_ref[:, 2 * task + 1 - flip, :, :lanes] = jnp.swapaxes(low, 0, 1)
-        out_ref[:, 2 * task + 1 - flip, :, lanes:] = jnp.swapaxes(high, 0, 1)
-
-
-def final(place, flip, pairs):
-    lags, rows, cols = pairs[0][0].shape
-    flat = [array for pair in pairs for array in pair]
+    chip = place_ref[1]
+    lags, step, half = far_ref.shape
+    near = near_ref[:lags]
+    first = near[:1] + rest_ref[lags:].astype(f32)
+    near = jnp.concatenate([first, near[1:] + turn_ref[: lags - 1].astype(f32)], 0)
+    far = far_ref[...] + rest_ref[:lags].astype(f32)
+    out_ref[:, 0, :, :half] = jnp.swapaxes(jnp.where(chip == 0, near, far), 0, 1)
+    out_ref[:, 0, :, half:] = jnp.swapaxes(jnp.where(chip == 0, far, near), 0, 1)
+
+
+def own_rows(place, flip, task, near, far, turn, rest, out):
+    lags, rows, half = far.shape
+    step = 16
+    count = rows // step
     smem = pl.BlockSpec(memory_space=pltpu.SMEM)
+
+    def piece(array):
+        return pl.BlockSpec((array.shape[0], step, half), lambda s, flip, place: (0, s, 0))
+
+    def half_piece(array):
+        return pl.BlockSpec(
+            (array.shape[0], step, half), lambda s, flip, place: (0, place[1] * count + s, 0)
+        )
+
+    extra = [] if out is None else [out]
+    return pl.pallas_call(
+        own_rows_kernel,
+        out_shape=jax.ShapeDtypeStruct((rows, ROUNDS, lags, 2 * half), f32),
+        grid_spec=pltpu.PrefetchScalarGridSpec(
+            num_scalar_prefetch=2,
+            grid=(count,),
+            in_specs=[half_piece(near), piece(far), half_piece(turn), piece(rest)]
+            + [pl.BlockSpec(memory_space=pl.ANY)] * len(extra),
+            out_specs=pl.BlockSpec(
+                (step, 1, lags, 2 * half),
+                lambda s, flip, place: (s, 2 * task + flip[task, place[2]], 0, 0),
+            ),
+        ),
+        input_output_aliases={6: 0} if extra else {},
+        compiler_params=params(),
+        cost_estimate=pl.CostEstimate(flops=0, bytes_accessed=5_000_000, transcendentals=0),
+        name="own_rows",
+    )(flip, place, near, far, turn, rest, *extra)
+
+
+def gather_back_kernel(index_ref, source_ref, out_ref, sems):
+    places, tasks = out_ref.shape[:2]
+    copies = []
+    for place in range(places):
+        for task in range(tasks):
+            copy = pltpu.make_async_copy(
+                source_ref.at[index_ref[task, place], task],
+                out_ref.at[place, task],
+                sems.at[task, place],
+            )
+            copy.start()
+            copies.append(copy)
+    for copy in copies:
+        copy.wait()
+
+
+def gather_back(source, index):
+    return pl.pallas_call(
+        gather_back_kernel,
+        out_shape=jax.ShapeDtypeStruct(source.shape, source.dtype),
+        in_specs=[
+            pl.BlockSpec(memory_space=pltpu.SMEM),
+            pl.BlockSpec(memory_space=pltpu.VMEM),
+        ],
+        out_specs=pl.BlockSpec(memory_space=pl.ANY),
+        scratch_shapes=[pltpu.SemaphoreType.DMA(index.shape)],
+        compiler_params=params(),
+        name="gather_back",
+    )(index, source)
+
+
+def mirrored_rows_kernel(flip_ref, place_ref, near_ref, far_ref, in_ref, out_ref):
+    core = place_ref[0]
+    near = near_ref[:, 0].astype(f32)
+    far = far_ref[:, 0].astype(f32)
+    first = jnp.where(core == 0, near, far)
+    second = jnp.where(core == 0, far, near)
+    lanes = first.shape[2]
+    lane = lax.broadcasted_iota(jnp.int32, first.shape, 2)
+    quarter = lanes // 2
+    low = jnp.where(lane < quarter, first, pltpu.roll(second, quarter, 2))
+    high = jnp.where(lane < quarter, pltpu.roll(first, quarter, 2), second)
+    out_ref[:, 0, :, :lanes] = jnp.swapaxes(low, 0, 1)
+    out_ref[:, 0, :, lanes:] = jnp.swapaxes(high, 0, 1)
+
+
+def mirrored_rows(place, flip, near, far, out):
+    rows, _, lags, cols = out.shape
+    tasks = near.shape[1]
     step = 16
-    specs = [pl.BlockSpec((array.shape[0], step, array.shape[2]), lambda s: (0, s, 0)) for array in flat]
-    return pl.pallas_call(
-        functools.partial(final_kernel, len(pairs)),
-        grid=(rows // step,),
-        out_shape=jax.ShapeDtypeStruct((rows, 2 * len(pairs), lags, cols), f32),
-        in_specs=[smem, smem] + specs,
-        out_specs=pl.BlockSpec((step, 2 * len(pairs), lags, cols), lambda s: (s, 0, 0, 0)),
-        compiler_params=params(),
-        name="final",
-    )(place, flip, *flat)
+    back = pl.BlockSpec((lags, 1, step, near.shape[3]), lambda t, s, flip, place: (0, t, s, 0))
+    return pl.pallas_call(
+        mirrored_rows_kernel,
+        out_shape=jax.ShapeDtypeStruct(out.shape, f32),
+        grid_spec=pltpu.PrefetchScalarGridSpec(
+            num_scalar_prefetch=2,
+            grid=(tasks, rows // step),
+            in_specs=[back, back, pl.BlockSpec(memory_space=pl.ANY)],
+            out_specs=pl.BlockSpec(
+                (step, 1, lags, cols),
+                lambda t, s, flip, place: (s, 2 * t + 1 - flip[t, place[2]], 0, 0),
+            ),
+        ),
+        input_output_aliases={4: 0},
+        compiler_params=params(),
+        name="mirrored_rows",
+    )(flip, place, near, far, out)
 
 
 def exchange(array):
     return lax.all_to_all(array, "pair", split_axis=0, concat_axis=0, tiled=True)
+
+
+def after(array, *others):
+    return lax.optimization_barrier((array,) + others)[0]
 
 
 def local(spectra, channel_order, partners):
@@ -418,24 +493,29 @@
     mate_of, back_of, flip = plan(partners)
     shares = exchange(own)
     arranged = list(gather(shares, mate_of))
-    arranged[0], own_turned = lax.optimization_barrier((arranged[0], own_turned))
-    mates = [exchange(arranged[task]) for task in range(tasks)]
-    pairs = []
+    first = after(arranged[0], own_turned)
+    mates = [exchange(first)] + [exchange(block) for block in arranged[1:]]
+    parts, back, moved = [], [], []
     for task in range(tasks):
         keep, send = correlate(own_turned, mates[task], place, norm, LAGS + 1)
-        own_sum, other_sum, chip_send = core_sum(
-            place, keep, lax.ppermute(send, "win", other_core)
-        )
+        recv = lax.ppermute(after(send, *moved), "win", other_core)
+        near, far, turn_send, rest_send = core_sum(place, keep, recv)
+        turn_recv = lax.ppermute(turn_send, "win", other_chip)
         if task + 1 < tasks:
-            mates[task + 1], chip_send = lax.optimization_barrier((mates[task + 1], chip_send))
-        mine, back_keep, back_send = chip_sum(
-            place, own_sum, other_sum, lax.ppermute(chip_send, "win", other_chip)
-        )
-        back_recv = lax.ppermute(back_send, "win", other_core)
-        spread = exchange(jnp.concatenate([back_keep, back_recv], 0))
-        (returned,) = gather(spread, back_of[task : task + 1])
-        pairs.append((mine, exchange(returned)))
-    return final(place, flip, pairs)[None]
+            mates[task + 1] = after(mates[task + 1], turn_send)
+            rest_recv = lax.ppermute(rest_send, "win", other_chip)
+            moved = [turn_recv, rest_recv]
+            back = [mirror(place, near, turn_recv, back)]
+            out = own_rows(place, flip, task, near, far, turn_recv, rest_recv, None)
+        else:
+            turn_recv, out = lax.optimization_barrier((turn_recv, out))
+            back = [mirror(place, near, turn_recv, back)]
+            rest_recv = lax.ppermute(after(rest_send, turn_recv), "win", other_chip)
+    spread = after(exchange(back[0]), rest_recv)
+    out = own_rows(place, flip, tasks - 1, near, far, turn_recv, rest_recv, out)
+    returned = after(exchange(gather_back(spread, back_of)), out)
+    far = lax.ppermute(returned[LAGS:], "win", other_core)
+    return mirrored_rows(place, flip, returned, far, out)[None]
 
 
 def solution(mesh):

time: 288 us -> 273 us (0.948)
  blocking collectives: 62.9 us -> 46.2 us
  Pallas kernels: 70.9 us -> 78.9 us
  starting transfers between devices: 47.7 us -> 43.8 us
  other arithmetic: 4.23 us -> 0.6 us
    all_to_all x2 -> x1, blocking collectives: 62.9 us -> 46.2 us  [exchange(): lax.all_to_all(array, 'pair', split_axis=0, concat_axis=0, tiled=True)]
    pallas_call x3 -> x6, Pallas kernels: 11.1 us -> 23.2 us  [the longest x2 8.82 us: own_rows(): pl.pallas_call(own_rows_kernel, out_shape=jax.ShapeDtypeStruct((rows, ROU...]
    ppermute x6 -> x7, waiting for transfers between devices: 19.3 us -> 30.9 us  [the longest x1 17.5 us: local(): rest_recv = lax.ppermute(after(rest_send, turn_recv), 'win', other_chip)]
    all_to_all x5 -> x4, waiting for transfers between devices: 69.7 us -> 59.8 us  [exchange(): lax.all_to_all(array, 'pair', split_axis=0, concat_axis=0, tiled=True)]
    pallas_call x3 -> x1, Pallas kernels: 9.35 us -> 5.11 us  [gather(): pl.pallas_call(gather_kernel, out_shape=[jax.ShapeDtypeStruct((places,) +...]
    all_to_all x5 -> x4, starting transfers between devices: 42.5 us -> 38.3 us  [exchange(): lax.all_to_all(array, 'pair', split_axis=0, concat_axis=0, tiled=True)]
    concatenate x2 -> x0, other arithmetic: 3.58 us -> none  [local(): spread = exchange(jnp.concatenate([back_keep, back_recv], 0))]
  transfers between devices with their start and end apart: 11 -> 11, of which waited for: 11 -> 8; matrix products, arithmetic and copies ran while one was open for 2% -> 0% of each run, Pallas kernels for 15% -> 19%
where the time goes in v4:
time: 273 us; the launch traced here: 268 us
  waiting for transfers between devices  90.7 us (33%)
  Pallas kernels  78.9 us (29%)
  blocking collectives  46.2 us (17%)
  starting transfers between devices  43.8 us (16%)
  local copies, waits for them, and re-layouts  7.98 us (3%)
    all_to_all x4, waiting for transfers between devices, exchange(): lax.all_to_all(array, 'pair', split_axis=0, concat_axis=0, tiled=True)  59.8 us
    all_to_all x1, blocking collectives, exchange(): lax.all_to_all(array, 'pair', split_axis=0, concat_axis=0, tiled=True)  46.2 us
    all_to_all x4, starting transfers between devices, exchange(): lax.all_to_all(array, 'pair', split_axis=0, concat_axis=0, tiled=True)  38.3 us
    pallas_call x2, Pallas kernels, correlate(): pl.pallas_call(functools.partial(correlate_kernel, norm), grid=(num_bins...  25.2 us
    ppermute x1, waiting for transfers between devices, local(): rest_recv = lax.ppermute(after(rest_send, turn_recv), 'win', other_chip)  17.5 us
    pallas_call x2, Pallas kernels, own_rows(): pl.pallas_call(own_rows_kernel, out_shape=jax.ShapeDtypeStruct((rows, ROU...  8.82 us
    pallas_call x1, Pallas kernels, turn(): pl.pallas_call(turn_kernel, grid=(num_bins // bins,), out_shape=jax.Shape...  8.3 us
    unnamed x22, local copies, waits for them, and re-layouts  7.94 us
  transfers between devices with their start and end apart: 11, of which 8 were waited for; matrix products, arithmetic and copies ran while one was open for 0% of the time, Pallas kernels for 19%

profile of v4, /device:TPU:16, one launch (start us, length us, event | category | flops | bytes accessed | tf_op | source)
XLA Modules:
  0.0 268.3 jit_solution(762447686338622738)
XLA Ops:
  0.0 6.2 %whiten.1 = bf16[32,2,96,256]{3,2,1,0:T(8,128)(2,1)} custom-call(s32[1,256]{1,0:T(1,128)} %order_ref.1, bf16[32,2,96,256]{3,2,1,0:T(8,128)(2,1)} %spectra_ref.1), custom_call_target="tpu_custom_call" | custom-call | tf_op jit(solution)/shard_map/whiten/pallas_call | solution.py:45
  6.2 10.9 %all-to-all-start = ((bf16[32,192,256]{2,1,0:T(8,128)(2,1)}), bf16[32,192,256]{2,1,0:T(8,128)(2,1)S(1)}, u32[]{:S(2)}, u32[]{:S(2)}) async-start(bf16[32,192,256]{2,1,0:T(8,128)(2,1)} %bitcast.5), calls=%async_computation | async-start | bytes 6291456 | tf_op jit(solution)/shard_map/all_to_all | solution.py:474
  17.1 8.3 %turn.1.own_ref = bf16[32,512,192]{2,1,0:T(8,128)(2,1)} custom-call(bf16[32,192,256]{2,1,0:T(8,128)(2,1)} %bitcast.6), custom_call_target="tpu_custom_call" | custom-call | bytes 12000000 | tf_op jit(solution)/shard_map/turn/pallas_call | solution.py:76
  25.4 3.3 %plan.1 = (s32[2,32]{1,0:T(2,128)}, s32[2,32]{1,0:T(2,128)}, s32[2,32]{1,0:T(2,128)}) custom-call(s32[4,32]{1,0:T(4,128)} %partners_ref.1), custom_call_target="tpu_custom_call" | custom-call | tf_op jit(solution)/shard_map/plan/pallas_call | solution.py:276
  28.8 30.6 %all-to-all-done.source_ref = bf16[32,192,256]{2,1,0:T(8,128)(2,1)S(1)} async-done(((bf16[32,192,256]{2,1,0:T(8,128)(2,1)}), bf16[32,192,256]{2,1,0:T(8,128)(2,1)S(1)}, u32[]{:S(2)}, u32[]{:S(2)}) %all-to-all-start) | async-done | bytes 3145760 | tf_op jit(solution)/shard_map/all_to_all | solution.py:474
  59.4 1.7 copy-done
  61.0 5.1 %gather.1 = (bf16[32,192,256]{2,1,0:T(8,128)(2,1)}, bf16[32,192,256]{2,1,0:T(8,128)(2,1)}) custom-call(s32[2,32]{1,0:T(2,128)} %get-tuple-element.32.index_ref, bf16[32,192,256]{2,1,0:T(8,128)(2,1)} %copy-done), custom_call_target="tpu_custom_call" | custom-call | tf_op jit(solution)/shard_map/gather/pallas_call | solution.py:104
  66.2 46.2 %all_to_all.25.mate_ref = bf16[32,192,256]{2,1,0:T(8,128)(2,1)} all-to-all(bf16[32,192,256]{2,1,0:T(8,128)(2,1)} %get-tuple-element.35), channel_id=1, replica_groups=mesh['pair'=32,'win'=4] {'pair'}, dimensions={0} | all-to-all | bytes 6291456 | tf_op jit(solution)/shard_map/all_to_all | solution.py:474
  112.3 6.9 %all-to-all-start.1 = ((bf16[32,192,256]{2,1,0:T(8,128)(2,1)}), bf16[32,192,256]{2,1,0:T(8,128)(2,1)S(1)}, u32[]{:S(2)}, u32[]{:S(2)}) async-start(bf16[32,192,256]{2,1,0:T(8,128)(2,1)} %get-tuple-element.33), calls=%async_computation.1 | async-start | bytes 6291456 | tf_op jit(solution)/shard_map/all_to_all | solution.py:474
  119.3 0.6 pad_add_fusion.core_ref.place_ref
  119.9 12.6 %correlate.2 = (f32[17,128,256]{2,1,0:T(8,128)}, bf16[17,128,256]{2,1,0:T(8,128)(2,1)}) custom-call(s32[3]{0:T(128)} %pad_add_fusion.core_ref.place_ref, bf16[32,512,192]{2,1,0:T(8,128)(2,1)} %turn.1.own_ref, bf16[32,192,256]{2,1,0:T(8,128)(2,1)} %all_to_all.25.mate_ref), custom_call_target="tpu_custom_call" | custom-call | flops 1610612736 | bytes 20000000 | tf_op jit(solution)/shard_map/correlate/pallas_call | solution.py:219
  132.5 0.0 collective-permute-start
  132.5 3.0 %collective-permute-done.recv_ref = bf16[17,128,256]{2,1,0:T(8,128)(2,1)S(1)} collective-permute-done((bf16[17,128,256]{2,1,0:T(8,128)(2,1)}, bf16[17,128,256]{2,1,0:T(8,128)(2,1)S(1)}, u32[]{:S(2)}, u32[]{:S(2)}) %collective-permute-start) | collective-permute-done | bytes 1114144 | tf_op jit(solution)/shard_map/ppermute | solution.py:501
  135.5 1.0 copy-done.5
  136.5 3.7 %core_sum.2 = (f32[17,128,128]{2,1,0:T(8,128)}, f32[16,64,128]{2,1,0:T(8,128)}, bf16[16,128,128]{2,1,0:T(8,128)(2,1)}, bf16[17,64,128]{2,1,0:T(8,128)(2,1)}) custom-call(s32[3]{0:T(128)} %pad_add_fusion.core_ref.place_ref, f32[17,128,256]{2,1,0:T(8,128)} %get-tuple-element.36.keep_ref, bf16[17,128,256]{2,1,0:T(8,128)(2,1)} %copy-done.5), custom_call_target="tpu_custom_call" | custom-call | bytes 10000000 | tf_op jit(solution)/shard_map/core_sum/pallas_call | solution.py:312
  140.2 2.2 collective-permute-start.1
  142.4 0.0 collective-permute-start.2
  142.5 17.8 %all-to-all-done.1.mate_ref = bf16[32,192,256]{2,1,0:T(8,128)(2,1)S(1)} async-done(((bf16[32,192,256]{2,1,0:T(8,128)(2,1)}), bf16[32,192,256]{2,1,0:T(8,128)(2,1)S(1)}, u32[]{:S(2)}, u32[]{:S(2)}) %all-to-all-start.1) | async-done | bytes 3145760 | tf_op jit(solution)/shard_map/all_to_all | solution.py:474
  160.3 1.7 copy-done.1
  161.9 12.6 %correlate.3 = (f32[17,128,256]{2,1,0:T(8,128)}, bf16[17,128,256]{2,1,0:T(8,128)(2,1)}) custom-call(s32[3]{0:T(128)} %pad_add_fusion.core_ref.place_ref, bf16[32,512,192]{2,1,0:T(8,128)(2,1)} %turn.1.own_ref, bf16[32,192,256]{2,1,0:T(8,128)(2,1)} %copy-done.1), custom_call_target="tpu_custom_call" | custom-call | flops 1610612736 | bytes 20000000 | tf_op jit(solution)/shard_map/correlate/pallas_call | solution.py:219
  174.5 0.0 collective-permute-done.2.rest_ref
  174.5 0.0 collective-permute-done.1.turn_ref.recv_ref
  174.6 0.1 collective-permute-start.3
  174.6 3.0 %collective-permute-done.3.recv_ref = bf16[17,128,256]{2,1,0:T(8,128)(2,1)S(1)} collective-permute-done((bf16[17,128,256]{2,1,0:T(8,128)(2,1)}, bf16[17,128,256]{2,1,0:T(8,128)(2,1)S(1)}, u32[]{:S(2)}, u32[]{:S(2)}) %collective-permute-start.3) | collective-permute-done | bytes 1114144 | tf_op jit(solution)/shard_map/ppermute | solution.py:501
  177.6 1.0 copy-done.6
  178.6 3.7 %core_sum.3 = (f32[17,128,128]{2,1,0:T(8,128)}, f32[16,64,128]{2,1,0:T(8,128)}, bf16[16,128,128]{2,1,0:T(8,128)(2,1)}, bf16[17,64,128]{2,1,0:T(8,128)(2,1)}) custom-call(s32[3]{0:T(128)} %pad_add_fusion.core_ref.place_ref, f32[17,128,256]{2,1,0:T(8,128)} %get-tuple-element.40.keep_ref, bf16[17,128,256]{2,1,0:T(8,128)(2,1)} %copy-done.6), custom_call_target="tpu_custom_call" | custom-call | bytes 10000000 | tf_op jit(solution)/shard_map/core_sum/pallas_call | solution.py:312
  182.3 2.6 collective-permute-start.4
  184.9 2.4 mirror.2.refs_0_
  187.3 0.0 copy-done.8
  187.3 4.4 %own_rows.2.refs_0_ = f32[64,4,16,256]{3,2,1,0:T(8,128)} custom-call(s32[2,32]{1,0:T(2,128)} %get-tuple-element.30.flip_ref, s32[3]{0:T(128)} %pad_add_fusion.core_ref.place_ref, f32[17,128,128]{2,1,0:T(8,128)} %get-tuple-element.46.near_ref, f32[16,64,128]{2,1,0:T(8,128)} %get-tuple-element.47.far_ref, ...), custom_call_target="tpu_custom_call" | custom-call | bytes 5000000 | tf_op jit(solution)/shard_map/own_rows/pallas_call | solution.py:384
  191.7 5.6 %collective-permute-done.4.recv_ref.turn_ref = bf16[16,128,128]{2,1,0:T(8,128)(2,1)S(1)} collective-permute-done((bf16[16,128,128]{2,1,0:T(8,128)(2,1)}, bf16[16,128,128]{2,1,0:T(8,128)(2,1)S(1)}, u32[]{:S(2)}, u32[]{:S(2)}) %collective-permute-start.4) | collective-permute-done | bytes 524320 | tf_op jit(solution)/shard_map/ppermute | solution.py:503
  197.4 0.8 copy-done.4
  198.2 2.7 %mirror.3 = bf16[32,2,64,128]{3,2,1,0:T(8,128)(2,1)} custom-call(s32[3]{0:T(128)} %pad_add_fusion.core_ref.place_ref, f32[17,128,128]{2,1,0:T(8,128)} %get-tuple-element.44.near_ref, bf16[16,128,128]{2,1,0:T(8,128)(2,1)} %copy-done.4, bf16[32,1,64,128]{3,2,1,0:T(8,128)(2,1)} %mirror.2.refs_0_), custom_call_target="tpu_custom_call" | custom-call | bytes 8000000 | tf_op jit(solution)/shard_map/mirror/pallas_call | solution.py:346
  200.9 11.0 %all-to-all-start.3 = ((bf16[32,2,64,128]{3,2,1,0:T(8,128)(2,1)}), bf16[32,2,64,128]{3,2,1,0:T(8,128)(2,1)S(1)}, u32[]{:S(2)}, u32[]{:S(2)}) async-start(bf16[32,2,64,128]{3,2,1,0:T(8,128)(2,1)} %mirror.3), calls=%async_computation.3 | async-start | bytes 2097152 | tf_op jit(solution)/shard_map/all_to_all | solution.py:474
  211.9 0.0 copy-done.10
  211.9 0.4 collective-permute-start.5
  212.3 17.5 %collective-permute-done.5.rest_ref = bf16[17,64,128]{2,1,0:T(8,128)(2,1)S(1)} collective-permute-done((bf16[17,64,128]{2,1,0:T(8,128)(2,1)S(1)}, bf16[17,64,128]{2,1,0:T(8,128)(2,1)S(1)}, u32[]{:S(2)}, u32[]{:S(2)}) %collective-permute-start.5) | collective-permute-done | bytes 278560 | tf_op jit(solution)/shard_map/ppermute | solution.py:513
  229.8 0.0 all-to-all-done.3.source_ref
  229.8 1.0 copy-done.3
  230.8 2.8 %gather_back.1 = bf16[32,2,64,128]{3,2,1,0:T(8,128)(2,1)} custom-call(s32[2,32]{1,0:T(2,128)} %get-tuple-element.31.index_ref, bf16[32,2,64,128]{3,2,1,0:T(8,128)(2,1)} %copy-done.3), custom_call_target="tpu_custom_call" | custom-call | tf_op jit(solution)/shard_map/gather_back/pallas_call | solution.py:421
  233.6 9.6 %all-to-all-start.4 = ((bf16[32,2,64,128]{3,2,1,0:T(8,128)(2,1)}), bf16[32,2,64,128]{3,2,1,0:T(8,128)(2,1)S(1)}, u32[]{:S(2)}, u32[]{:S(2)}) async-start(bf16[32,2,64,128]{3,2,1,0:T(8,128)(2,1)} %gather_back.1), calls=%async_computation.4 | async-start | bytes 2097152 | tf_op jit(solution)/shard_map/all_to_all | solution.py:474
  243.2 4.4 %own_rows.3.in_ref = f32[64,4,16,256]{3,2,1,0:T(8,128)} custom-call(s32[2,32]{1,0:T(2,128)} %get-tuple-element.30.flip_ref, s32[3]{0:T(128)} %pad_add_fusion.core_ref.place_ref, f32[17,128,128]{2,1,0:T(8,128)} %get-tuple-element.44.near_ref, f32[16,64,128]{2,1,0:T(8,128)} %get-tuple-element.52.far_ref, ...), custom_call_target="tpu_custom_call", output_to_operand_aliasing={{}: (6, {})} | custom-call | bytes 5000000 | tf_op jit(solution)/shard_map/own_rows/pallas_call | solution.py:384
  247.6 11.4 %all-to-all-done.4.near_ref = bf16[32,2,64,128]{3,2,1,0:T(8,128)(2,1)S(1)} async-done(((bf16[32,2,64,128]{3,2,1,0:T(8,128)(2,1)}), bf16[32,2,64,128]{3,2,1,0:T(8,128)(2,1)S(1)}, u32[]{:S(2)}, u32[]{:S(2)}) %all-to-all-start.4) | async-done | bytes 1048608 | tf_op jit(solution)/shard_map/all_to_all | solution.py:474
  259.0 0.1 collective-permute-start.6
  259.1 1.9 collective-permute-done.6.far_ref
  261.0 0.0 copy-done.2
  261.0 0.8 copy-done.7
  261.8 6.5 %mirrored_rows.1 = f32[64,4,16,256]{3,2,1,0:T(8,128)} custom-call(s32[2,32]{1,0:T(2,128)} %get-tuple-element.30.flip_ref, s32[3]{0:T(128)} %pad_add_fusion.core_ref.place_ref, bf16[32,2,64,128]{3,2,1,0:T(8,128)(2,1)} %copy-done.2, bf16[16,2,64,128]{3,2,1,0:T(8,128)(2,1)} %copy-done.7, f32[64,4,16,256]{3,2,1,0:T(8,128)} %own_rows.3.in_ref), custom_call_target="tpu_custom_call", output_to_operand_aliasing={{}: (4, {})} | custom-call | tf_op jit(solution)/shard_map/mirrored_rows/pallas_call | solution.py:455
  (13 shorter events, 0.1 us)
Async XLA Ops:
  6.2 53.1 %all-to-all-start = ((bf16[32,192,256]{2,1,0:T(8,128)(2,1)}), bf16[32,192,256]{2,1,0:T(8,128)(2,1)S(1)}, u32[]{:S(2)}, u32[]{:S(2)}) async-start(bf16[32,192,256]{2,1,0:T(8,128)(2,1)} %bitcast.5), calls=%async_computation | async-start | bytes 6291456 | tf_op jit(solution)/shard_map/all_to_all | solution.py:474
  59.4 1.7 copy-start
  112.3 47.9 %all-to-all-start.1 = ((bf16[32,192,256]{2,1,0:T(8,128)(2,1)}), bf16[32,192,256]{2,1,0:T(8,128)(2,1)S(1)}, u32[]{:S(2)}, u32[]{:S(2)}) async-start(bf16[32,192,256]{2,1,0:T(8,128)(2,1)} %get-tuple-element.33), calls=%async_computation.1 | async-start | bytes 6291456 | tf_op jit(solution)/shard_map/all_to_all | solution.py:474
  132.5 3.0 %collective-permute-start = (bf16[17,128,256]{2,1,0:T(8,128)(2,1)}, bf16[17,128,256]{2,1,0:T(8,128)(2,1)S(1)}, u32[]{:S(2)}, u32[]{:S(2)}) collective-permute-start(bf16[17,128,256]{2,1,0:T(8,128)(2,1)} %get-tuple-element.37), channel_id=1, source_target_pairs={{0,1},{1,0},{2,3},{3,2},{4,5},{5,4},{6,7},{7,6},{8,9},{9,8},{10,11... | collective-permute-start | bytes 3342344 | tf_op jit(solution)/shard_map/ppermute | solution.py:501
  135.5 1.0 copy-start.5
  140.2 34.3 %collective-permute-start.1 = (bf16[16,128,128]{2,1,0:T(8,128)(2,1)}, bf16[16,128,128]{2,1,0:T(8,128)(2,1)}, u32[]{:S(2)}, u32[]{:S(2)}) collective-permute-start(bf16[16,128,128]{2,1,0:T(8,128)(2,1)} %get-tuple-element.38), channel_id=1, source_target_pairs={{0,2},{1,3},{2,0},{3,1},{4,6},{5,7},{6,4},{7,5},{8,10},{9,11},{10,... | collective-permute-start | bytes 1572872 | tf_op jit(solution)/shard_map/ppermute | solution.py:503
  142.4 32.1 %collective-permute-start.2 = (bf16[17,64,128]{2,1,0:T(8,128)(2,1)}, bf16[17,64,128]{2,1,0:T(8,128)(2,1)S(1)}, u32[]{:S(2)}, u32[]{:S(2)}) collective-permute-start(bf16[17,64,128]{2,1,0:T(8,128)(2,1)} %get-tuple-element.42), channel_id=1, source_target_pairs={{0,2},{1,3},{2,0},{3,1},{4,6},{5,7},{6,4},{7,5},{8,10},{9,11},{10,... | collective-permute-start | bytes 835592 | tf_op jit(solution)/shard_map/ppermute | solution.py:506
  160.3 1.7 copy-start.1
  174.5 12.8 %copy-start.8 = (bf16[17,64,128]{2,1,0:T(8,128)(2,1)}, bf16[17,64,128]{2,1,0:T(8,128)(2,1)S(1)}, u32[]{:S(2)}) copy-start(bf16[17,64,128]{2,1,0:T(8,128)(2,1)S(1)} %collective-permute-done.2.rest_ref) | copy-start | bytes 835588
  174.6 3.0 %collective-permute-start.3 = (bf16[17,128,256]{2,1,0:T(8,128)(2,1)}, bf16[17,128,256]{2,1,0:T(8,128)(2,1)S(1)}, u32[]{:S(2)}, u32[]{:S(2)}) collective-permute-start(bf16[17,128,256]{2,1,0:T(8,128)(2,1)} %get-tuple-element.43), channel_id=1, source_target_pairs={{0,1},{1,0},{2,3},{3,2},{4,5},{5,4},{6,7},{7,6},{8,9},{9,8},{10,11... | collective-permute-start | bytes 3342344 | tf_op jit(solution)/shard_map/ppermute | solution.py:501
  177.6 1.0 copy-start.6
  182.3 15.0 %collective-permute-start.4 = (bf16[16,128,128]{2,1,0:T(8,128)(2,1)}, bf16[16,128,128]{2,1,0:T(8,128)(2,1)S(1)}, u32[]{:S(2)}, u32[]{:S(2)}) collective-permute-start(bf16[16,128,128]{2,1,0:T(8,128)(2,1)} %get-tuple-element.45), channel_id=1, source_target_pairs={{0,2},{1,3},{2,0},{3,1},{4,6},{5,7},{6,4},{7,5},{8,10},{9,11},{10,... | collective-permute-start | bytes 1572872 | tf_op jit(solution)/shard_map/ppermute | solution.py:503
  191.7 20.1 %copy-start.10 = (bf16[17,64,128]{2,1,0:T(8,128)(2,1)S(1)}, bf16[17,64,128]{2,1,0:T(8,128)(2,1)}, u32[]{:S(2)}) copy-start(bf16[17,64,128]{2,1,0:T(8,128)(2,1)} %get-tuple-element.50) | copy-start | bytes 835588
  197.4 0.8 copy-start.4
  200.9 28.9 %all-to-all-start.3 = ((bf16[32,2,64,128]{3,2,1,0:T(8,128)(2,1)}), bf16[32,2,64,128]{3,2,1,0:T(8,128)(2,1)S(1)}, u32[]{:S(2)}, u32[]{:S(2)}) async-start(bf16[32,2,64,128]{3,2,1,0:T(8,128)(2,1)} %mirror.3), calls=%async_computation.3 | async-start | bytes 2097152 | tf_op jit(solution)/shard_map/all_to_all | solution.py:474
  211.9 17.9 %collective-permute-start.5 = (bf16[17,64,128]{2,1,0:T(8,128)(2,1)S(1)}, bf16[17,64,128]{2,1,0:T(8,128)(2,1)S(1)}, u32[]{:S(2)}, u32[]{:S(2)}) collective-permute-start(bf16[17,64,128]{2,1,0:T(8,128)(2,1)S(1)} %copy-done.10), channel_id=1, source_target_pairs={{0,2},{1,3},{2,0},{3,1},{4,6},{5,7},{6,4},{7,5},{8,10},{9,11},{10,... | collective-permute-start | bytes 835592 | tf_op jit(solution)/shard_map/ppermute | solution.py:513
  229.8 13.4 %copy-start.9 = (bf16[17,64,128]{2,1,0:T(8,128)(2,1)}, bf16[17,64,128]{2,1,0:T(8,128)(2,1)S(1)}, u32[]{:S(2)}) copy-start(bf16[17,64,128]{2,1,0:T(8,128)(2,1)S(1)} %collective-permute-done.5.rest_ref) | copy-start | bytes 835588
  229.8 1.0 copy-start.3
  233.6 25.4 %all-to-all-start.4 = ((bf16[32,2,64,128]{3,2,1,0:T(8,128)(2,1)}), bf16[32,2,64,128]{3,2,1,0:T(8,128)(2,1)S(1)}, u32[]{:S(2)}, u32[]{:S(2)}) async-start(bf16[32,2,64,128]{3,2,1,0:T(8,128)(2,1)} %gather_back.1), calls=%async_computation.4 | async-start | bytes 2097152 | tf_op jit(solution)/shard_map/all_to_all | solution.py:474
  259.0 2.0 copy-start.2
  259.0 2.0 collective-permute-start.6
  261.0 0.8 copy-start.7

commit v5 on v4

v5 whole, which is shorter than its diff:
```python
import functools
import math

import jax
import jax.numpy as jnp
from jax import lax
from jax.experimental import pallas as pl
from jax.experimental.pallas import tpu as pltpu
from jax.sharding import PartitionSpec as P

LAGS = 16
ROUNDS = 4
VMEM_BYTES = 62 * 1024 * 1024
QUARTER_ORDER = (0, 2, 1, 3)
bf16 = jnp.bfloat16
f32 = jnp.float32


def params(**more):
    return pltpu.CompilerParams(vmem_limit_bytes=VMEM_BYTES, **more)


def whiten_kernel(order_ref, spectra_ref, out_ref):
    num_bins, _, rows, cols = spectra_ref.shape
    slots = lax.broadcasted_iota(jnp.int32, (cols, cols), 0)
    pick = (slots == order_ref[...]).astype(f32).astype(bf16)
    values = spectra_ref[...].astype(f32)
    power = values[:, 0] * values[:, 0] + values[:, 1] * values[:, 1]
    parts = []
    for f in range(num_bins):
        lo, hi = max(f - 2, 0), min(f + 2, num_bins - 1)
        total = power[lo]
        for g in range(lo + 1, hi + 1):
            total = total + power[g]
        inv_scale = jnp.minimum(lax.rsqrt(total * (1.0 / (hi - lo + 1))), 2.0)
        parts.append((values[f] * inv_scale[None]).astype(bf16).reshape(2 * rows, cols))
    flat = jnp.concatenate(parts, 0)
    ordered = jnp.dot(flat, pick, preferred_element_type=f32).astype(bf16)
    out_ref[...] = ordered.reshape(num_bins, 2, rows, cols)


def whiten(spectra, channel_order):
    num_bins, _, num_windows, cols = spectra.shape
    rows = 32
    return pl.pallas_call(
        whiten_kernel,
        grid=(num_windows // rows,),
        out_shape=jax.ShapeDtypeStruct(spectra.shape, bf16),
        in_specs=[
            pl.BlockSpec((1, cols), lambda s: (0, 0)),
            pl.BlockSpec((num_bins, 2, rows, cols), lambda s: (0, 0, s, 0)),
        ],
        out_specs=pl.BlockSpec((num_bins, 2, rows, cols), lambda s: (0, 0, s, 0)),
        compiler_params=params(),
        name="whiten",
    )(channel_order, spectra)


def turn_kernel(own_ref, out_ref):
    bins, _, cols = own_ref.shape
    quarter = cols // 4
    for f in range(bins):
        turned = own_ref[f].astype(f32).T.astype(bf16)
        for place, source in enumerate(QUARTER_ORDER):
            out_ref[f, place * quarter : (place + 1) * quarter, :] = turned[
                source * quarter : (source + 1) * quarter
            ]


def turn(own_rows):
    num_bins, depth, cols = own_rows.shape
    bins = 8
    return pl.pallas_call(
        turn_kernel,
        grid=(num_bins // bins,),
        out_shape=jax.ShapeDtypeStruct((num_bins, cols, depth), bf16),
        in_specs=[pl.BlockSpec((bins, depth, cols), lambda s: (s, 0, 0))],
        out_specs=pl.BlockSpec((bins, cols, depth), lambda s: (s, 0, 0)),
        compiler_params=params(),
        cost_estimate=pl.CostEstimate(flops=0, bytes_accessed=12_000_000, transcendentals=0),
        name="turn",
    )(own_rows)


def gather_kernel(index_ref, source_ref, *refs):
    *out_refs, sems = refs
    copies = []
    for group, out_ref in enumerate(out_refs):
        for place in range(out_ref.shape[0]):
            copy = pltpu.make_async_copy(
                source_ref.at[index_ref[group, place]], out_ref.at[place], sems.at[group, place]
            )
            copy.start()
            copies.append(copy)
    for copy in copies:
        copy.wait()


def gather(source, index):
    groups, places = index.shape
    return pl.pallas_call(
        gather_kernel,
        out_shape=[jax.ShapeDtypeStruct((places,) + source.shape[1:], source.dtype)] * groups,
        in_specs=[
            pl.BlockSpec(memory_space=pltpu.SMEM),
            pl.BlockSpec(memory_space=pltpu.VMEM),
        ],
        out_specs=[pl.BlockSpec(memory_space=pl.ANY)] * groups,
        scratch_shapes=[pltpu.SemaphoreType.DMA(index.shape)],
        compiler_params=params(),
        name="gather",
    )(index, source)


def weighted(terms):
    total = None
    for weight, value in terms:
        if abs(weight) < 1e-12:
            continue
        term = value * weight
        total = term if total is None else total + term
    return total


def lag_sums(real, imag, norm):
    cosine = lambda f, t: math.cos(math.pi * f * t / 32) * norm
    sine = lambda f, t: -math.sin(math.pi * f * t / 32) * norm
    even, odd = {}, {}
    low = {0: real(0), 16: real(16)}
    diff = {0: low[0]}
    for f in range(1, 16):
        a, b = real(f), real(32 - f)
        low[f], diff[f] = a + b, a - b
    for t in (1, 3, 5, 7):
        even[t] = weighted([(cosine(f, t), diff[f]) for f in range(16)])
    minus = {f: low[f] - low[16 - f] for f in range(8)}
    for t in (2, 6):
        even[t] = weighted([(cosine(f, t), minus[f]) for f in range(8)])
    plus = {f: low[f] + low[16 - f] for f in range(8)}
    plus[8] = low[8]
    even[4] = weighted([(cosine(f, 4), plus[f] - plus[8 - f]) for f in range(4)])
    sums = {f: plus[f] + plus[8 - f] for f in range(4)}
    sums[4] = plus[4]
    even[8] = weighted([(cosine(f, 8), sums[f]) for f in range(5)])
    total = sums[0]
    for f in range(1, 5):
        total = total + sums[f]
    even[0] = total * norm

    add = {16: imag(16)}
    sub = {}
    for f in range(1, 16):
        a, b = imag(f), imag(32 - f)
        add[f], sub[f] = a + b, a - b
    for t in (1, 3, 5, 7):
        odd[t] = weighted([(sine(f, t), add[f]) for f in range(1, 17)])
    sums = {f: sub[f] + sub[16 - f] for f in range(1, 8)}
    sums[8] = sub[8]
    for t in (2, 6):
        odd[t] = weighted([(sine(f, t), sums[f]) for f in range(1, 9)])
    minus = {f: sub[f] - sub[16 - f] for f in range(1, 8)}
    odd[4] = weighted(
        [(sine(f, 4), minus[f] + minus[8 - f]) for f in range(1, 4)] + [(sine(4, 4), minus[4])]
    )
    odd[8] = weighted([(sine(f, 8), minus[f] - minus[8 - f]) for f in range(1, 4)])
    return even, odd


def correlate_kernel(
    norm, place_ref, own_ref, mate_ref, keep_ref, send_ref, own, mate, cross, own_sems, mate_sems
):
    num_bins, slots, _ = own.shape
    chunks = own_sems.shape[0]
    bins = num_bins // chunks
    copies = []
    for chunk in range(chunks):
        where = pl.ds(chunk * bins, bins)
        pair = (
            pltpu.make_async_copy(own_ref.at[where], own.at[where], own_sems.at[chunk]),
            pltpu.make_async_copy(mate_ref.at[where], mate.at[where], mate_sems.at[chunk]),
        )
        for copy in pair:
            copy.start()
        copies.append(pair)
    for chunk in range(chunks):
        for copy in copies[chunk]:
            copy.wait()
        for f in range(chunk * bins, (chunk + 1) * bins):
            left, right = own[f], mate[f]
            half = right.shape[0] // 2
            turned = jnp.concatenate([right[half:], -right[:half]], 0)
            cross[f, :slots] = jnp.dot(left, right, preferred_element_type=f32)
            cross[f, slots:] = jnp.dot(left, turned, preferred_element_type=f32)

    lags, half, cols = keep_ref.shape
    core = place_ref[0]
    rows, lanes = 16, 128

    def part(out_ref, base):
        def body(chunk, carry):
            row = pl.multiple_of(chunk * rows, rows)
            where = pl.ds(pl.multiple_of(base + row, rows), rows)
            turned = pl.ds(pl.multiple_of(slots + base + row, rows), rows)
            for lane in range(0, cols, lanes):
                even, odd = lag_sums(
                    lambda f: cross[f, where, lane : lane + lanes],
                    lambda f: cross[f, turned, lane : lane + lanes],
                    norm,
                )
                for lag in range(lags):
                    t = lag - LAGS // 2
                    if t == 0:
                        value = even[0]
                    elif t > 0:
                        value = even[t] + odd[t]
                    else:
                        value = even[-t] - odd[-t]
                    out_ref[lag, pl.ds(row, rows), lane : lane + lanes] = value.astype(
                        out_ref.dtype
                    )
            return carry

        lax.fori_loop(0, half // rows, body, 0)

    part(keep_ref, core * half)
    part(send_ref, (1 - core) * half)


def correlate(own, mate, place, norm, lags):
    num_bins, slots, depth = own.shape
    cols = mate.shape[2]
    chunks = 8
    anywhere = pl.BlockSpec(memory_space=pl.ANY)
    vmem = pl.BlockSpec(memory_space=pltpu.VMEM)
    return pl.pallas_call(
        functools.partial(correlate_kernel, norm),
        out_shape=[
            jax.ShapeDtypeStruct((lags, slots // 2, cols), f32),
            jax.ShapeDtypeStruct((lags, slots // 2, cols), bf16),
        ],
        in_specs=[pl.BlockSpec(memory_space=pltpu.SMEM), anywhere, anywhere],
        out_specs=[vmem, vmem],
        scratch_shapes=[
            pltpu.VMEM(own.shape, bf16),
            pltpu.VMEM(mate.shape, bf16),
            pltpu.VMEM((num_bins, 2 * slots, cols), f32),
            pltpu.SemaphoreType.DMA((chunks,)),
            pltpu.SemaphoreType.DMA((chunks,)),
        ],
        compiler_params=params(),
        cost_estimate=pl.CostEstimate(
            flops=4 * num_bins * slots * depth * cols, bytes_accessed=20_000_000, transcendentals=0
        ),
        name="correlate",
    )(place, own, mate)


def plan_kernel(partners_ref, mate_ref, back_ref, flip_ref):
    rounds, blocks = partners_ref.shape
    for task in range(rounds // 2):
        first, second = 2 * task, 2 * task + 1

        def clear(block, carry):
            flip_ref[task, block] = -1
            return carry

        def walk(block):
            partner = partners_ref[first, block]
            flip_ref[task, block] = 0
            flip_ref[task, partner] = 1
            mate_ref[task, block] = partner
            back_ref[task, partner] = block
            following = partners_ref[second, partner]
            mate_ref[task, partner] = following
            back_ref[task, following] = partner
            return following

        def start(block, carry):
            lax.while_loop(lambda block: flip_ref[task, block] < 0, walk, block)
            return carry

        lax.fori_loop(0, blocks, clear, 0)
        lax.fori_loop(0, blocks, start, 0)


def plan(partners):
    rounds, blocks = partners.shape
    smem = pl.BlockSpec(memory_space=pltpu.SMEM)
    table = jax.ShapeDtypeStruct((rounds // 2, blocks), jnp.int32)
    return pl.pallas_call(
        plan_kernel,
        out_shape=[table] * 3,
        in_specs=[smem],
        out_specs=[smem] * 3,
        compiler_params=params(),
        name="plan",
    )(partners)


def core_sum_kernel(place_ref, keep_ref, recv_ref, *refs):
    own_ref, send_ref, piece_ref = refs[-3:]
    core, chip = place_ref[0], place_ref[1]
    lags, rows, cols = own_ref.shape
    own_rows = pl.ds(pl.multiple_of(chip * rows, rows), rows)
    other_rows = pl.ds(pl.multiple_of((1 - chip) * rows, rows), rows)
    for lag in range(lags + 1):
        if lag < lags:
            own_ref[lag] = keep_ref[lag, own_rows, :] + recv_ref[lag, own_rows, :].astype(f32)
            send_ref[lag] = (
                keep_ref[lag, other_rows, :] + recv_ref[lag, other_rows, :].astype(f32)
            ).astype(bf16)
        if lag > 0:
            back = lags - lag
            turned = (keep_ref[lag] + recv_ref[lag].astype(f32)).T
            for half in range(2):
                low = turned[2 * half * rows : (2 * half + 1) * rows]
                high = turned[(2 * half + 1) * rows : (2 * half + 2) * rows]
                base = 2 * half * lags + back
                piece_ref[base, 0] = jnp.where(core == 0, low, high).astype(bf16)
                piece_ref[base + lags, 0] = jnp.where(core == 0, high, low).astype(bf16)


def core_sum(place, keep, recv, task, tasks, pieces):
    lags, rows, cols = keep.shape
    vmem = pl.BlockSpec(memory_space=pltpu.VMEM)
    count = 4 * (lags - 1)
    shape = (count, tasks, cols // 4, rows)
    whole = pl.BlockSpec((lags - 1, rows // 2, cols), lambda s: (0, 0, 0))
    given = pl.BlockSpec((lags, rows, cols), lambda s: (0, 0, 0))
    extra = [] if pieces is None else [pieces]
    return pl.pallas_call(
        core_sum_kernel,
        grid=(1,),
        out_shape=[
            jax.ShapeDtypeStruct((lags - 1, rows // 2, cols), f32),
            jax.ShapeDtypeStruct((lags - 1, rows // 2, cols), bf16),
            jax.ShapeDtypeStruct(shape, bf16),
        ],
        in_specs=[pl.BlockSpec(memory_space=pltpu.SMEM), given, given]
        + [pl.BlockSpec(memory_space=pl.ANY)] * len(extra),
        out_specs=[
            whole,
            whole,
            pl.BlockSpec((count, 1) + shape[2:], lambda s: (0, task, 0, 0)),
        ],
        input_output_aliases={3: 2} if extra else {},
        compiler_params=params(),
        cost_estimate=pl.CostEstimate(flops=0, bytes_accessed=12_000_000, transcendentals=0),
        name="core_sum",
    )(place, keep, recv, *extra)


def gather_sum_kernel(index_ref, spread_ref, out_ref):
    places, tasks = out_ref.shape[:2]

    def body(place, carry):
        for task in range(tasks):
            source = index_ref[task, place]
            out_ref[place, task] = (
                spread_ref[source, task].astype(f32)
                + spread_ref[places + source, task].astype(f32)
            ).astype(bf16)
        return carry

    lax.fori_loop(0, places, body, 0, unroll=4)


def gather_sum(index, spread):
    places = index.shape[1]
    vmem = pl.BlockSpec(memory_space=pltpu.VMEM)
    return pl.pallas_call(
        gather_sum_kernel,
        out_shape=jax.ShapeDtypeStruct((places,) + spread.shape[1:], bf16),
        in_specs=[pl.BlockSpec(memory_space=pltpu.SMEM), vmem],
        out_specs=vmem,
        compiler_params=params(),
        name="gather_sum",
    )(index, spread)


def own_rows_kernel(flip_ref, place_ref, own_ref, recv_ref, *refs):
    out_ref = refs[-1]
    out_ref[:, 0] = jnp.swapaxes(own_ref[...] + recv_ref[...].astype(f32), 0, 1)


def own_rows(place, flip, task, own, recv, out):
    lags, rows, cols = own.shape
    step = 16
    extra = [] if out is None else [out]
    piece = pl.BlockSpec((lags, step, cols), lambda s, flip, place: (0, s, 0))
    return pl.pallas_call(
        own_rows_kernel,
        out_shape=jax.ShapeDtypeStruct((rows, ROUNDS, lags, cols), f32),
        grid_spec=pltpu.PrefetchScalarGridSpec(
            num_scalar_prefetch=2,
            grid=(rows // step,),
            in_specs=[piece, piece] + [pl.BlockSpec(memory_space=pl.ANY)] * len(extra),
            out_specs=pl.BlockSpec(
                (step, 1, lags, cols),
                lambda s, flip, place: (s, 2 * task + flip[task, place[2]], 0, 0),
            ),
        ),
        input_output_aliases={4: 0} if extra else {},
        compiler_params=params(),
        cost_estimate=pl.CostEstimate(flops=0, bytes_accessed=5_000_000, transcendentals=0),
        name="own_rows",
    )(flip, place, own, recv, *extra)


def mirrored_rows_kernel(flip_ref, place_ref, near_ref, far_ref, in_ref, out_ref):
    core = place_ref[0]
    near = near_ref[:, 0].astype(f32)
    far = far_ref[:, 0].astype(f32)
    first = jnp.where(core == 0, near, far)
    second = jnp.where(core == 0, far, near)
    lanes = first.shape[2]
    lane = lax.broadcasted_iota(jnp.int32, first.shape, 2)
    quarter = lanes // 2
    low = jnp.where(lane < quarter, first, pltpu.roll(second, quarter, 2))
    high = jnp.where(lane < quarter, pltpu.roll(first, quarter, 2), second)
    out_ref[:, 0, :, :lanes] = jnp.swapaxes(low, 0, 1)
    out_ref[:, 0, :, lanes:] = jnp.swapaxes(high, 0, 1)


def mirrored_rows(place, flip, near, far, out):
    rows, _, lags, cols = out.shape
    tasks = near.shape[1]
    step = 32
    back = pl.BlockSpec((lags, 1, step, near.shape[3]), lambda t, s, flip, place: (0, t, s, 0))
    return pl.pallas_call(
        mirrored_rows_kernel,
        out_shape=jax.ShapeDtypeStruct(out.shape, f32),
        grid_spec=pltpu.PrefetchScalarGridSpec(
            num_scalar_prefetch=2,
            grid=(tasks, rows // step),
            in_specs=[back, back, pl.BlockSpec(memory_space=pl.ANY)],
            out_specs=pl.BlockSpec(
                (step, 1, lags, cols),
                lambda t, s, flip, place: (s, 2 * t + 1 - flip[t, place[2]], 0, 0),
            ),
        ),
        input_output_aliases={4: 0},
        compiler_params=params(),
        name="mirrored_rows",
    )(flip, place, near, far, out)


def exchange(array):
    return lax.all_to_all(array, "pair", split_axis=0, concat_axis=0, tiled=True)


def after(array, *others):
    return lax.optimization_barrier((array,) + others)[0]


def local(spectra, channel_order, partners):
    num_bins, _, num_windows, cols = spectra.shape
    win_count = lax.axis_size("win")
    win = lax.axis_index("win")
    place = jnp.stack([win % 2, win // 2, lax.axis_index("pair")]).astype(jnp.int32)
    other_core = [(i, i ^ 1) for i in range(win_count)]
    other_chip = [(i, i ^ 2) for i in range(win_count)]
    norm = 1.0 / math.sqrt(num_windows * win_count * num_bins)
    tasks = ROUNDS // 2
    num_blocks = lax.axis_size("pair")

    own = whiten(spectra, channel_order).reshape(num_bins, 2 * num_windows, cols)
    own_turned = turn(own)
    mate_of, back_of, flip = plan(partners)
    shares = exchange(own)
    arranged = gather(shares, mate_of)
    mates = [exchange(after(arranged[0], own_turned)), exchange(arranged[1])]
    groups = [
        [(block * 2 + chip_index) * 2 + core_index for chip_index in range(2) for block in range(num_blocks)]
        for core_index in range(2)
    ]
    rows, moved, pieces = [], [], None
    for task in range(tasks):
        keep, send = correlate(own_turned, mates[task], place, norm, LAGS + 1)
        recv = lax.ppermute(after(send, *moved), "win", other_core)
        own_sum, row_send, pieces = core_sum(place, keep, recv, task, tasks, pieces)
        if task + 1 < tasks:
            mates[task + 1] = after(mates[task + 1], row_send)
        if task + 1 < tasks:
            rows.append((own_sum, lax.ppermute(row_send, "win", other_chip)))
            moved = [rows[task][1]]
    out = own_rows(place, flip, 0, *rows[0], None)
    spread = lax.all_to_all(
        after(pieces, out), ("pair", "win"), 0, 0, tiled=True, axis_index_groups=groups
    )
    row_recv = lax.ppermute(row_send, "win", other_chip)
    returned = exchange(after(gather_sum(back_of, spread), row_recv))
    out = own_rows(place, flip, 1, own_sum, row_recv, out)
    returned = after(returned, out)
    far = lax.ppermute(returned[LAGS:], "win", other_core)
    return mirrored_rows(place, flip, returned, far, out)[None]


def solution(mesh):
    return jax.shard_map(
        local,
        mesh=mesh,
        in_specs=(P(None, None, "win", "pair"), P("pair", None), P()),
        out_specs=P("pair", "win", None, None, None),
        check_vma=False,
    )
```

time: 273 us -> 265 us (0.971)
  Pallas kernels: 78.9 us -> 66.5 us
  waiting for transfers between devices: 90.7 us -> 99.8 us
  local copies, waits for them, and re-layouts: 7.98 us -> 3.38 us
    all_to_all x0 -> x1, waiting for transfers between devices: none -> 26.8 us  [local(): lax.all_to_all(after(pieces, out), ('pair', 'win'), 0, 0, tiled=True, axi...]
    ppermute x4 -> x2, waiting for transfers between devices: 23.1 us -> 4.1 us  [the longest x1 4.09 us: local(): row_recv = lax.ppermute(row_send, 'win', other_chip)]
    all_to_all x0 -> x1, starting transfers between devices: none -> 11.9 us  [local(): lax.all_to_all(after(pieces, out), ('pair', 'win'), 0, 0, tiled=True, axi...]
    all_to_all x4 -> x3, starting transfers between devices: 38.3 us -> 28 us  [exchange(): lax.all_to_all(array, 'pair', split_axis=0, concat_axis=0, tiled=True)]
    pallas_call x7 -> x5, Pallas kernels: 40.6 us -> 34.3 us  [the longest x2 23.5 us: correlate(): pl.pallas_call(functools.partial(correlate_kernel, norm), out_shape=[jax....]
    unnamed x22 -> x14, local copies, waits for them, and re-layouts: 7.94 us -> 3.35 us
    all_to_all x4 -> x3, waiting for transfers between devices: 59.8 us -> 64 us  [exchange(): lax.all_to_all(array, 'pair', split_axis=0, concat_axis=0, tiled=True)]
    pallas_call x1, Pallas kernels: 8.3 us -> 4.99 us  [turn(): pl.pallas_call(turn_kernel, grid=(num_bins // bins,), out_shape=jax.Shape...]
  transfers between devices with their start and end apart: 11 -> 9, of which waited for: 8 -> 7; matrix products, arithmetic and copies ran while one was open for 0% -> 0% of each run, Pallas kernels for 19% -> 18%
where the time goes in v5:
time: 265 us; the launch traced here: 261 us
  waiting for transfers between devices  99.8 us (38%)
  Pallas kernels  66.5 us (25%)
  blocking collectives  46.2 us (17%)
  starting transfers between devices  43.9 us (17%)
  local copies, waits for them, and re-layouts  3.38 us (1%)
    all_to_all x3, waiting for transfers between devices, exchange(): lax.all_to_all(array, 'pair', split_axis=0, concat_axis=0, tiled=True)  64 us
    all_to_all x1, blocking collectives, exchange(): lax.all_to_all(array, 'pair', split_axis=0, concat_axis=0, tiled=True)  46.2 us
    all_to_all x3, starting transfers between devices, exchange(): lax.all_to_all(array, 'pair', split_axis=0, concat_axis=0, tiled=True)  28 us
    all_to_all x1, waiting for transfers between devices, local(): lax.all_to_all(after(pieces, out), ('pair', 'win'), 0, 0, tiled=True, axi...  26.8 us
    pallas_call x2, Pallas kernels, correlate(): pl.pallas_call(functools.partial(correlate_kernel, norm), out_shape=[jax....  23.5 us
    all_to_all x1, starting transfers between devices, local(): lax.all_to_all(after(pieces, out), ('pair', 'win'), 0, 0, tiled=True, axi...  11.9 us
    pallas_call x2, Pallas kernels, own_rows(): pl.pallas_call(own_rows_kernel, out_shape=jax.ShapeDtypeStruct((rows, ROU...  8.51 us
    pallas_call x2, Pallas kernels, core_sum(): pl.pallas_call(core_sum_kernel, grid=(1,), out_shape=[jax.ShapeDtypeStruc...  7.91 us
  transfers between devices with their start and end apart: 9, of which 7 were waited for; matrix products, arithmetic and copies ran while one was open for 0% of the time, Pallas kernels for 18%

profile of v5, /device:TPU:16, one launch (start us, length us, event | category | flops | bytes accessed | tf_op | source)
XLA Modules:
  0.0 260.6 jit_solution(5548020504595222023)
XLA Ops:
  0.0 5.4 %whiten.1 = bf16[32,2,96,256]{3,2,1,0:T(8,128)(2,1)} custom-call(s32[1,256]{1,0:T(1,128)} %order_ref.1, bf16[32,2,96,256]{3,2,1,0:T(8,128)(2,1)} %spectra_ref.1), custom_call_target="tpu_custom_call" | custom-call | tf_op jit(solution)/shard_map/whiten/pallas_call | solution.py:45
  5.4 10.9 %all-to-all-start = ((bf16[32,192,256]{2,1,0:T(8,128)(2,1)}), bf16[32,192,256]{2,1,0:T(8,128)(2,1)}, u32[]{:S(2)}, u32[]{:S(2)}) async-start(bf16[32,192,256]{2,1,0:T(8,128)(2,1)} %bitcast.5), calls=%async_computation | async-start | bytes 6291456 | tf_op jit(solution)/shard_map/all_to_all | solution.py:449
  16.4 5.0 %turn.1.own_ref = bf16[32,256,192]{2,1,0:T(8,128)(2,1)} custom-call(bf16[32,192,256]{2,1,0:T(8,128)(2,1)} %bitcast.6), custom_call_target="tpu_custom_call" | custom-call | bytes 12000000 | tf_op jit(solution)/shard_map/turn/pallas_call | solution.py:73
  21.4 3.3 %plan.1 = (s32[2,32]{1,0:T(2,128)}, s32[2,32]{1,0:T(2,128)}, s32[2,32]{1,0:T(2,128)}) custom-call(s32[4,32]{1,0:T(4,128)} %partners_ref.1), custom_call_target="tpu_custom_call" | custom-call | tf_op jit(solution)/shard_map/plan/pallas_call | solution.py:290
  24.7 34.0 %all-to-all-done.source_ref = bf16[32,192,256]{2,1,0:T(8,128)(2,1)} async-done(((bf16[32,192,256]{2,1,0:T(8,128)(2,1)}), bf16[32,192,256]{2,1,0:T(8,128)(2,1)}, u32[]{:S(2)}, u32[]{:S(2)}) %all-to-all-start) | async-done | bytes 3145760 | tf_op jit(solution)/shard_map/all_to_all | solution.py:449
  58.7 5.2 %gather.1 = (bf16[32,192,256]{2,1,0:T(8,128)(2,1)}, bf16[32,192,256]{2,1,0:T(8,128)(2,1)}) custom-call(s32[2,32]{1,0:T(2,128)} %get-tuple-element.28.index_ref, bf16[32,192,256]{2,1,0:T(8,128)(2,1)} %all-to-all-done.source_ref), custom_call_target="tpu_custom_call" | custom-call | tf_op jit(solution)/shard_map/gather/pallas_call | solution.py:101
  63.8 46.2 %all_to_all.25.mate_ref = bf16[32,192,256]{2,1,0:T(8,128)(2,1)} all-to-all(bf16[32,192,256]{2,1,0:T(8,128)(2,1)} %get-tuple-element.31), channel_id=1, replica_groups=mesh['pair'=32,'win'=4] {'pair'}, dimensions={0} | all-to-all | bytes 6291456 | tf_op jit(solution)/shard_map/all_to_all | solution.py:449
  110.0 7.1 %all-to-all-start.1 = ((bf16[32,192,256]{2,1,0:T(8,128)(2,1)}), bf16[32,192,256]{2,1,0:T(8,128)(2,1)}, u32[]{:S(2)}, u32[]{:S(2)}) async-start(bf16[32,192,256]{2,1,0:T(8,128)(2,1)} %get-tuple-element.29), calls=%async_computation.1 | async-start | bytes 6291456 | tf_op jit(solution)/shard_map/all_to_all | solution.py:449
  117.2 0.7 pad_add_fusion.place_ref
  117.8 11.8 %correlate.2 = (f32[17,128,256]{2,1,0:T(8,128)}, bf16[17,128,256]{2,1,0:T(8,128)(2,1)}) custom-call(s32[3]{0:T(128)} %pad_add_fusion.place_ref, bf16[32,256,192]{2,1,0:T(8,128)(2,1)} %turn.1.own_ref, bf16[32,192,256]{2,1,0:T(8,128)(2,1)} %all_to_all.25.mate_ref), custom_call_target="tpu_custom_call" | custom-call | flops 1610612736 | bytes 20000000 | tf_op jit(solution)/shard_map/correlate/pallas_call | solution.py:235
  129.6 0.1 collective-permute-start
  129.7 3.0 %collective-permute-done.recv_ref = bf16[17,128,256]{2,1,0:T(8,128)(2,1)S(1)} collective-permute-done((bf16[17,128,256]{2,1,0:T(8,128)(2,1)}, bf16[17,128,256]{2,1,0:T(8,128)(2,1)S(1)}, u32[]{:S(2)}, u32[]{:S(2)}) %collective-permute-start) | collective-permute-done | bytes 1114144 | tf_op jit(solution)/shard_map/ppermute | solution.py:480
  132.7 0.0 copy-start.2
  132.7 1.0 copy-done.2
  133.7 3.9 %core_sum.2 = (f32[16,64,256]{2,1,0:T(8,128)}, bf16[16,64,256]{2,1,0:T(8,128)(2,1)}, bf16[64,2,64,128]{3,2,1,0:T(8,128)(2,1)}) custom-call(s32[3]{0:T(128)} %pad_add_fusion.place_ref, f32[17,128,256]{2,1,0:T(8,128)} %get-tuple-element.32.keep_ref, bf16[17,128,256]{2,1,0:T(8,128)(2,1)} %copy-done.2), custom_call_target="tpu_custom_call" | custom-call | bytes 12000000 | tf_op jit(solution)/shard_map/core_sum/pallas_call | solution.py:331
  137.7 2.2 collective-permute-start.1
  139.9 18.1 %all-to-all-done.1.mate_ref = bf16[32,192,256]{2,1,0:T(8,128)(2,1)} async-done(((bf16[32,192,256]{2,1,0:T(8,128)(2,1)}), bf16[32,192,256]{2,1,0:T(8,128)(2,1)}, u32[]{:S(2)}, u32[]{:S(2)}) %all-to-all-start.1) | async-done | bytes 3145760 | tf_op jit(solution)/shard_map/all_to_all | solution.py:449
  158.0 11.7 %correlate.3 = (f32[17,128,256]{2,1,0:T(8,128)}, bf16[17,128,256]{2,1,0:T(8,128)(2,1)}) custom-call(s32[3]{0:T(128)} %pad_add_fusion.place_ref, bf16[32,256,192]{2,1,0:T(8,128)(2,1)} %turn.1.own_ref, bf16[32,192,256]{2,1,0:T(8,128)(2,1)} %all-to-all-done.1.mate_ref), custom_call_target="tpu_custom_call" | custom-call | flops 1610612736 | bytes 20000000 | tf_op jit(solution)/shard_map/correlate/pallas_call | solution.py:235
  169.7 0.0 collective-permute-done.1.recv_ref
  169.7 0.0 copy-start.3
  169.7 0.3 collective-permute-start.2
  170.0 0.5 copy-done.3
  170.5 4.2 %own_rows.2.refs_0_ = f32[64,4,16,256]{3,2,1,0:T(8,128)} custom-call(s32[2,32]{1,0:T(2,128)} %get-tuple-element.26.flip_ref, s32[3]{0:T(128)} %pad_add_fusion.place_ref, f32[16,64,256]{2,1,0:T(8,128)} %get-tuple-element.41.own_ref, bf16[16,64,256]{2,1,0:T(8,128)(2,1)} %copy-done.3), custom_call_target="tpu_custom_call" | custom-call | bytes 5000000 | tf_op jit(solution)/shard_map/own_rows/pallas_call | solution.py:391
  174.8 0.0 collective-permute-done.2.recv_ref
  174.8 0.0 copy-start.1
  174.8 1.0 copy-done.1
  175.8 4.0 %core_sum.3 = (f32[16,64,256]{2,1,0:T(8,128)}, bf16[16,64,256]{2,1,0:T(8,128)(2,1)}, bf16[64,2,64,128]{3,2,1,0:T(8,128)(2,1)}) custom-call(s32[3]{0:T(128)} %pad_add_fusion.place_ref, f32[17,128,256]{2,1,0:T(8,128)} %get-tuple-element.36.keep_ref, bf16[17,128,256]{2,1,0:T(8,128)(2,1)} %copy-done.1, ...), custom_call_target="tpu_custom_call", output_to_operand_aliasing={{2}: (3, {})} | custom-call | bytes 12000000 | tf_op jit(solution)/shard_map/core_sum/pallas_call | solution.py:331
  179.7 0.0 copy-start.6
  179.7 11.9 %all-to-all-start.3 = ((bf16[64,2,64,128]{3,2,1,0:T(8,128)(2,1)}), bf16[64,2,64,128]{3,2,1,0:T(8,128)(2,1)}, u32[]{:S(2)}, u32[]{:S(2)}) async-start(bf16[64,2,64,128]{3,2,1,0:T(8,128)(2,1)} %get-tuple-element.42), calls=%async_computation.3 | async-start | bytes 4194304 | tf_op jit(solution)/shard_map/all_to_all | solution.py:488
  191.6 0.0 copy-done.6
  191.6 1.4 collective-permute-start.3
  193.0 26.8 %all-to-all-done.3.spread_ref = bf16[64,2,64,128]{3,2,1,0:T(8,128)(2,1)} async-done(((bf16[64,2,64,128]{3,2,1,0:T(8,128)(2,1)}), bf16[64,2,64,128]{3,2,1,0:T(8,128)(2,1)}, u32[]{:S(2)}, u32[]{:S(2)}) %all-to-all-start.3) | async-done | bytes 2097184 | tf_op jit(solution)/shard_map/all_to_all | solution.py:488
  219.8 2.9 %gather_sum.1 = bf16[32,2,64,128]{3,2,1,0:T(8,128)(2,1)} custom-call(s32[2,32]{1,0:T(2,128)} %get-tuple-element.27.index_ref, bf16[64,2,64,128]{3,2,1,0:T(8,128)(2,1)} %all-to-all-done.3.spread_ref), custom_call_target="tpu_custom_call" | custom-call | tf_op jit(solution)/shard_map/gather_sum/pallas_call | solution.py:371
  222.7 4.1 %collective-permute-done.3.recv_ref = bf16[16,64,256]{2,1,0:T(8,128)(2,1)S(1)} collective-permute-done((bf16[16,64,256]{2,1,0:T(8,128)(2,1)S(1)}, bf16[16,64,256]{2,1,0:T(8,128)(2,1)S(1)}, u32[]{:S(2)}, u32[]{:S(2)}) %collective-permute-start.3) | collective-permute-done | bytes 524320 | tf_op jit(solution)/shard_map/ppermute | solution.py:491
  226.8 0.0 copy-start.4
  226.8 10.0 %all-to-all-start.4 = ((bf16[32,2,64,128]{3,2,1,0:T(8,128)(2,1)}), bf16[32,2,64,128]{3,2,1,0:T(8,128)(2,1)S(1)}, u32[]{:S(2)}, u32[]{:S(2)}) async-start(bf16[32,2,64,128]{3,2,1,0:T(8,128)(2,1)} %gather_sum.1), calls=%async_computation.4 | async-start | bytes 2097152 | tf_op jit(solution)/shard_map/all_to_all | solution.py:449
  236.8 0.0 copy-done.4
  236.8 4.3 %own_rows.3.in_ref = f32[64,4,16,256]{3,2,1,0:T(8,128)} custom-call(s32[2,32]{1,0:T(2,128)} %get-tuple-element.26.flip_ref, s32[3]{0:T(128)} %pad_add_fusion.place_ref, f32[16,64,256]{2,1,0:T(8,128)} %get-tuple-element.45.own_ref, bf16[16,64,256]{2,1,0:T(8,128)(2,1)} %copy-done.4, f32[64,4,16,256]{3,2,1,0:T(8,128)} %own_rows.2.refs_0_), custom_call_target="tpu_custom_call", output_to_operand_aliasing={{}: (4, {})} | custom-call | bytes 5000000 | tf_op jit(solution)/shard_map/own_rows/pallas_call | solution.py:391
  241.1 11.9 %all-to-all-done.4.near_ref = bf16[32,2,64,128]{3,2,1,0:T(8,128)(2,1)S(1)} async-done(((bf16[32,2,64,128]{3,2,1,0:T(8,128)(2,1)}), bf16[32,2,64,128]{3,2,1,0:T(8,128)(2,1)S(1)}, u32[]{:S(2)}, u32[]{:S(2)}) %all-to-all-start.4) | async-done | bytes 1048608 | tf_op jit(solution)/shard_map/all_to_all | solution.py:449
  253.0 0.0 copy-start
  253.0 0.1 collective-permute-start.4
  253.1 1.9 collective-permute-done.4.far_ref
  255.0 0.0 copy-done
  255.0 0.0 copy-start.5
  255.0 0.8 copy-done.5
  255.8 4.7 %mirrored_rows.1 = f32[64,4,16,256]{3,2,1,0:T(8,128)} custom-call(s32[2,32]{1,0:T(2,128)} %get-tuple-element.26.flip_ref, s32[3]{0:T(128)} %pad_add_fusion.place_ref, bf16[32,2,64,128]{3,2,1,0:T(8,128)(2,1)} %copy-done, bf16[16,2,64,128]{3,2,1,0:T(8,128)(2,1)} %copy-done.5, f32[64,4,16,256]{3,2,1,0:T(8,128)} %own_rows.3.in_ref), custom_call_target="tpu_custom_call", output_to_operand_aliasing={{}: (4, {})} | custom-call | tf_op jit(solution)/shard_map/mirrored_rows/pallas_call | solution.py:430
  (1 shorter events, 0.0 us)
Async XLA Ops:
  5.4 53.2 %all-to-all-start = ((bf16[32,192,256]{2,1,0:T(8,128)(2,1)}), bf16[32,192,256]{2,1,0:T(8,128)(2,1)}, u32[]{:S(2)}, u32[]{:S(2)}) async-start(bf16[32,192,256]{2,1,0:T(8,128)(2,1)} %bitcast.5), calls=%async_computation | async-start | bytes 6291456 | tf_op jit(solution)/shard_map/all_to_all | solution.py:449
  110.0 48.0 %all-to-all-start.1 = ((bf16[32,192,256]{2,1,0:T(8,128)(2,1)}), bf16[32,192,256]{2,1,0:T(8,128)(2,1)}, u32[]{:S(2)}, u32[]{:S(2)}) async-start(bf16[32,192,256]{2,1,0:T(8,128)(2,1)} %get-tuple-element.29), calls=%async_computation.1 | async-start | bytes 6291456 | tf_op jit(solution)/shard_map/all_to_all | solution.py:449
  129.6 3.0 %collective-permute-start = (bf16[17,128,256]{2,1,0:T(8,128)(2,1)}, bf16[17,128,256]{2,1,0:T(8,128)(2,1)S(1)}, u32[]{:S(2)}, u32[]{:S(2)}) collective-permute-start(bf16[17,128,256]{2,1,0:T(8,128)(2,1)} %get-tuple-element.33), channel_id=1, source_target_pairs={{0,1},{1,0},{2,3},{3,2},{4,5},{5,4},{6,7},{7,6},{8,9},{9,8},{10,11... | collective-permute-start | bytes 3342344 | tf_op jit(solution)/shard_map/ppermute | solution.py:480
  132.7 1.0 copy-start.2
  137.7 32.0 %collective-permute-start.1 = (bf16[16,64,256]{2,1,0:T(8,128)(2,1)}, bf16[16,64,256]{2,1,0:T(8,128)(2,1)S(1)}, u32[]{:S(2)}, u32[]{:S(2)}) collective-permute-start(bf16[16,64,256]{2,1,0:T(8,128)(2,1)} %get-tuple-element.34), channel_id=1, source_target_pairs={{0,2},{1,3},{2,0},{3,1},{4,6},{5,7},{6,4},{7,5},{8,10},{9,11},{10,... | collective-permute-start | bytes 1572872 | tf_op jit(solution)/shard_map/ppermute | solution.py:485
  169.7 0.8 copy-start.3
  169.7 5.0 %collective-permute-start.2 = (bf16[17,128,256]{2,1,0:T(8,128)(2,1)}, bf16[17,128,256]{2,1,0:T(8,128)(2,1)S(1)}, u32[]{:S(2)}, u32[]{:S(2)}) collective-permute-start(bf16[17,128,256]{2,1,0:T(8,128)(2,1)} %get-tuple-element.38), channel_id=1, source_target_pairs={{0,1},{1,0},{2,3},{3,2},{4,5},{5,4},{6,7},{7,6},{8,9},{9,8},{10,11... | collective-permute-start | bytes 3342344 | tf_op jit(solution)/shard_map/ppermute | solution.py:480
  174.8 1.0 copy-start.1
  179.7 11.9 %copy-start.6 = (bf16[16,64,256]{2,1,0:T(8,128)(2,1)S(1)}, bf16[16,64,256]{2,1,0:T(8,128)(2,1)}, u32[]{:S(2)}) copy-start(bf16[16,64,256]{2,1,0:T(8,128)(2,1)} %get-tuple-element.43) | copy-start | bytes 1572868
  179.7 40.1 %all-to-all-start.3 = ((bf16[64,2,64,128]{3,2,1,0:T(8,128)(2,1)}), bf16[64,2,64,128]{3,2,1,0:T(8,128)(2,1)}, u32[]{:S(2)}, u32[]{:S(2)}) async-start(bf16[64,2,64,128]{3,2,1,0:T(8,128)(2,1)} %get-tuple-element.42), calls=%async_computation.3 | async-start | bytes 4194304 | tf_op jit(solution)/shard_map/all_to_all | solution.py:488
  191.6 35.2 %collective-permute-start.3 = (bf16[16,64,256]{2,1,0:T(8,128)(2,1)S(1)}, bf16[16,64,256]{2,1,0:T(8,128)(2,1)S(1)}, u32[]{:S(2)}, u32[]{:S(2)}) collective-permute-start(bf16[16,64,256]{2,1,0:T(8,128)(2,1)S(1)} %copy-done.6), channel_id=1, source_target_pairs={{0,2},{1,3},{2,0},{3,1},{4,6},{5,7},{6,4},{7,5},{8,10},{9,11},{10,... | collective-permute-start | bytes 1572872 | tf_op jit(solution)/shard_map/ppermute | solution.py:491
  226.8 10.0 %copy-start.4 = (bf16[16,64,256]{2,1,0:T(8,128)(2,1)}, bf16[16,64,256]{2,1,0:T(8,128)(2,1)S(1)}, u32[]{:S(2)}) copy-start(bf16[16,64,256]{2,1,0:T(8,128)(2,1)S(1)} %collective-permute-done.3.recv_ref) | copy-start | bytes 1572868
  226.8 26.2 %all-to-all-start.4 = ((bf16[32,2,64,128]{3,2,1,0:T(8,128)(2,1)}), bf16[32,2,64,128]{3,2,1,0:T(8,128)(2,1)S(1)}, u32[]{:S(2)}, u32[]{:S(2)}) async-start(bf16[32,2,64,128]{3,2,1,0:T(8,128)(2,1)} %gather_sum.1), calls=%async_computation.4 | async-start | bytes 2097152 | tf_op jit(solution)/shard_map/all_to_all | solution.py:449
  253.0 2.0 copy-start
  253.0 2.0 collective-permute-start.4
  255.0 0.8 copy-start.5

commit v6 on v5

--- a/solution.py
+++ b/solution.py
@@ -41,7 +41,7 @@
 
 def whiten(spectra, channel_order):
     num_bins, _, num_windows, cols = spectra.shape
-    rows = 32
+    rows = 48
     return pl.pallas_call(
         whiten_kernel,
         grid=(num_windows // rows,),
@@ -83,12 +83,22 @@
 
 
 def gather_kernel(index_ref, source_ref, *refs):
-    *out_refs, sems = refs
+    *out_refs, arranged, sems = refs
+    places = source_ref.shape[0]
+    chunks = sems.shape[1]
+    step = places // chunks
     copies = []
     for group, out_ref in enumerate(out_refs):
-        for place in range(out_ref.shape[0]):
+        for chunk in range(chunks):
+
+            def body(place, carry):
+                arranged[group, place] = source_ref[index_ref[group, place]]
+                return carry
+
+            lax.fori_loop(chunk * step, (chunk + 1) * step, body, 0)
+            where = pl.ds(chunk * step, step)
             copy = pltpu.make_async_copy(
-                source_ref.at[index_ref[group, place]], out_ref.at[place], sems.at[group, place]
+                arranged.at[group, where], out_ref.at[where], sems.at[group, chunk]
             )
             copy.start()
             copies.append(copy)
@@ -97,16 +107,20 @@
 
 
 def gather(source, index):
-    groups, places = index.shape
+    groups = index.shape[0]
+    anywhere = pl.BlockSpec(memory_space=pl.ANY)
     return pl.pallas_call(
         gather_kernel,
-        out_shape=[jax.ShapeDtypeStruct((places,) + source.shape[1:], source.dtype)] * groups,
+        out_shape=[jax.ShapeDtypeStruct(source.shape, source.dtype)] * groups,
         in_specs=[
             pl.BlockSpec(memory_space=pltpu.SMEM),
             pl.BlockSpec(memory_space=pltpu.VMEM),
         ],
-        out_specs=[pl.BlockSpec(memory_space=pl.ANY)] * groups,
-        scratch_shapes=[pltpu.SemaphoreType.DMA(index.shape)],
+        out_specs=[anywhere] * groups,
+        scratch_shapes=[
+            pltpu.VMEM((groups,) + source.shape, source.dtype),
+            pltpu.SemaphoreType.DMA((groups, 4)),
+        ],
         compiler_params=params(),
         name="gather",
     )(index, source)
@@ -297,51 +311,84 @@
     )(partners)
 
 
-def core_sum_kernel(place_ref, keep_ref, recv_ref, *refs):
-    own_ref, send_ref, piece_ref = refs[-3:]
+def core_sum_kernel(task, place_ref, keep_ref, recv_ref, *refs):
+    own_ref, send_ref, piece_ref, keep, recv, own, send, piece, in_sems, out_sems, piece_sems = refs[-11:]
     core, chip = place_ref[0], place_ref[1]
-    lags, rows, cols = own_ref.shape
+    lags, rows, cols = own.shape
     own_rows = pl.ds(pl.multiple_of(chip * rows, rows), rows)
     other_rows = pl.ds(pl.multiple_of((1 - chip) * rows, rows), rows)
-    for lag in range(lags + 1):
-        if lag < lags:
-            own_ref[lag] = keep_ref[lag, own_rows, :] + recv_ref[lag, own_rows, :].astype(f32)
-            send_ref[lag] = (
-                keep_ref[lag, other_rows, :] + recv_ref[lag, other_rows, :].astype(f32)
-            ).astype(bf16)
-        if lag > 0:
+    chunks = in_sems.shape[1]
+    step = lags // chunks
+    bounds = [0] + [chunk * step + 1 for chunk in range(1, chunks)] + [lags + 1]
+    arrivals, departures = [], []
+    for chunk in range(chunks):
+        where = pl.ds(bounds[chunk], bounds[chunk + 1] - bounds[chunk])
+        pair = (
+            pltpu.make_async_copy(keep_ref.at[where], keep.at[where], in_sems.at[0, chunk]),
+            pltpu.make_async_copy(recv_ref.at[where], recv.at[where], in_sems.at[1, chunk]),
+        )
+        for copy in pair:
+            copy.start()
+        arrivals.append(pair)
+
+    def leave(source, target, sem):
+        copy = pltpu.make_async_copy(source, target, sem)
+        copy.start()
+        departures.append(copy)
+
+    for chunk in range(chunks):
+        for copy in arrivals[chunk]:
+            copy.wait()
+        first, last = bounds[chunk], bounds[chunk + 1]
+        for lag in range(first, min(last, lags)):
+            own[lag] = keep[lag, own_rows, :] + recv[lag, own_rows, :].astype(f32)
+            send[lag] = (keep[lag, other_rows, :] + recv[lag, other_rows, :].astype(f32)).astype(
+                bf16
+            )
+        for lag in range(max(first, 1), last):
             back = lags - lag
-            turned = (keep_ref[lag] + recv_ref[lag].astype(f32)).T
+            turned = (keep[lag] + recv[lag].astype(f32)).T
             for half in range(2):
                 low = turned[2 * half * rows : (2 * half + 1) * rows]
                 high = turned[(2 * half + 1) * rows : (2 * half + 2) * rows]
                 base = 2 * half * lags + back
-                piece_ref[base, 0] = jnp.where(core == 0, low, high).astype(bf16)
-                piece_ref[base + lags, 0] = jnp.where(core == 0, high, low).astype(bf16)
+                piece[base] = jnp.where(core == 0, low, high).astype(bf16)
+                piece[base + lags] = jnp.where(core == 0, high, low).astype(bf16)
+        where = pl.ds(first, min(last, lags) - first)
+        leave(own.at[where], own_ref.at[where], out_sems.at[0, chunk])
+        leave(send.at[where], send_ref.at[where], out_sems.at[1, chunk])
+        for group in range(4):
+            where = pl.ds(group * lags + lags - last + 1, step)
+            leave(piece.at[where], piece_ref.at[where, task], piece_sems.at[group, chunk])
+    for copy in departures:
+        copy.wait()
 
 
 def core_sum(place, keep, recv, task, tasks, pieces):
     lags, rows, cols = keep.shape
-    vmem = pl.BlockSpec(memory_space=pltpu.VMEM)
+    anywhere = pl.BlockSpec(memory_space=pl.ANY)
     count = 4 * (lags - 1)
-    shape = (count, tasks, cols // 4, rows)
-    whole = pl.BlockSpec((lags - 1, rows // 2, cols), lambda s: (0, 0, 0))
-    given = pl.BlockSpec((lags, rows, cols), lambda s: (0, 0, 0))
+    part = (lags - 1, rows // 2, cols)
+    piece = (cols // 4, rows)
     extra = [] if pieces is None else [pieces]
     return pl.pallas_call(
-        core_sum_kernel,
-        grid=(1,),
+        functools.partial(core_sum_kernel, task),
         out_shape=[
-            jax.ShapeDtypeStruct((lags - 1, rows // 2, cols), f32),
-            jax.ShapeDtypeStruct((lags - 1, rows // 2, cols), bf16),
-            jax.ShapeDtypeStruct(shape, bf16),
-        ],
-        in_specs=[pl.BlockSpec(memory_space=pltpu.SMEM), given, given]
-        + [pl.BlockSpec(memory_space=pl.ANY)] * len(extra),
-        out_specs=[
-            whole,
-            whole,
-            pl.BlockSpec((count, 1) + shape[2:], lambda s: (0, task, 0, 0)),
+            jax.ShapeDtypeStruct(part, f32),
+            jax.ShapeDtypeStruct(part, bf16),
+            jax.ShapeDtypeStruct((count, tasks) + piece, bf16),
+        ],
+        in_specs=[pl.BlockSpec(memory_space=pltpu.SMEM)] + [anywhere] * (2 + len(extra)),
+        out_specs=[anywhere] * 3,
+        scratch_shapes=[
+            pltpu.VMEM(keep.shape, f32),
+            pltpu.VMEM(keep.shape, bf16),
+            pltpu.VMEM(part, f32),
+            pltpu.VMEM(part, bf16),
+            pltpu.VMEM((count,) + piece, bf16),
+            pltpu.SemaphoreType.DMA((2, 4)),
+            pltpu.SemaphoreType.DMA((2, 4)),
+            pltpu.SemaphoreType.DMA((4, 4)),
         ],
         input_output_aliases={3: 2} if extra else {},
         compiler_params=params(),
@@ -385,7 +432,7 @@
 
 def own_rows(place, flip, task, own, recv, out):
     lags, rows, cols = own.shape
-    step = 16
+    step = 64
     extra = [] if out is None else [out]
     piece = pl.BlockSpec((lags, step, cols), lambda s, flip, place: (0, s, 0))
     return pl.pallas_call(
@@ -425,7 +472,7 @@
 def mirrored_rows(place, flip, near, far, out):
     rows, _, lags, cols = out.shape
     tasks = near.shape[1]
-    step = 32
+    step = 64
     back = pl.BlockSpec((lags, 1, step, near.shape[3]), lambda t, s, flip, place: (0, t, s, 0))
     return pl.pallas_call(
         mirrored_rows_kernel,
@@ -486,12 +533,12 @@
             moved = [rows[task][1]]
     out = own_rows(place, flip, 0, *rows[0], None)
     spread = lax.all_to_all(
-        after(pieces, out), ("pair", "win"), 0, 0, tiled=True, axis_index_groups=groups
+        pieces, ("pair", "win"), 0, 0, tiled=True, axis_index_groups=groups
     )
+    spread = after(spread, out)
     row_recv = lax.ppermute(row_send, "win", other_chip)
-    returned = exchange(after(gather_sum(back_of, spread), row_recv))
+    returned = exchange(gather_sum(back_of, spread))
     out = own_rows(place, flip, 1, own_sum, row_recv, out)
-    returned = after(returned, out)
     far = lax.ppermute(returned[LAGS:], "win", other_core)
     return mirrored_rows(place, flip, returned, far, out)[None]
 

time: 265 us -> 258 us (0.974); the launches traced: 261 us -> 257 us
  waiting for transfers between devices: 99.8 us -> 105 us
  Pallas kernels: 66.5 us -> 62.2 us
  starting transfers between devices: 43.9 us -> 40.2 us
    all_to_all x3, starting transfers between devices: 28 us -> 23.9 us  [exchange(): lax.all_to_all(array, 'pair', split_axis=0, concat_axis=0, tiled=True)]
    ppermute x1, waiting for transfers between devices: 4.09 us -> 7.5 us  [local(): row_recv = lax.ppermute(row_send, 'win', other_chip)]
    ppermute x2, waiting for transfers between devices: 2.95 us -> 5.9 us  [local(): recv = lax.ppermute(after(send, *moved), 'win', other_core)]
  transfers between devices with their start and end apart: 9 -> 9, of which waited for: 7 -> 7; matrix products, arithmetic and copies ran while one was open for 0% -> 0% of each run, Pallas kernels for 18% -> 16%
where the time goes in v6:
time: 258 us; the launch traced here: 257 us
  waiting for transfers between devices  105 us (41%)
  Pallas kernels  62.2 us (24%)
  blocking collectives  46.2 us (18%)
  starting transfers between devices  40.2 us (16%)
    all_to_all x3, waiting for transfers between devices, exchange(): lax.all_to_all(array, 'pair', split_axis=0, concat_axis=0, tiled=True)  66.7 us
    all_to_all x1, blocking collectives, exchange(): lax.all_to_all(array, 'pair', split_axis=0, concat_axis=0, tiled=True)  46.2 us
    all_to_all x1, waiting for transfers between devices, local(): lax.all_to_all(pieces, ('pair', 'win'), 0, 0, tiled=True, axis_index_grou...  25.1 us
    all_to_all x3, starting transfers between devices, exchange(): lax.all_to_all(array, 'pair', split_axis=0, concat_axis=0, tiled=True)  23.9 us
    pallas_call x2, Pallas kernels, correlate(): pl.pallas_call(functools.partial(correlate_kernel, norm), out_shape=[jax....  23.5 us
    all_to_all x1, starting transfers between devices, local(): lax.all_to_all(pieces, ('pair', 'win'), 0, 0, tiled=True, axis_index_grou...  11.7 us
    pallas_call x2, Pallas kernels, core_sum(): pl.pallas_call(functools.partial(core_sum_kernel, task), out_shape=[jax.S...  7.66 us
    ppermute x1, waiting for transfers between devices, local(): row_recv = lax.ppermute(row_send, 'win', other_chip)  7.5 us
  transfers between devices with their start and end apart: 9, of which 7 were waited for; matrix products, arithmetic and copies ran while one was open for 0% of the time, Pallas kernels for 16%

profile of v6, /device:TPU:16, one launch (start us, length us, event | category | flops | bytes accessed | tf_op | source)
XLA Modules:
  0.0 256.6 jit_solution(10968664164731149115)
XLA Ops:
  0.0 4.9 %whiten.1 = bf16[32,2,96,256]{3,2,1,0:T(8,128)(2,1)} custom-call(s32[1,256]{1,0:T(1,128)} %order_ref.1, bf16[32,2,96,256]{3,2,1,0:T(8,128)(2,1)} %spectra_ref.1), custom_call_target="tpu_custom_call" | custom-call | tf_op jit(solution)/shard_map/whiten/pallas_call | solution.py:45
  4.9 10.9 %all-to-all-start = ((bf16[32,192,256]{2,1,0:T(8,128)(2,1)}), bf16[32,192,256]{2,1,0:T(8,128)(2,1)}, u32[]{:S(2)}, u32[]{:S(2)}) async-start(bf16[32,192,256]{2,1,0:T(8,128)(2,1)} %bitcast.5), calls=%async_computation | async-start | bytes 6291456 | tf_op jit(solution)/shard_map/all_to_all | solution.py:496
  15.9 5.0 %turn.1.own_ref = bf16[32,256,192]{2,1,0:T(8,128)(2,1)} custom-call(bf16[32,192,256]{2,1,0:T(8,128)(2,1)} %bitcast.6), custom_call_target="tpu_custom_call" | custom-call | bytes 12000000 | tf_op jit(solution)/shard_map/turn/pallas_call | solution.py:73
  20.9 3.3 %plan.1 = (s32[2,32]{1,0:T(2,128)}, s32[2,32]{1,0:T(2,128)}, s32[2,32]{1,0:T(2,128)}) custom-call(s32[4,32]{1,0:T(4,128)} %partners_ref.1), custom_call_target="tpu_custom_call" | custom-call | tf_op jit(solution)/shard_map/plan/pallas_call | solution.py:304
  24.2 33.9 %all-to-all-done.source_ref = bf16[32,192,256]{2,1,0:T(8,128)(2,1)} async-done(((bf16[32,192,256]{2,1,0:T(8,128)(2,1)}), bf16[32,192,256]{2,1,0:T(8,128)(2,1)}, u32[]{:S(2)}, u32[]{:S(2)}) %all-to-all-start) | async-done | bytes 3145760 | tf_op jit(solution)/shard_map/all_to_all | solution.py:496
  58.1 4.7 %gather.1 = (bf16[32,192,256]{2,1,0:T(8,128)(2,1)}, bf16[32,192,256]{2,1,0:T(8,128)(2,1)}) custom-call(s32[2,32]{1,0:T(2,128)} %get-tuple-element.26.index_ref, bf16[32,192,256]{2,1,0:T(8,128)(2,1)} %all-to-all-done.source_ref), custom_call_target="tpu_custom_call" | custom-call | tf_op jit(solution)/shard_map/gather/pallas_call | solution.py:112
  62.9 46.2 %all_to_all.25.mate_ref = bf16[32,192,256]{2,1,0:T(8,128)(2,1)} all-to-all(bf16[32,192,256]{2,1,0:T(8,128)(2,1)} %get-tuple-element.29), channel_id=1, replica_groups=mesh['pair'=32,'win'=4] {'pair'}, dimensions={0} | all-to-all | bytes 6291456 | tf_op jit(solution)/shard_map/all_to_all | solution.py:496
  109.1 7.1 %all-to-all-start.1 = ((bf16[32,192,256]{2,1,0:T(8,128)(2,1)}), bf16[32,192,256]{2,1,0:T(8,128)(2,1)}, u32[]{:S(2)}, u32[]{:S(2)}) async-start(bf16[32,192,256]{2,1,0:T(8,128)(2,1)} %get-tuple-element.27), calls=%async_computation.1 | async-start | bytes 6291456 | tf_op jit(solution)/shard_map/all_to_all | solution.py:496
  116.3 0.6 pad_add_fusion.place_ref
  116.9 11.7 %correlate.2 = (f32[17,128,256]{2,1,0:T(8,128)}, bf16[17,128,256]{2,1,0:T(8,128)(2,1)}) custom-call(s32[3]{0:T(128)} %pad_add_fusion.place_ref, bf16[32,256,192]{2,1,0:T(8,128)(2,1)} %turn.1.own_ref, bf16[32,192,256]{2,1,0:T(8,128)(2,1)} %all_to_all.25.mate_ref), custom_call_target="tpu_custom_call" | custom-call | flops 1610612736 | bytes 20000000 | tf_op jit(solution)/shard_map/correlate/pallas_call | solution.py:249
  128.6 0.1 collective-permute-start
  128.7 3.0 %collective-permute-done.recv_ref = bf16[17,128,256]{2,1,0:T(8,128)(2,1)S(1)} collective-permute-done((bf16[17,128,256]{2,1,0:T(8,128)(2,1)}, bf16[17,128,256]{2,1,0:T(8,128)(2,1)S(1)}, u32[]{:S(2)}, u32[]{:S(2)}) %collective-permute-start) | collective-permute-done | bytes 1114144 | tf_op jit(solution)/shard_map/ppermute | solution.py:527
  131.6 0.0 copy-start.2
  131.6 1.0 copy-done.2
  132.7 3.8 %core_sum.2 = (f32[16,64,256]{2,1,0:T(8,128)}, bf16[16,64,256]{2,1,0:T(8,128)(2,1)}, bf16[64,2,64,128]{3,2,1,0:T(8,128)(2,1)}) custom-call(s32[3]{0:T(128)} %pad_add_fusion.place_ref, f32[17,128,256]{2,1,0:T(8,128)} %get-tuple-element.30.keep_ref, bf16[17,128,256]{2,1,0:T(8,128)(2,1)} %copy-done.2), custom_call_target="tpu_custom_call" | custom-call | bytes 12000000 | tf_op jit(solution)/shard_map/core_sum/pallas_call | solution.py:374
  136.5 2.3 collective-permute-start.1
  138.8 18.3 %all-to-all-done.1.mate_ref = bf16[32,192,256]{2,1,0:T(8,128)(2,1)} async-done(((bf16[32,192,256]{2,1,0:T(8,128)(2,1)}), bf16[32,192,256]{2,1,0:T(8,128)(2,1)}, u32[]{:S(2)}, u32[]{:S(2)}) %all-to-all-start.1) | async-done | bytes 3145760 | tf_op jit(solution)/shard_map/all_to_all | solution.py:496
  157.1 11.7 %correlate.3 = (f32[17,128,256]{2,1,0:T(8,128)}, bf16[17,128,256]{2,1,0:T(8,128)(2,1)}) custom-call(s32[3]{0:T(128)} %pad_add_fusion.place_ref, bf16[32,256,192]{2,1,0:T(8,128)(2,1)} %turn.1.own_ref, bf16[32,192,256]{2,1,0:T(8,128)(2,1)} %all-to-all-done.1.mate_ref), custom_call_target="tpu_custom_call" | custom-call | flops 1610612736 | bytes 20000000 | tf_op jit(solution)/shard_map/correlate/pallas_call | solution.py:249
  168.9 0.0 collective-permute-done.1.recv_ref
  168.9 0.0 copy-start.3
  168.9 0.3 collective-permute-start.2
  169.2 3.0 %collective-permute-done.2.recv_ref = bf16[17,128,256]{2,1,0:T(8,128)(2,1)S(1)} collective-permute-done((bf16[17,128,256]{2,1,0:T(8,128)(2,1)}, bf16[17,128,256]{2,1,0:T(8,128)(2,1)S(1)}, u32[]{:S(2)}, u32[]{:S(2)}) %collective-permute-start.2) | collective-permute-done | bytes 1114144 | tf_op jit(solution)/shard_map/ppermute | solution.py:527
  172.1 0.0 copy-start.1
  172.1 1.0 copy-done.1
  173.1 3.8 %core_sum.3 = (f32[16,64,256]{2,1,0:T(8,128)}, bf16[16,64,256]{2,1,0:T(8,128)(2,1)}, bf16[64,2,64,128]{3,2,1,0:T(8,128)(2,1)}) custom-call(s32[3]{0:T(128)} %pad_add_fusion.place_ref, f32[17,128,256]{2,1,0:T(8,128)} %get-tuple-element.34.keep_ref, bf16[17,128,256]{2,1,0:T(8,128)(2,1)} %copy-done.1, ...), custom_call_target="tpu_custom_call", output_to_operand_aliasing={{2}: (3, {})} | custom-call | bytes 12000000 | tf_op jit(solution)/shard_map/core_sum/pallas_call | solution.py:374
  176.9 11.7 %all-to-all-start.3 = ((bf16[64,2,64,128]{3,2,1,0:T(8,128)(2,1)}), bf16[64,2,64,128]{3,2,1,0:T(8,128)(2,1)}, u32[]{:S(2)}, u32[]{:S(2)}) async-start(bf16[64,2,64,128]{3,2,1,0:T(8,128)(2,1)} %get-tuple-element.38), calls=%async_computation.3 | async-start | bytes 4194304 | tf_op jit(solution)/shard_map/all_to_all | solution.py:535
  188.7 0.0 copy-done.3
  188.7 3.3 %own_rows.2.refs_0_ = f32[64,4,16,256]{3,2,1,0:T(8,128)} custom-call(s32[2,32]{1,0:T(2,128)} %get-tuple-element.24.flip_ref, s32[3]{0:T(128)} %pad_add_fusion.place_ref, f32[16,64,256]{2,1,0:T(8,128)} %get-tuple-element.39.own_ref, bf16[16,64,256]{2,1,0:T(8,128)(2,1)} %copy-done.3), custom_call_target="tpu_custom_call" | custom-call | bytes 5000000 | tf_op jit(solution)/shard_map/own_rows/pallas_call | solution.py:438
  191.9 25.1 %all-to-all-done.3.spread_ref = bf16[64,2,64,128]{3,2,1,0:T(8,128)(2,1)} async-done(((bf16[64,2,64,128]{3,2,1,0:T(8,128)(2,1)}), bf16[64,2,64,128]{3,2,1,0:T(8,128)(2,1)}, u32[]{:S(2)}, u32[]{:S(2)}) %all-to-all-start.3) | async-done | bytes 2097184 | tf_op jit(solution)/shard_map/all_to_all | solution.py:535
  217.1 2.9 %gather_sum.1 = bf16[32,2,64,128]{3,2,1,0:T(8,128)(2,1)} custom-call(s32[2,32]{1,0:T(2,128)} %get-tuple-element.25.index_ref, bf16[64,2,64,128]{3,2,1,0:T(8,128)(2,1)} %all-to-all-done.3.spread_ref), custom_call_target="tpu_custom_call" | custom-call | tf_op jit(solution)/shard_map/gather_sum/pallas_call | solution.py:418
  220.0 5.8 %all-to-all-start.4 = ((bf16[32,2,64,128]{3,2,1,0:T(8,128)(2,1)}), bf16[32,2,64,128]{3,2,1,0:T(8,128)(2,1)S(1)}, u32[]{:S(2)}, u32[]{:S(2)}) async-start(bf16[32,2,64,128]{3,2,1,0:T(8,128)(2,1)} %gather_sum.1), calls=%async_computation.4 | async-start | bytes 2097152 | tf_op jit(solution)/shard_map/all_to_all | solution.py:496
  225.8 1.9 collective-permute-start.4
  227.6 14.5 %all-to-all-done.4.near_ref = bf16[32,2,64,128]{3,2,1,0:T(8,128)(2,1)S(1)} async-done(((bf16[32,2,64,128]{3,2,1,0:T(8,128)(2,1)}), bf16[32,2,64,128]{3,2,1,0:T(8,128)(2,1)S(1)}, u32[]{:S(2)}, u32[]{:S(2)}) %all-to-all-start.4) | async-done | bytes 1048608 | tf_op jit(solution)/shard_map/all_to_all | solution.py:496
  242.1 0.0 copy-start
  242.1 0.1 collective-permute-start.3
  242.2 7.5 %collective-permute-done.4.recv_ref = bf16[16,64,256]{2,1,0:T(8,128)(2,1)} collective-permute-done((bf16[16,64,256]{2,1,0:T(8,128)(2,1)}, bf16[16,64,256]{2,1,0:T(8,128)(2,1)}, u32[]{:S(2)}, u32[]{:S(2)}) %collective-permute-start.4) | collective-permute-done | bytes 524320 | tf_op jit(solution)/shard_map/ppermute | solution.py:539
  249.7 3.3 %own_rows.3.in_ref = f32[64,4,16,256]{3,2,1,0:T(8,128)} custom-call(s32[2,32]{1,0:T(2,128)} %get-tuple-element.24.flip_ref, s32[3]{0:T(128)} %pad_add_fusion.place_ref, f32[16,64,256]{2,1,0:T(8,128)} %get-tuple-element.41.own_ref, bf16[16,64,256]{2,1,0:T(8,128)(2,1)} %collective-permute-done.4.recv_ref, ...), custom_call_target="tpu_custom_call", output_to_operand_aliasing={{}: (4, {})} | custom-call | bytes 5000000 | tf_op jit(solution)/shard_map/own_rows/pallas_call | solution.py:438
  253.0 0.0 copy-done
  253.0 0.0 collective-permute-done.3.far_ref
  253.0 3.6 %mirrored_rows.1 = f32[64,4,16,256]{3,2,1,0:T(8,128)} custom-call(s32[2,32]{1,0:T(2,128)} %get-tuple-element.24.flip_ref, s32[3]{0:T(128)} %pad_add_fusion.place_ref, bf16[32,2,64,128]{3,2,1,0:T(8,128)(2,1)} %copy-done, bf16[16,2,64,128]{3,2,1,0:T(8,128)(2,1)} %collective-permute-done.3.far_ref, ...), custom_call_target="tpu_custom_call", output_to_operand_aliasing={{}: (4, {})} | custom-call | tf_op jit(solution)/shard_map/mirrored_rows/pallas_call | solution.py:477
  (1 shorter events, 0.0 us)
Async XLA Ops:
  4.9 53.2 %all-to-all-start = ((bf16[32,192,256]{2,1,0:T(8,128)(2,1)}), bf16[32,192,256]{2,1,0:T(8,128)(2,1)}, u32[]{:S(2)}, u32[]{:S(2)}) async-start(bf16[32,192,256]{2,1,0:T(8,128)(2,1)} %bitcast.5), calls=%async_computation | async-start | bytes 6291456 | tf_op jit(solution)/shard_map/all_to_all | solution.py:496
  109.1 48.0 %all-to-all-start.1 = ((bf16[32,192,256]{2,1,0:T(8,128)(2,1)}), bf16[32,192,256]{2,1,0:T(8,128)(2,1)}, u32[]{:S(2)}, u32[]{:S(2)}) async-start(bf16[32,192,256]{2,1,0:T(8,128)(2,1)} %get-tuple-element.27), calls=%async_computation.1 | async-start | bytes 6291456 | tf_op jit(solution)/shard_map/all_to_all | solution.py:496
  128.6 3.0 %collective-permute-start = (bf16[17,128,256]{2,1,0:T(8,128)(2,1)}, bf16[17,128,256]{2,1,0:T(8,128)(2,1)S(1)}, u32[]{:S(2)}, u32[]{:S(2)}) collective-permute-start(bf16[17,128,256]{2,1,0:T(8,128)(2,1)} %get-tuple-element.31), channel_id=1, source_target_pairs={{0,1},{1,0},{2,3},{3,2},{4,5},{5,4},{6,7},{7,6},{8,9},{9,8},{10,11... | collective-permute-start | bytes 3342344 | tf_op jit(solution)/shard_map/ppermute | solution.py:527
  131.6 1.0 copy-start.2
  136.5 32.3 %collective-permute-start.1 = (bf16[16,64,256]{2,1,0:T(8,128)(2,1)}, bf16[16,64,256]{2,1,0:T(8,128)(2,1)S(1)}, u32[]{:S(2)}, u32[]{:S(2)}) collective-permute-start(bf16[16,64,256]{2,1,0:T(8,128)(2,1)} %get-tuple-element.32), channel_id=1, source_target_pairs={{0,2},{1,3},{2,0},{3,1},{4,6},{5,7},{6,4},{7,5},{8,10},{9,11},{10,... | collective-permute-start | bytes 1572872 | tf_op jit(solution)/shard_map/ppermute | solution.py:532
  168.9 19.8 %copy-start.3 = (bf16[16,64,256]{2,1,0:T(8,128)(2,1)}, bf16[16,64,256]{2,1,0:T(8,128)(2,1)S(1)}, u32[]{:S(2)}) copy-start(bf16[16,64,256]{2,1,0:T(8,128)(2,1)S(1)} %collective-permute-done.1.recv_ref) | copy-start | bytes 1572868
  168.9 3.2 %collective-permute-start.2 = (bf16[17,128,256]{2,1,0:T(8,128)(2,1)}, bf16[17,128,256]{2,1,0:T(8,128)(2,1)S(1)}, u32[]{:S(2)}, u32[]{:S(2)}) collective-permute-start(bf16[17,128,256]{2,1,0:T(8,128)(2,1)} %get-tuple-element.36), channel_id=1, source_target_pairs={{0,1},{1,0},{2,3},{3,2},{4,5},{5,4},{6,7},{7,6},{8,9},{9,8},{10,11... | collective-permute-start | bytes 3342344 | tf_op jit(solution)/shard_map/ppermute | solution.py:527
  172.1 1.0 copy-start.1
  176.9 40.1 %all-to-all-start.3 = ((bf16[64,2,64,128]{3,2,1,0:T(8,128)(2,1)}), bf16[64,2,64,128]{3,2,1,0:T(8,128)(2,1)}, u32[]{:S(2)}, u32[]{:S(2)}) async-start(bf16[64,2,64,128]{3,2,1,0:T(8,128)(2,1)} %get-tuple-element.38), calls=%async_computation.3 | async-start | bytes 4194304 | tf_op jit(solution)/shard_map/all_to_all | solution.py:535
  220.0 22.1 %all-to-all-start.4 = ((bf16[32,2,64,128]{3,2,1,0:T(8,128)(2,1)}), bf16[32,2,64,128]{3,2,1,0:T(8,128)(2,1)S(1)}, u32[]{:S(2)}, u32[]{:S(2)}) async-start(bf16[32,2,64,128]{3,2,1,0:T(8,128)(2,1)} %gather_sum.1), calls=%async_computation.4 | async-start | bytes 2097152 | tf_op jit(solution)/shard_map/all_to_all | solution.py:496
  225.8 24.0 %collective-permute-start.4 = (bf16[16,64,256]{2,1,0:T(8,128)(2,1)}, bf16[16,64,256]{2,1,0:T(8,128)(2,1)}, u32[]{:S(2)}, u32[]{:S(2)}) collective-permute-start(bf16[16,64,256]{2,1,0:T(8,128)(2,1)} %get-tuple-element.42), channel_id=1, source_target_pairs={{0,2},{1,3},{2,0},{3,1},{4,6},{5,7},{6,4},{7,5},{8,10},{9,11},{10,... | collective-permute-start | bytes 1572872 | tf_op jit(solution)/shard_map/ppermute | solution.py:539
  242.1 10.9 %copy-start = (bf16[32,2,64,128]{3,2,1,0:T(8,128)(2,1)}, bf16[32,2,64,128]{3,2,1,0:T(8,128)(2,1)S(1)}, u32[]{:S(2)}) copy-start(bf16[32,2,64,128]{3,2,1,0:T(8,128)(2,1)S(1)} %all-to-all-done.4.near_ref) | copy-start | bytes 3145732
  242.1 10.9 %collective-permute-start.3 = (bf16[16,2,64,128]{3,2,1,0:T(8,128)(2,1)S(1)}, bf16[16,2,64,128]{3,2,1,0:T(8,128)(2,1)}, u32[]{:S(2)}, u32[]{:S(2)}) collective-permute-start(bf16[16,2,64,128]{3,2,1,0:T(8,128)(2,1)S(1)} %slice.4), channel_id=1, source_target_pairs={{0,1},{1,0},{2,3},{3,2},{4,5},{5,4},{6,7},{7,6},{8,9},{9,8},{10,11... | collective-permute-start | bytes 1572872 | tf_op jit(solution)/shard_map/ppermute | solution.py:542

commit v7 on v6

--- a/solution.py
+++ b/solution.py
@@ -10,7 +10,7 @@
 
 LAGS = 16
 ROUNDS = 4
-VMEM_BYTES = 62 * 1024 * 1024
+VMEM_BYTES = 63 * 1024 * 1024
 QUARTER_ORDER = (0, 2, 1, 3)
 bf16 = jnp.bfloat16
 f32 = jnp.float32
@@ -82,23 +82,52 @@
     )(own_rows)
 
 
-def gather_kernel(index_ref, source_ref, *refs):
-    *out_refs, arranged, sems = refs
-    places = source_ref.shape[0]
+def plan_task(task, partners_ref, mate_ref, back_ref, flip_ref):
+    blocks = partners_ref.shape[1]
+    first, second = 2 * task, 2 * task + 1
+    for block in range(blocks):
+        flip_ref[task, block] = -1
+
+    def walk(block):
+        partner = partners_ref[first, block]
+        following = partners_ref[second, partner]
+        flip_ref[task, block] = 0
+        flip_ref[task, partner] = 1
+        mate_ref[task, block] = partner
+        back_ref[task, partner] = block
+        mate_ref[task, partner] = following
+        back_ref[task, following] = partner
+        return following
+
+    def start(block, carry):
+        lax.while_loop(lambda block: flip_ref[task, block] < 0, walk, block)
+        return carry
+
+    lax.fori_loop(0, blocks, start, 0)
+
+
+def gather_kernel(partners_ref, source_ref, *refs):
+    *out_refs, mate_ref, back_ref, flip_ref, source, arranged, in_sem, sems = refs
+    arrival = pltpu.make_async_copy(source_ref, source, in_sem.at[0])
+    arrival.start()
+    places = source.shape[0]
     chunks = sems.shape[1]
     step = places // chunks
     copies = []
-    for group, out_ref in enumerate(out_refs):
+    for task, out_ref in enumerate(out_refs):
+        plan_task(task, partners_ref, mate_ref, back_ref, flip_ref)
+        if task == 0:
+            arrival.wait()
         for chunk in range(chunks):
 
             def body(place, carry):
-                arranged[group, place] = source_ref[index_ref[group, place]]
+                arranged[task, place] = source[mate_ref[task, place]]
                 return carry
 
             lax.fori_loop(chunk * step, (chunk + 1) * step, body, 0)
             where = pl.ds(chunk * step, step)
             copy = pltpu.make_async_copy(
-                arranged.at[group, where], out_ref.at[where], sems.at[group, chunk]
+                arranged.at[task, where], out_ref.at[where], sems.at[task, chunk]
             )
             copy.start()
             copies.append(copy)
@@ -106,24 +135,27 @@
         copy.wait()
 
 
-def gather(source, index):
-    groups = index.shape[0]
+def gather(source, partners):
+    rounds, blocks = partners.shape
+    tasks = rounds // 2
     anywhere = pl.BlockSpec(memory_space=pl.ANY)
-    return pl.pallas_call(
+    smem = pl.BlockSpec(memory_space=pltpu.SMEM)
+    table = jax.ShapeDtypeStruct((tasks, blocks), jnp.int32)
+    results = pl.pallas_call(
         gather_kernel,
-        out_shape=[jax.ShapeDtypeStruct(source.shape, source.dtype)] * groups,
-        in_specs=[
-            pl.BlockSpec(memory_space=pltpu.SMEM),
-            pl.BlockSpec(memory_space=pltpu.VMEM),
+        out_shape=[jax.ShapeDtypeStruct(source.shape, source.dtype)] * tasks + [table] * 3,
+        in_specs=[smem, anywhere],
+        out_specs=[anywhere] * tasks + [smem] * 3,
+        scratch_shapes=[
+            pltpu.VMEM(source.shape, source.dtype),
+            pltpu.VMEM((tasks,) + source.shape, source.dtype),
+            pltpu.SemaphoreType.DMA((1,)),
+            pltpu.SemaphoreType.DMA((tasks, 4)),
         ],
-        out_specs=[anywhere] * groups,
-        scratch_shapes=[
-            pltpu.VMEM((groups,) + source.shape, source.dtype),
-            pltpu.SemaphoreType.DMA((groups, 4)),
-        ],
         compiler_params=params(),
         name="gather",
-    )(index, source)
+    )(partners, source)
+    return results[:tasks], results[tasks + 1], results[tasks + 2]
 
 
 def weighted(terms):
@@ -134,6 +166,28 @@
         term = value * weight
         total = term if total is None else total + term
     return total
+
+
+def odd_multiples(base, sign):
+    twice = lambda f, k: 2 * math.cos(math.pi * f * k / 16)
+    plus = {f: base[f] + base[16 - f] for f in range(1, 8)}
+    minus = {f: base[f] - base[16 - f] for f in range(1, 8)}
+    end = base[16] if base[0] is None else base[0]
+    flip = -1 if base[0] is None else 1
+    doubled = end + end
+    first = end + base[8]
+    for f in range(1, 8):
+        first = first + plus[f]
+    sums = [first]
+    for k in (1, 2, 3):
+        if k == 2:
+            total = weighted([(twice(f, k), plus[f] - plus[8 - f]) for f in range(1, 4)])
+            total = total + doubled - (base[8] + base[8])
+        else:
+            total = weighted([(twice(f, k), minus[f]) for f in range(1, 8)])
+            total = total + doubled if flip > 0 else total - doubled
+        sums.append(total + sums[-1] if sign > 0 else total - sums[-1])
+    return sums
 
 
 def lag_sums(real, imag, norm):
@@ -145,8 +199,9 @@
     for f in range(1, 16):
         a, b = real(f), real(32 - f)
         low[f], diff[f] = a + b, a - b
-    for t in (1, 3, 5, 7):
-        even[t] = weighted([(cosine(f, t), diff[f]) for f in range(16)])
+    base = {f: diff[f] * cosine(f, 1) for f in range(16)}
+    base[16] = None
+    even[1], even[3], even[5], even[7] = odd_multiples(base, -1)
     minus = {f: low[f] - low[16 - f] for f in range(8)}
     for t in (2, 6):
         even[t] = weighted([(cosine(f, t), minus[f]) for f in range(8)])
@@ -166,8 +221,9 @@
     for f in range(1, 16):
         a, b = imag(f), imag(32 - f)
         add[f], sub[f] = a + b, a - b
-    for t in (1, 3, 5, 7):
-        odd[t] = weighted([(sine(f, t), add[f]) for f in range(1, 17)])
+    base = {f: add[f] * sine(f, 1) for f in range(1, 17)}
+    base[0] = None
+    odd[1], odd[3], odd[5], odd[7] = odd_multiples(base, 1)
     sums = {f: sub[f] + sub[16 - f] for f in range(1, 8)}
     sums[8] = sub[8]
     for t in (2, 6):
@@ -267,48 +323,6 @@
         ),
         name="correlate",
     )(place, own, mate)
-
-
-def plan_kernel(partners_ref, mate_ref, back_ref, flip_ref):
-    rounds, blocks = partners_ref.shape
-    for task in range(rounds // 2):
-        first, second = 2 * task, 2 * task + 1
-
-        def clear(block, carry):
-            flip_ref[task, block] = -1
-            return carry
-
-        def walk(block):
-            partner = partners_ref[first, block]
-            flip_ref[task, block] = 0
-            flip_ref[task, partner] = 1
-            mate_ref[task, block] = partner
-            back_ref[task, partner] = block
-            following = partners_ref[second, partner]
-            mate_ref[task, partner] = following
-            back_ref[task, following] = partner
-            return following
-
-        def start(block, carry):
-            lax.while_loop(lambda block: flip_ref[task, block] < 0, walk, block)
-            return carry
-
-        lax.fori_loop(0, blocks, clear, 0)
-        lax.fori_loop(0, blocks, start, 0)
-
-
-def plan(partners):
-    rounds, blocks = partners.shape
-    smem = pl.BlockSpec(memory_space=pltpu.SMEM)
-    table = jax.ShapeDtypeStruct((rounds // 2, blocks), jnp.int32)
-    return pl.pallas_call(
-        plan_kernel,
-        out_shape=[table] * 3,
-        in_specs=[smem],
-        out_specs=[smem] * 3,
-        compiler_params=params(),
-        name="plan",
-    )(partners)
 
 
 def core_sum_kernel(task, place_ref, keep_ref, recv_ref, *refs):
@@ -512,11 +526,10 @@
     num_blocks = lax.axis_size("pair")
 
     own = whiten(spectra, channel_order).reshape(num_bins, 2 * num_windows, cols)
-    own_turned = turn(own)
-    mate_of, back_of, flip = plan(partners)
     shares = exchange(own)
-    arranged = gather(shares, mate_of)
-    mates = [exchange(after(arranged[0], own_turned)), exchange(arranged[1])]
+    arranged, back_of, flip = gather(shares, partners)
+    mates = [exchange(block) for block in arranged]
+    own_turned = turn(after(own, mates[0]))
     groups = [
         [(block * 2 + chip_index) * 2 + core_index for chip_index in range(2) for block in range(num_blocks)]
         for core_index in range(2)
@@ -533,9 +546,8 @@
             moved = [rows[task][1]]
     out = own_rows(place, flip, 0, *rows[0], None)
     spread = lax.all_to_all(
-        pieces, ("pair", "win"), 0, 0, tiled=True, axis_index_groups=groups
+        after(pieces, out), ("pair", "win"), 0, 0, tiled=True, axis_index_groups=groups
     )
-    spread = after(spread, out)
     row_recv = lax.ppermute(row_send, "win", other_chip)
     returned = exchange(gather_sum(back_of, spread))
     out = own_rows(place, flip, 1, own_sum, row_recv, out)

time: 258 us -> 252 us (0.977)
  blocking collectives: 46.2 us -> 135 us
  waiting for transfers between devices: 105 us -> 38.3 us
  starting transfers between devices: 40.2 us -> 16.7 us
  Pallas kernels: 62.2 us -> 59 us
    all_to_all x1 -> x2, blocking collectives: 46.2 us -> 95.7 us  [exchange(): lax.all_to_all(array, 'pair', split_axis=0, concat_axis=0, tiled=True)]
    all_to_all x0 -> x1, blocking collectives: none -> 39.5 us  [local(): lax.all_to_all(after(pieces, out), ('pair', 'win'), 0, 0, tiled=True, axi...]
    all_to_all x3 -> x2, waiting for transfers between devices: 66.7 us -> 28.6 us  [exchange(): lax.all_to_all(array, 'pair', split_axis=0, concat_axis=0, tiled=True)]
    all_to_all x1 -> x0, waiting for transfers between devices: 25.1 us -> none  [local(): lax.all_to_all(pieces, ('pair', 'win'), 0, 0, tiled=True, axis_index_grou...]
    all_to_all x1 -> x0, starting transfers between devices: 11.7 us -> none  [local(): lax.all_to_all(pieces, ('pair', 'win'), 0, 0, tiled=True, axis_index_grou...]
    all_to_all x3 -> x2, starting transfers between devices: 23.9 us -> 13 us  [exchange(): lax.all_to_all(array, 'pair', split_axis=0, concat_axis=0, tiled=True)]
    pallas_call x1 -> x0, Pallas kernels: 3.32 us -> none  [plan(): pl.pallas_call(plan_kernel, out_shape=[table] * 3, in_specs=[smem], out_s...]
    ppermute x2, waiting for transfers between devices: 5.9 us -> 3.08 us  [local(): recv = lax.ppermute(after(send, *moved), 'win', other_core)]
  transfers between devices with their start and end apart: 9 -> 7, of which waited for: 7 -> 4; matrix products, arithmetic and copies ran while one was open for 0% -> 0% of each run, Pallas kernels for 16% -> 15%
where the time goes in v7:
time: 252 us; the launch traced here: 251 us
  blocking collectives  135 us (54%)
  Pallas kernels  59 us (23%)
  waiting for transfers between devices  38.3 us (15%)
  starting transfers between devices  16.7 us (7%)
    all_to_all x2, blocking collectives, exchange(): lax.all_to_all(array, 'pair', split_axis=0, concat_axis=0, tiled=True)  95.7 us
    all_to_all x1, blocking collectives, local(): lax.all_to_all(after(pieces, out), ('pair', 'win'), 0, 0, tiled=True, axi...  39.5 us
    all_to_all x2, waiting for transfers between devices, exchange(): lax.all_to_all(array, 'pair', split_axis=0, concat_axis=0, tiled=True)  28.6 us
    pallas_call x2, Pallas kernels, correlate(): pl.pallas_call(functools.partial(correlate_kernel, norm), out_shape=[jax....  22.1 us
    all_to_all x2, starting transfers between devices, exchange(): lax.all_to_all(array, 'pair', split_axis=0, concat_axis=0, tiled=True)  13 us
    pallas_call x2, Pallas kernels, core_sum(): pl.pallas_call(functools.partial(core_sum_kernel, task), out_shape=[jax.S...  7.71 us
    ppermute x1, waiting for transfers between devices, local(): row_recv = lax.ppermute(row_send, 'win', other_chip)  6.56 us
    pallas_call x2, Pallas kernels, own_rows(): pl.pallas_call(own_rows_kernel, out_shape=jax.ShapeDtypeStruct((rows, ROU...  6.53 us
  transfers between devices with their start and end apart: 7, of which 4 were waited for; matrix products, arithmetic and copies ran while one was open for 0% of the time, Pallas kernels for 15%

profile of v7, /device:TPU:16, one launch (start us, length us, event | category | flops | bytes accessed | tf_op | source)
XLA Modules:
  0.0 251.5 jit_solution(15705303578560786171)
XLA Ops:
  0.0 5.0 %whiten.1 = bf16[32,2,96,256]{3,2,1,0:T(8,128)(2,1)} custom-call(s32[1,256]{1,0:T(1,128)} %order_ref.1, bf16[32,2,96,256]{3,2,1,0:T(8,128)(2,1)} %spectra_ref.1), custom_call_target="tpu_custom_call" | custom-call | tf_op jit(solution)/shard_map/whiten/pallas_call | solution.py:45
  5.0 49.9 %all_to_all.25.source_ref = bf16[32,192,256]{2,1,0:T(8,128)(2,1)} all-to-all(bf16[32,192,256]{2,1,0:T(8,128)(2,1)} %bitcast.5), channel_id=1, replica_groups=mesh['pair'=32,'win'=4] {'pair'}, dimensions={0} | all-to-all | bytes 6291456 | tf_op jit(solution)/shard_map/all_to_all | solution.py:510
  54.9 6.2 %gather.1 = (bf16[32,192,256]{2,1,0:T(8,128)(2,1)}, bf16[32,192,256]{2,1,0:T(8,128)(2,1)}, s32[2,32]{1,0:T(2,128)}, s32[2,32]{1,0:T(2,128)}, s32[2,32]{1,0:T(2,128)}) custom-call(s32[4,32]{1,0:T(4,128)} %partners_ref.1, bf16[32,192,256]{2,1,0:T(8,128)(2,1)} %all_to_all.25.source_ref), custom_call_target="tpu_custom_call" | custom-call | tf_op jit(solution)/shard_map/gather/pallas_call | solution.py:144
  61.1 45.7 %all_to_all.26.mate_ref = bf16[32,192,256]{2,1,0:T(8,128)(2,1)} all-to-all(bf16[32,192,256]{2,1,0:T(8,128)(2,1)} %get-tuple-element.25), channel_id=1, replica_groups=mesh['pair'=32,'win'=4] {'pair'}, dimensions={0} | all-to-all | bytes 6291456 | tf_op jit(solution)/shard_map/all_to_all | solution.py:510
  106.9 7.1 %all-to-all-start.2 = ((bf16[32,192,256]{2,1,0:T(8,128)(2,1)}), bf16[32,192,256]{2,1,0:T(8,128)(2,1)}, u32[]{:S(2)}, u32[]{:S(2)}) async-start(bf16[32,192,256]{2,1,0:T(8,128)(2,1)} %get-tuple-element.27), calls=%async_computation.2 | async-start | bytes 6291456 | tf_op jit(solution)/shard_map/all_to_all | solution.py:510
  114.0 0.6 pad_add_fusion.place_ref
  114.6 5.0 %turn.1.own_ref = bf16[32,256,192]{2,1,0:T(8,128)(2,1)} custom-call(bf16[32,192,256]{2,1,0:T(8,128)(2,1)} %bitcast.6), custom_call_target="tpu_custom_call" | custom-call | bytes 12000000 | tf_op jit(solution)/shard_map/turn/pallas_call | solution.py:73
  119.6 11.1 %correlate.2 = (f32[17,128,256]{2,1,0:T(8,128)}, bf16[17,128,256]{2,1,0:T(8,128)(2,1)}) custom-call(s32[3]{0:T(128)} %pad_add_fusion.place_ref, bf16[32,256,192]{2,1,0:T(8,128)(2,1)} %turn.1.own_ref, bf16[32,192,256]{2,1,0:T(8,128)(2,1)} %all_to_all.26.mate_ref), custom_call_target="tpu_custom_call" | custom-call | flops 1610612736 | bytes 20000000 | tf_op jit(solution)/shard_map/correlate/pallas_call | solution.py:305
  130.7 0.1 collective-permute-start
  130.8 3.1 %collective-permute-done.recv_ref = bf16[17,128,256]{2,1,0:T(8,128)(2,1)} collective-permute-done((bf16[17,128,256]{2,1,0:T(8,128)(2,1)}, bf16[17,128,256]{2,1,0:T(8,128)(2,1)}, u32[]{:S(2)}, u32[]{:S(2)}) %collective-permute-start) | collective-permute-done | bytes 1114144 | tf_op jit(solution)/shard_map/ppermute | solution.py:540
  133.8 3.8 %core_sum.2 = (f32[16,64,256]{2,1,0:T(8,128)}, bf16[16,64,256]{2,1,0:T(8,128)(2,1)}, bf16[64,2,64,128]{3,2,1,0:T(8,128)(2,1)}) custom-call(s32[3]{0:T(128)} %pad_add_fusion.place_ref, f32[17,128,256]{2,1,0:T(8,128)} %get-tuple-element.28.keep_ref, bf16[17,128,256]{2,1,0:T(8,128)(2,1)} %collective-permute-done.recv_ref), custom_call_target="tpu_custom_call" | custom-call | bytes 12000000 | tf_op jit(solution)/shard_map/core_sum/pallas_call | solution.py:388
  137.6 1.5 collective-permute-start.1
  139.2 14.4 %all-to-all-done.2.mate_ref = bf16[32,192,256]{2,1,0:T(8,128)(2,1)} async-done(((bf16[32,192,256]{2,1,0:T(8,128)(2,1)}), bf16[32,192,256]{2,1,0:T(8,128)(2,1)}, u32[]{:S(2)}, u32[]{:S(2)}) %all-to-all-start.2) | async-done | bytes 3145760 | tf_op jit(solution)/shard_map/all_to_all | solution.py:510
  153.5 11.0 %correlate.3 = (f32[17,128,256]{2,1,0:T(8,128)}, bf16[17,128,256]{2,1,0:T(8,128)(2,1)}) custom-call(s32[3]{0:T(128)} %pad_add_fusion.place_ref, bf16[32,256,192]{2,1,0:T(8,128)(2,1)} %turn.1.own_ref, bf16[32,192,256]{2,1,0:T(8,128)(2,1)} %all-to-all-done.2.mate_ref), custom_call_target="tpu_custom_call" | custom-call | flops 1610612736 | bytes 20000000 | tf_op jit(solution)/shard_map/correlate/pallas_call | solution.py:305
  164.6 0.0 collective-permute-done.1.recv_ref
  164.6 0.0 copy-start.1
  164.6 0.3 collective-permute-start.2
  164.9 0.5 copy-done.1
  165.4 3.3 %own_rows.2.refs_0_ = f32[64,4,16,256]{3,2,1,0:T(8,128)} custom-call(s32[2,32]{1,0:T(2,128)} %get-tuple-element.23.flip_ref, s32[3]{0:T(128)} %pad_add_fusion.place_ref, f32[16,64,256]{2,1,0:T(8,128)} %get-tuple-element.37.own_ref, bf16[16,64,256]{2,1,0:T(8,128)(2,1)} %copy-done.1), custom_call_target="tpu_custom_call" | custom-call | bytes 5000000 | tf_op jit(solution)/shard_map/own_rows/pallas_call | solution.py:452
  168.7 0.0 collective-permute-done.2.recv_ref
  168.7 3.9 %core_sum.3 = (f32[16,64,256]{2,1,0:T(8,128)}, bf16[16,64,256]{2,1,0:T(8,128)(2,1)}, bf16[64,2,64,128]{3,2,1,0:T(8,128)(2,1)}) custom-call(s32[3]{0:T(128)} %pad_add_fusion.place_ref, f32[17,128,256]{2,1,0:T(8,128)} %get-tuple-element.32.keep_ref, bf16[17,128,256]{2,1,0:T(8,128)(2,1)} %collective-permute-done.2.recv_ref, ...), custom_call_target="tpu_custom_call", output_to_operand_aliasing={{2}: (3, {})} | custom-call | bytes 12000000 | tf_op jit(solution)/shard_map/core_sum/pallas_call | solution.py:388
  172.6 39.5 %all_to_all.27.spread_ref = bf16[64,2,64,128]{3,2,1,0:T(8,128)(2,1)} all-to-all(bf16[64,2,64,128]{3,2,1,0:T(8,128)(2,1)} %get-tuple-element.38), channel_id=1, replica_groups={{0,4,8,12,16,20,24,28,32,36,40,44,48,52,56,60,64,68,72,76,80,84,88,92,9..., dimensions={0} | all-to-all | bytes 4194304 | tf_op jit(solution)/shard_map/all_to_all | solution.py:548
  212.1 2.9 %gather_sum.1 = bf16[32,2,64,128]{3,2,1,0:T(8,128)(2,1)} custom-call(s32[2,32]{1,0:T(2,128)} %get-tuple-element.24.index_ref, bf16[64,2,64,128]{3,2,1,0:T(8,128)(2,1)} %all_to_all.27.spread_ref), custom_call_target="tpu_custom_call" | custom-call | tf_op jit(solution)/shard_map/gather_sum/pallas_call | solution.py:432
  215.0 5.8 %all-to-all-start.4 = ((bf16[32,2,64,128]{3,2,1,0:T(8,128)(2,1)}), bf16[32,2,64,128]{3,2,1,0:T(8,128)(2,1)S(1)}, u32[]{:S(2)}, u32[]{:S(2)}) async-start(bf16[32,2,64,128]{3,2,1,0:T(8,128)(2,1)} %gather_sum.1), calls=%async_computation.4 | async-start | bytes 2097152 | tf_op jit(solution)/shard_map/all_to_all | solution.py:510
  220.8 1.8 collective-permute-start.4
  222.6 14.3 %all-to-all-done.4.near_ref = bf16[32,2,64,128]{3,2,1,0:T(8,128)(2,1)S(1)} async-done(((bf16[32,2,64,128]{3,2,1,0:T(8,128)(2,1)}), bf16[32,2,64,128]{3,2,1,0:T(8,128)(2,1)S(1)}, u32[]{:S(2)}, u32[]{:S(2)}) %all-to-all-start.4) | async-done | bytes 1048608 | tf_op jit(solution)/shard_map/all_to_all | solution.py:510
  236.9 0.0 copy-start
  236.9 1.0 copy-done
  237.9 0.1 collective-permute-start.3
  238.0 6.6 %collective-permute-done.4.recv_ref = bf16[16,64,256]{2,1,0:T(8,128)(2,1)} collective-permute-done((bf16[16,64,256]{2,1,0:T(8,128)(2,1)}, bf16[16,64,256]{2,1,0:T(8,128)(2,1)}, u32[]{:S(2)}, u32[]{:S(2)}) %collective-permute-start.4) | collective-permute-done | bytes 524320 | tf_op jit(solution)/shard_map/ppermute | solution.py:551
  244.6 3.3 %own_rows.3.in_ref = f32[64,4,16,256]{3,2,1,0:T(8,128)} custom-call(s32[2,32]{1,0:T(2,128)} %get-tuple-element.23.flip_ref, s32[3]{0:T(128)} %pad_add_fusion.place_ref, f32[16,64,256]{2,1,0:T(8,128)} %get-tuple-element.39.own_ref, bf16[16,64,256]{2,1,0:T(8,128)(2,1)} %collective-permute-done.4.recv_ref, ...), custom_call_target="tpu_custom_call", output_to_operand_aliasing={{}: (4, {})} | custom-call | bytes 5000000 | tf_op jit(solution)/shard_map/own_rows/pallas_call | solution.py:452
  247.9 0.0 collective-permute-done.3.far_ref
  247.9 3.6 %mirrored_rows.1 = f32[64,4,16,256]{3,2,1,0:T(8,128)} custom-call(s32[2,32]{1,0:T(2,128)} %get-tuple-element.23.flip_ref, s32[3]{0:T(128)} %pad_add_fusion.place_ref, bf16[32,2,64,128]{3,2,1,0:T(8,128)(2,1)} %copy-done, bf16[16,2,64,128]{3,2,1,0:T(8,128)(2,1)} %collective-permute-done.3.far_ref, ...), custom_call_target="tpu_custom_call", output_to_operand_aliasing={{}: (4, {})} | custom-call | tf_op jit(solution)/shard_map/mirrored_rows/pallas_call | solution.py:491
  (1 shorter events, 0.0 us)
Async XLA Ops:
  106.9 46.7 %all-to-all-start.2 = ((bf16[32,192,256]{2,1,0:T(8,128)(2,1)}), bf16[32,192,256]{2,1,0:T(8,128)(2,1)}, u32[]{:S(2)}, u32[]{:S(2)}) async-start(bf16[32,192,256]{2,1,0:T(8,128)(2,1)} %get-tuple-element.27), calls=%async_computation.2 | async-start | bytes 6291456 | tf_op jit(solution)/shard_map/all_to_all | solution.py:510
  130.7 3.2 %collective-permute-start = (bf16[17,128,256]{2,1,0:T(8,128)(2,1)}, bf16[17,128,256]{2,1,0:T(8,128)(2,1)}, u32[]{:S(2)}, u32[]{:S(2)}) collective-permute-start(bf16[17,128,256]{2,1,0:T(8,128)(2,1)} %get-tuple-element.29), channel_id=1, source_target_pairs={{0,1},{1,0},{2,3},{3,2},{4,5},{5,4},{6,7},{7,6},{8,9},{9,8},{10,11... | collective-permute-start | bytes 3342344 | tf_op jit(solution)/shard_map/ppermute | solution.py:540
  137.6 26.9 %collective-permute-start.1 = (bf16[16,64,256]{2,1,0:T(8,128)(2,1)}, bf16[16,64,256]{2,1,0:T(8,128)(2,1)S(1)}, u32[]{:S(2)}, u32[]{:S(2)}) collective-permute-start(bf16[16,64,256]{2,1,0:T(8,128)(2,1)} %get-tuple-element.30), channel_id=1, source_target_pairs={{0,2},{1,3},{2,0},{3,1},{4,6},{5,7},{6,4},{7,5},{8,10},{9,11},{10,... | collective-permute-start | bytes 1572872 | tf_op jit(solution)/shard_map/ppermute | solution.py:545
  164.6 0.8 copy-start.1
  164.6 4.1 %collective-permute-start.2 = (bf16[17,128,256]{2,1,0:T(8,128)(2,1)}, bf16[17,128,256]{2,1,0:T(8,128)(2,1)}, u32[]{:S(2)}, u32[]{:S(2)}) collective-permute-start(bf16[17,128,256]{2,1,0:T(8,128)(2,1)} %get-tuple-element.34), channel_id=1, source_target_pairs={{0,1},{1,0},{2,3},{3,2},{4,5},{5,4},{6,7},{7,6},{8,9},{9,8},{10,11... | collective-permute-start | bytes 3342344 | tf_op jit(solution)/shard_map/ppermute | solution.py:540
  215.0 21.9 %all-to-all-start.4 = ((bf16[32,2,64,128]{3,2,1,0:T(8,128)(2,1)}), bf16[32,2,64,128]{3,2,1,0:T(8,128)(2,1)S(1)}, u32[]{:S(2)}, u32[]{:S(2)}) async-start(bf16[32,2,64,128]{3,2,1,0:T(8,128)(2,1)} %gather_sum.1), calls=%async_computation.4 | async-start | bytes 2097152 | tf_op jit(solution)/shard_map/all_to_all | solution.py:510
  220.8 23.8 %collective-permute-start.4 = (bf16[16,64,256]{2,1,0:T(8,128)(2,1)}, bf16[16,64,256]{2,1,0:T(8,128)(2,1)}, u32[]{:S(2)}, u32[]{:S(2)}) collective-permute-start(bf16[16,64,256]{2,1,0:T(8,128)(2,1)} %get-tuple-element.40), channel_id=1, source_target_pairs={{0,2},{1,3},{2,0},{3,1},{4,6},{5,7},{6,4},{7,5},{8,10},{9,11},{10,... | collective-permute-start | bytes 1572872 | tf_op jit(solution)/shard_map/ppermute | solution.py:551
  236.9 1.0 copy-start
  237.9 9.9 %collective-permute-start.3 = (bf16[16,2,64,128]{3,2,1,0:T(8,128)(2,1)S(1)}, bf16[16,2,64,128]{3,2,1,0:T(8,128)(2,1)}, u32[]{:S(2)}, u32[]{:S(2)}) collective-permute-start(bf16[16,2,64,128]{3,2,1,0:T(8,128)(2,1)S(1)} %slice.4), channel_id=1, source_target_pairs={{0,1},{1,0},{2,3},{3,2},{4,5},{5,4},{6,7},{7,6},{8,9},{9,8},{10,11... | collective-permute-start | bytes 1572872 | tf_op jit(solution)/shard_map/ppermute | solution.py:554

commit v8 on v7

--- a/solution.py
+++ b/solution.py
@@ -412,28 +412,31 @@
 
 
 def gather_sum_kernel(index_ref, spread_ref, out_ref):
-    places, tasks = out_ref.shape[:2]
+    places = out_ref.shape[0]
+    task = pl.program_id(0)
 
     def body(place, carry):
-        for task in range(tasks):
-            source = index_ref[task, place]
-            out_ref[place, task] = (
-                spread_ref[source, task].astype(f32)
-                + spread_ref[places + source, task].astype(f32)
-            ).astype(bf16)
+        source = index_ref[task, place]
+        out_ref[place, 0] = (
+            spread_ref[source, 0].astype(f32) + spread_ref[places + source, 0].astype(f32)
+        ).astype(bf16)
         return carry
 
-    lax.fori_loop(0, places, body, 0, unroll=4)
+    lax.fori_loop(0, places, body, 0, unroll=8)
 
 
 def gather_sum(index, spread):
-    places = index.shape[1]
-    vmem = pl.BlockSpec(memory_space=pltpu.VMEM)
+    tasks, places = index.shape
+    pieces, piece = spread.shape[0], spread.shape[2:]
     return pl.pallas_call(
         gather_sum_kernel,
-        out_shape=jax.ShapeDtypeStruct((places,) + spread.shape[1:], bf16),
-        in_specs=[pl.BlockSpec(memory_space=pltpu.SMEM), vmem],
-        out_specs=vmem,
+        grid=(tasks,),
+        out_shape=jax.ShapeDtypeStruct((places, tasks) + piece, bf16),
+        in_specs=[
+            pl.BlockSpec(memory_space=pltpu.SMEM),
+            pl.BlockSpec((pieces, 1) + piece, lambda t: (0, t, 0, 0)),
+        ],
+        out_specs=pl.BlockSpec((places, 1) + piece, lambda t: (0, t, 0, 0)),
         compiler_params=params(),
         name="gather_sum",
     )(index, spread)
@@ -468,42 +471,57 @@
     )(flip, place, own, recv, *extra)
 
 
-def mirrored_rows_kernel(flip_ref, place_ref, near_ref, far_ref, in_ref, out_ref):
-    core = place_ref[0]
-    near = near_ref[:, 0].astype(f32)
-    far = far_ref[:, 0].astype(f32)
-    first = jnp.where(core == 0, near, far)
-    second = jnp.where(core == 0, far, near)
-    lanes = first.shape[2]
-    lane = lax.broadcasted_iota(jnp.int32, first.shape, 2)
-    quarter = lanes // 2
-    low = jnp.where(lane < quarter, first, pltpu.roll(second, quarter, 2))
-    high = jnp.where(lane < quarter, pltpu.roll(first, quarter, 2), second)
-    out_ref[:, 0, :, :lanes] = jnp.swapaxes(low, 0, 1)
-    out_ref[:, 0, :, lanes:] = jnp.swapaxes(high, 0, 1)
-
-
-def mirrored_rows(place, flip, near, far, out):
+def last_rows_kernel(flip_ref, place_ref, own_ref, recv_ref, near_ref, far_ref, in_ref, out_ref):
+    step = pl.program_id(0)
+
+    @pl.when(step == 0)
+    def _():
+        out_ref[:, 0] = jnp.swapaxes(own_ref[...] + recv_ref[...].astype(f32), 0, 1)
+
+    @pl.when(step > 0)
+    def _():
+        core = place_ref[0]
+        near = near_ref[:, 0].astype(f32)
+        far = far_ref[:, 0].astype(f32)
+        first = jnp.where(core == 0, near, far)
+        second = jnp.where(core == 0, far, near)
+        lanes = first.shape[2]
+        lane = lax.broadcasted_iota(jnp.int32, first.shape, 2)
+        quarter = lanes // 2
+        low = jnp.where(lane < quarter, first, pltpu.roll(second, quarter, 2))
+        high = jnp.where(lane < quarter, pltpu.roll(first, quarter, 2), second)
+        out_ref[:, 0, :, :lanes] = jnp.swapaxes(low, 0, 1)
+        out_ref[:, 0, :, lanes:] = jnp.swapaxes(high, 0, 1)
+
+
+def last_rows(place, flip, own, recv, near, far, out):
     rows, _, lags, cols = out.shape
     tasks = near.shape[1]
-    step = 64
-    back = pl.BlockSpec((lags, 1, step, near.shape[3]), lambda t, s, flip, place: (0, t, s, 0))
-    return pl.pallas_call(
-        mirrored_rows_kernel,
+    whole = pl.BlockSpec((lags, rows, cols), lambda s, flip, place: (0, 0, 0))
+    back = pl.BlockSpec(
+        (lags, 1, rows, near.shape[3]),
+        lambda s, flip, place: (0, jnp.maximum(s - 1, 0), 0, 0),
+    )
+
+    def target(s, flip, place):
+        task = jnp.maximum(s - 1, 0)
+        block = place[2]
+        mirrored = 2 * task + 1 - flip[task, block]
+        return (0, jnp.where(s == 0, 2 * (tasks - 1) + flip[tasks - 1, block], mirrored), 0, 0)
+
+    return pl.pallas_call(
+        last_rows_kernel,
         out_shape=jax.ShapeDtypeStruct(out.shape, f32),
         grid_spec=pltpu.PrefetchScalarGridSpec(
             num_scalar_prefetch=2,
-            grid=(tasks, rows // step),
-            in_specs=[back, back, pl.BlockSpec(memory_space=pl.ANY)],
-            out_specs=pl.BlockSpec(
-                (step, 1, lags, cols),
-                lambda t, s, flip, place: (s, 2 * t + 1 - flip[t, place[2]], 0, 0),
-            ),
+            grid=(tasks + 1,),
+            in_specs=[whole, whole, back, back, pl.BlockSpec(memory_space=pl.ANY)],
+            out_specs=pl.BlockSpec((rows, 1, lags, cols), target),
         ),
-        input_output_aliases={4: 0},
-        compiler_params=params(),
-        name="mirrored_rows",
-    )(flip, place, near, far, out)
+        input_output_aliases={6: 0},
+        compiler_params=params(),
+        name="last_rows",
+    )(flip, place, own, recv, near, far, out)
 
 
 def exchange(array):
@@ -550,9 +568,8 @@
     )
     row_recv = lax.ppermute(row_send, "win", other_chip)
     returned = exchange(gather_sum(back_of, spread))
-    out = own_rows(place, flip, 1, own_sum, row_recv, out)
     far = lax.ppermute(returned[LAGS:], "win", other_core)
-    return mirrored_rows(place, flip, returned, far, out)[None]
+    return last_rows(place, flip, own_sum, row_recv, returned, far, out)[None]
 
 
 def solution(mesh):

time: 252 us -> 251 us (level)
    pallas_call x2 -> x1, Pallas kernels: 6.53 us -> 3.27 us  [own_rows(): pl.pallas_call(own_rows_kernel, out_shape=jax.ShapeDtypeStruct((rows, ROU...]
  transfers between devices with their start and end apart: 7 -> 7, of which waited for: 4 -> 4; matrix products, arithmetic and copies ran while one was open for 0% -> 0% of each run, Pallas kernels for 15% -> 14%
where the time goes in v8:
time: 251 us; the launch traced here: 250 us
  blocking collectives  135 us (54%)
  Pallas kernels  57.3 us (23%)
  waiting for transfers between devices  38 us (15%)
  starting transfers between devices  16.8 us (7%)
    all_to_all x2, blocking collectives, exchange(): lax.all_to_all(array, 'pair', split_axis=0, concat_axis=0, tiled=True)  95.7 us
    all_to_all x1, blocking collectives, local(): lax.all_to_all(after(pieces, out), ('pair', 'win'), 0, 0, tiled=True, axi...  39.5 us
    all_to_all x2, waiting for transfers between devices, exchange(): lax.all_to_all(array, 'pair', split_axis=0, concat_axis=0, tiled=True)  28.5 us
    pallas_call x2, Pallas kernels, correlate(): pl.pallas_call(functools.partial(correlate_kernel, norm), out_shape=[jax....  22.2 us
    all_to_all x2, starting transfers between devices, exchange(): lax.all_to_all(array, 'pair', split_axis=0, concat_axis=0, tiled=True)  13 us
    pallas_call x2, Pallas kernels, core_sum(): pl.pallas_call(functools.partial(core_sum_kernel, task), out_shape=[jax.S...  7.67 us
    ppermute x1, waiting for transfers between devices, local(): row_recv = lax.ppermute(row_send, 'win', other_chip)  6.42 us
    pallas_call x1, Pallas kernels, gather(): pl.pallas_call(gather_kernel, out_shape=[jax.ShapeDtypeStruct(source.shap...  6.22 us
  transfers between devices with their start and end apart: 7, of which 4 were waited for; matrix products, arithmetic and copies ran while one was open for 0% of the time, Pallas kernels for 14%

profile of v8, /device:TPU:16, one launch (start us, length us, event | category | flops | bytes accessed | tf_op | source)
XLA Modules:
  0.0 250.4 jit_solution(16480080251298099382)
XLA Ops:
  0.0 5.0 %whiten.1 = bf16[32,2,96,256]{3,2,1,0:T(8,128)(2,1)} custom-call(s32[1,256]{1,0:T(1,128)} %order_ref.1, bf16[32,2,96,256]{3,2,1,0:T(8,128)(2,1)} %spectra_ref.1), custom_call_target="tpu_custom_call" | custom-call | tf_op jit(solution)/shard_map/whiten/pallas_call | solution.py:45
  5.0 49.9 %all_to_all.25.source_ref = bf16[32,192,256]{2,1,0:T(8,128)(2,1)} all-to-all(bf16[32,192,256]{2,1,0:T(8,128)(2,1)} %bitcast.5), channel_id=1, replica_groups=mesh['pair'=32,'win'=4] {'pair'}, dimensions={0} | all-to-all | bytes 6291456 | tf_op jit(solution)/shard_map/all_to_all | solution.py:528
  55.0 6.2 %gather.1 = (bf16[32,192,256]{2,1,0:T(8,128)(2,1)}, bf16[32,192,256]{2,1,0:T(8,128)(2,1)}, s32[2,32]{1,0:T(2,128)}, s32[2,32]{1,0:T(2,128)}, s32[2,32]{1,0:T(2,128)}) custom-call(s32[4,32]{1,0:T(4,128)} %partners_ref.1, bf16[32,192,256]{2,1,0:T(8,128)(2,1)} %all_to_all.25.source_ref), custom_call_target="tpu_custom_call" | custom-call | tf_op jit(solution)/shard_map/gather/pallas_call | solution.py:144
  61.2 45.7 %all_to_all.26.mate_ref = bf16[32,192,256]{2,1,0:T(8,128)(2,1)} all-to-all(bf16[32,192,256]{2,1,0:T(8,128)(2,1)} %get-tuple-element.24), channel_id=1, replica_groups=mesh['pair'=32,'win'=4] {'pair'}, dimensions={0} | all-to-all | bytes 6291456 | tf_op jit(solution)/shard_map/all_to_all | solution.py:528
  106.9 7.2 %all-to-all-start.2 = ((bf16[32,192,256]{2,1,0:T(8,128)(2,1)}), bf16[32,192,256]{2,1,0:T(8,128)(2,1)}, u32[]{:S(2)}, u32[]{:S(2)}) async-start(bf16[32,192,256]{2,1,0:T(8,128)(2,1)} %get-tuple-element.26), calls=%async_computation.2 | async-start | bytes 6291456 | tf_op jit(solution)/shard_map/all_to_all | solution.py:528
  114.1 0.7 pad_add_fusion.place_ref
  114.8 5.0 %turn.1.own_ref = bf16[32,256,192]{2,1,0:T(8,128)(2,1)} custom-call(bf16[32,192,256]{2,1,0:T(8,128)(2,1)} %bitcast.6), custom_call_target="tpu_custom_call" | custom-call | bytes 12000000 | tf_op jit(solution)/shard_map/turn/pallas_call | solution.py:73
  119.7 11.1 %correlate.2 = (f32[17,128,256]{2,1,0:T(8,128)}, bf16[17,128,256]{2,1,0:T(8,128)(2,1)}) custom-call(s32[3]{0:T(128)} %pad_add_fusion.place_ref, bf16[32,256,192]{2,1,0:T(8,128)(2,1)} %turn.1.own_ref, bf16[32,192,256]{2,1,0:T(8,128)(2,1)} %all_to_all.26.mate_ref), custom_call_target="tpu_custom_call" | custom-call | flops 1610612736 | bytes 20000000 | tf_op jit(solution)/shard_map/correlate/pallas_call | solution.py:305
  130.8 0.1 collective-permute-start
  130.9 3.1 %collective-permute-done.recv_ref = bf16[17,128,256]{2,1,0:T(8,128)(2,1)} collective-permute-done((bf16[17,128,256]{2,1,0:T(8,128)(2,1)}, bf16[17,128,256]{2,1,0:T(8,128)(2,1)}, u32[]{:S(2)}, u32[]{:S(2)}) %collective-permute-start) | collective-permute-done | bytes 1114144 | tf_op jit(solution)/shard_map/ppermute | solution.py:558
  134.0 3.8 %core_sum.2 = (f32[16,64,256]{2,1,0:T(8,128)}, bf16[16,64,256]{2,1,0:T(8,128)(2,1)}, bf16[64,2,64,128]{3,2,1,0:T(8,128)(2,1)}) custom-call(s32[3]{0:T(128)} %pad_add_fusion.place_ref, f32[17,128,256]{2,1,0:T(8,128)} %get-tuple-element.27.keep_ref, bf16[17,128,256]{2,1,0:T(8,128)(2,1)} %collective-permute-done.recv_ref), custom_call_target="tpu_custom_call" | custom-call | bytes 12000000 | tf_op jit(solution)/shard_map/core_sum/pallas_call | solution.py:388
  137.8 1.5 collective-permute-start.1
  139.4 14.2 %all-to-all-done.2.mate_ref = bf16[32,192,256]{2,1,0:T(8,128)(2,1)} async-done(((bf16[32,192,256]{2,1,0:T(8,128)(2,1)}), bf16[32,192,256]{2,1,0:T(8,128)(2,1)}, u32[]{:S(2)}, u32[]{:S(2)}) %all-to-all-start.2) | async-done | bytes 3145760 | tf_op jit(solution)/shard_map/all_to_all | solution.py:528
  153.6 11.1 %correlate.3 = (f32[17,128,256]{2,1,0:T(8,128)}, bf16[17,128,256]{2,1,0:T(8,128)(2,1)}) custom-call(s32[3]{0:T(128)} %pad_add_fusion.place_ref, bf16[32,256,192]{2,1,0:T(8,128)(2,1)} %turn.1.own_ref, bf16[32,192,256]{2,1,0:T(8,128)(2,1)} %all-to-all-done.2.mate_ref), custom_call_target="tpu_custom_call" | custom-call | flops 1610612736 | bytes 20000000 | tf_op jit(solution)/shard_map/correlate/pallas_call | solution.py:305
  164.6 0.0 collective-permute-done.1.recv_ref
  164.6 0.0 copy-start.2
  164.6 0.3 collective-permute-start.2
  164.9 0.5 copy-done.2
  165.4 3.3 %own_rows.1.in_ref = f32[64,4,16,256]{3,2,1,0:T(8,128)} custom-call(s32[2,32]{1,0:T(2,128)} %get-tuple-element.23.flip_ref, s32[3]{0:T(128)} %pad_add_fusion.place_ref, f32[16,64,256]{2,1,0:T(8,128)} %get-tuple-element.39.own_ref, bf16[16,64,256]{2,1,0:T(8,128)(2,1)} %copy-done.2), custom_call_target="tpu_custom_call" | custom-call | bytes 5000000 | tf_op jit(solution)/shard_map/own_rows/pallas_call | solution.py:455
  168.7 0.0 collective-permute-done.2.recv_ref
  168.7 3.8 %core_sum.3 = (f32[16,64,256]{2,1,0:T(8,128)}, bf16[16,64,256]{2,1,0:T(8,128)(2,1)}, bf16[64,2,64,128]{3,2,1,0:T(8,128)(2,1)}) custom-call(s32[3]{0:T(128)} %pad_add_fusion.place_ref, f32[17,128,256]{2,1,0:T(8,128)} %get-tuple-element.31.keep_ref, bf16[17,128,256]{2,1,0:T(8,128)(2,1)} %collective-permute-done.2.recv_ref, ...), custom_call_target="tpu_custom_call", output_to_operand_aliasing={{2}: (3, {})} | custom-call | bytes 12000000 | tf_op jit(solution)/shard_map/core_sum/pallas_call | solution.py:388
  172.6 39.5 %all_to_all.27.spread_ref = bf16[64,2,64,128]{3,2,1,0:T(8,128)(2,1)} all-to-all(bf16[64,2,64,128]{3,2,1,0:T(8,128)(2,1)} %get-tuple-element.40), channel_id=1, replica_groups={{0,4,8,12,16,20,24,28,32,36,40,44,48,52,56,60,64,68,72,76,80,84,88,92,9..., dimensions={0} | all-to-all | bytes 4194304 | tf_op jit(solution)/shard_map/all_to_all | solution.py:566
  212.1 2.6 %gather_sum.1 = bf16[32,2,64,128]{3,2,1,0:T(8,128)(2,1)} custom-call(s32[2,32]{1,0:T(2,128)} %get-tuple-element.37.index_ref, bf16[64,2,64,128]{3,2,1,0:T(8,128)(2,1)} %all_to_all.27.spread_ref), custom_call_target="tpu_custom_call" | custom-call | tf_op jit(solution)/shard_map/gather_sum/pallas_call | solution.py:431
  214.7 5.8 %all-to-all-start.4 = ((bf16[32,2,64,128]{3,2,1,0:T(8,128)(2,1)}), bf16[32,2,64,128]{3,2,1,0:T(8,128)(2,1)S(1)}, u32[]{:S(2)}, u32[]{:S(2)}) async-start(bf16[32,2,64,128]{3,2,1,0:T(8,128)(2,1)} %gather_sum.1), calls=%async_computation.4 | async-start | bytes 2097152 | tf_op jit(solution)/shard_map/all_to_all | solution.py:528
  220.5 1.8 collective-permute-start.3
  222.3 14.3 %all-to-all-done.4.near_ref = bf16[32,2,64,128]{3,2,1,0:T(8,128)(2,1)S(1)} async-done(((bf16[32,2,64,128]{3,2,1,0:T(8,128)(2,1)}), bf16[32,2,64,128]{3,2,1,0:T(8,128)(2,1)S(1)}, u32[]{:S(2)}, u32[]{:S(2)}) %all-to-all-start.4) | async-done | bytes 1048608 | tf_op jit(solution)/shard_map/all_to_all | solution.py:528
  236.6 0.0 copy-start
  236.6 1.0 copy-done
  237.6 0.1 collective-permute-start.4
  237.7 6.4 %collective-permute-done.3.recv_ref = bf16[16,64,256]{2,1,0:T(8,128)(2,1)S(1)} collective-permute-done((bf16[16,64,256]{2,1,0:T(8,128)(2,1)}, bf16[16,64,256]{2,1,0:T(8,128)(2,1)S(1)}, u32[]{:S(2)}, u32[]{:S(2)}) %collective-permute-start.3) | collective-permute-done | bytes 524320 | tf_op jit(solution)/shard_map/ppermute | solution.py:569
  244.2 0.0 copy-start.1
  244.2 0.0 collective-permute-done.4.far_ref
  244.2 0.8 copy-done.1
  245.0 5.4 %last_rows.1 = f32[64,4,16,256]{3,2,1,0:T(8,128)} custom-call(s32[2,32]{1,0:T(2,128)} %get-tuple-element.23.flip_ref, s32[3]{0:T(128)} %pad_add_fusion.place_ref, f32[16,64,256]{2,1,0:T(8,128)} %get-tuple-element.35.own_ref, bf16[16,64,256]{2,1,0:T(8,128)(2,1)} %copy-done.1, bf16[32,2,64,128]{3,2,1,0:T(8,128)(2,1)} %copy-done, ...), custom_call_target="tpu_custom_call", output_to_operand_aliasing={{}: (6, {})} | custom-call | tf_op jit(solution)/shard_map/last_rows/pallas_call | solution.py:512
  (1 shorter events, 0.0 us)
Async XLA Ops:
  106.9 46.7 %all-to-all-start.2 = ((bf16[32,192,256]{2,1,0:T(8,128)(2,1)}), bf16[32,192,256]{2,1,0:T(8,128)(2,1)}, u32[]{:S(2)}, u32[]{:S(2)}) async-start(bf16[32,192,256]{2,1,0:T(8,128)(2,1)} %get-tuple-element.26), calls=%async_computation.2 | async-start | bytes 6291456 | tf_op jit(solution)/shard_map/all_to_all | solution.py:528
  130.8 3.2 %collective-permute-start = (bf16[17,128,256]{2,1,0:T(8,128)(2,1)}, bf16[17,128,256]{2,1,0:T(8,128)(2,1)}, u32[]{:S(2)}, u32[]{:S(2)}) collective-permute-start(bf16[17,128,256]{2,1,0:T(8,128)(2,1)} %get-tuple-element.28), channel_id=1, source_target_pairs={{0,1},{1,0},{2,3},{3,2},{4,5},{5,4},{6,7},{7,6},{8,9},{9,8},{10,11... | collective-permute-start | bytes 3342344 | tf_op jit(solution)/shard_map/ppermute | solution.py:558
  137.8 26.8 %collective-permute-start.1 = (bf16[16,64,256]{2,1,0:T(8,128)(2,1)}, bf16[16,64,256]{2,1,0:T(8,128)(2,1)S(1)}, u32[]{:S(2)}, u32[]{:S(2)}) collective-permute-start(bf16[16,64,256]{2,1,0:T(8,128)(2,1)} %get-tuple-element.29), channel_id=1, source_target_pairs={{0,2},{1,3},{2,0},{3,1},{4,6},{5,7},{6,4},{7,5},{8,10},{9,11},{10,... | collective-permute-start | bytes 1572872 | tf_op jit(solution)/shard_map/ppermute | solution.py:563
  164.6 0.8 copy-start.2
  164.6 4.1 %collective-permute-start.2 = (bf16[17,128,256]{2,1,0:T(8,128)(2,1)}, bf16[17,128,256]{2,1,0:T(8,128)(2,1)}, u32[]{:S(2)}, u32[]{:S(2)}) collective-permute-start(bf16[17,128,256]{2,1,0:T(8,128)(2,1)} %get-tuple-element.33), channel_id=1, source_target_pairs={{0,1},{1,0},{2,3},{3,2},{4,5},{5,4},{6,7},{7,6},{8,9},{9,8},{10,11... | collective-permute-start | bytes 3342344 | tf_op jit(solution)/shard_map/ppermute | solution.py:558
  214.7 21.9 %all-to-all-start.4 = ((bf16[32,2,64,128]{3,2,1,0:T(8,128)(2,1)}), bf16[32,2,64,128]{3,2,1,0:T(8,128)(2,1)S(1)}, u32[]{:S(2)}, u32[]{:S(2)}) async-start(bf16[32,2,64,128]{3,2,1,0:T(8,128)(2,1)} %gather_sum.1), calls=%async_computation.4 | async-start | bytes 2097152 | tf_op jit(solution)/shard_map/all_to_all | solution.py:528
  220.5 23.6 %collective-permute-start.3 = (bf16[16,64,256]{2,1,0:T(8,128)(2,1)}, bf16[16,64,256]{2,1,0:T(8,128)(2,1)S(1)}, u32[]{:S(2)}, u32[]{:S(2)}) collective-permute-start(bf16[16,64,256]{2,1,0:T(8,128)(2,1)} %get-tuple-element.36), channel_id=1, source_target_pairs={{0,2},{1,3},{2,0},{3,1},{4,6},{5,7},{6,4},{7,5},{8,10},{9,11},{10,... | collective-permute-start | bytes 1572872 | tf_op jit(solution)/shard_map/ppermute | solution.py:569
  236.6 1.0 copy-start
  237.6 6.5 %collective-permute-start.4 = (bf16[16,2,64,128]{3,2,1,0:T(8,128)(2,1)S(1)}, bf16[16,2,64,128]{3,2,1,0:T(8,128)(2,1)}, u32[]{:S(2)}, u32[]{:S(2)}) collective-permute-start(bf16[16,2,64,128]{3,2,1,0:T(8,128)(2,1)S(1)} %slice.4), channel_id=1, source_target_pairs={{0,1},{1,0},{2,3},{3,2},{4,5},{5,4},{6,7},{7,6},{8,9},{9,8},{10,11... | collective-permute-start | bytes 1572872 | tf_op jit(solution)/shard_map/ppermute | solution.py:571
  244.2 0.8 copy-start.1

commit v9 on v8

--- a/solution.py
+++ b/solution.py
@@ -299,7 +299,7 @@
 def correlate(own, mate, place, norm, lags):
     num_bins, slots, depth = own.shape
     cols = mate.shape[2]
-    chunks = 8
+    chunks = 16
     anywhere = pl.BlockSpec(memory_space=pl.ANY)
     vmem = pl.BlockSpec(memory_space=pltpu.VMEM)
     return pl.pallas_call(
@@ -564,11 +564,11 @@
             moved = [rows[task][1]]
     out = own_rows(place, flip, 0, *rows[0], None)
     spread = lax.all_to_all(
-        after(pieces, out), ("pair", "win"), 0, 0, tiled=True, axis_index_groups=groups
+        pieces, ("pair", "win"), 0, 0, tiled=True, axis_index_groups=groups
     )
     row_recv = lax.ppermute(row_send, "win", other_chip)
     returned = exchange(gather_sum(back_of, spread))
-    far = lax.ppermute(returned[LAGS:], "win", other_core)
+    far = lax.ppermute(after(returned[LAGS:], out), "win", other_core)
     return last_rows(place, flip, own_sum, row_recv, returned, far, out)[None]
 
 

time: 251 us -> 252 us (level)
    all_to_all x2, waiting for transfers between devices: 28.5 us -> 24.4 us  [exchange(): lax.all_to_all(array, 'pair', split_axis=0, concat_axis=0, tiled=True)]
    ppermute x2, waiting for transfers between devices: 3.08 us -> 6.16 us  [local(): recv = lax.ppermute(after(send, *moved), 'win', other_core)]
  transfers between devices with their start and end apart: 7 -> 7, of which waited for: 4 -> 5; matrix products, arithmetic and copies ran while one was open for 0% -> 1% of each run, Pallas kernels for 14% -> 15%
where the time goes in v9:
time: 252 us; the launch traced here: 251 us
  blocking collectives  135 us (54%)
  Pallas kernels  59.7 us (24%)
  waiting for transfers between devices  37 us (15%)
  starting transfers between devices  16.7 us (7%)
    all_to_all x2, blocking collectives, exchange(): lax.all_to_all(array, 'pair', split_axis=0, concat_axis=0, tiled=True)  95.7 us
    all_to_all x1, blocking collectives, local(): lax.all_to_all(pieces, ('pair', 'win'), 0, 0, tiled=True, axis_index_grou...  39.7 us
    pallas_call x2, Pallas kernels, correlate(): pl.pallas_call(functools.partial(correlate_kernel, norm), out_shape=[jax....  24.6 us
    all_to_all x2, waiting for transfers between devices, exchange(): lax.all_to_all(array, 'pair', split_axis=0, concat_axis=0, tiled=True)  24.4 us
    all_to_all x2, starting transfers between devices, exchange(): lax.all_to_all(array, 'pair', split_axis=0, concat_axis=0, tiled=True)  13.2 us
    pallas_call x2, Pallas kernels, core_sum(): pl.pallas_call(functools.partial(core_sum_kernel, task), out_shape=[jax.S...  7.62 us
    ppermute x1, waiting for transfers between devices, local(): row_recv = lax.ppermute(row_send, 'win', other_chip)  6.43 us
    pallas_call x1, Pallas kernels, gather(): pl.pallas_call(gather_kernel, out_shape=[jax.ShapeDtypeStruct(source.shap...  6.23 us
  transfers between devices with their start and end apart: 7, of which 5 were waited for; matrix products, arithmetic and copies ran while one was open for 1% of the time, Pallas kernels for 15%

profile of v9, /device:TPU:16, one launch (start us, length us, event | category | flops | bytes accessed | tf_op | source)
XLA Modules:
  0.0 251.4 jit_solution(17737825580441500144)
XLA Ops:
  0.0 5.0 %whiten.1 = bf16[32,2,96,256]{3,2,1,0:T(8,128)(2,1)} custom-call(s32[1,256]{1,0:T(1,128)} %order_ref.1, bf16[32,2,96,256]{3,2,1,0:T(8,128)(2,1)} %spectra_ref.1), custom_call_target="tpu_custom_call" | custom-call | tf_op jit(solution)/shard_map/whiten/pallas_call | solution.py:45
  5.0 49.9 %all_to_all.25.source_ref = bf16[32,192,256]{2,1,0:T(8,128)(2,1)} all-to-all(bf16[32,192,256]{2,1,0:T(8,128)(2,1)} %bitcast.5), channel_id=1, replica_groups=mesh['pair'=32,'win'=4] {'pair'}, dimensions={0} | all-to-all | bytes 6291456 | tf_op jit(solution)/shard_map/all_to_all | solution.py:528
  54.9 6.2 %gather.1 = (bf16[32,192,256]{2,1,0:T(8,128)(2,1)}, bf16[32,192,256]{2,1,0:T(8,128)(2,1)}, s32[2,32]{1,0:T(2,128)}, s32[2,32]{1,0:T(2,128)}, s32[2,32]{1,0:T(2,128)}) custom-call(s32[4,32]{1,0:T(4,128)} %partners_ref.1, bf16[32,192,256]{2,1,0:T(8,128)(2,1)} %all_to_all.25.source_ref), custom_call_target="tpu_custom_call" | custom-call | tf_op jit(solution)/shard_map/gather/pallas_call | solution.py:144
  61.1 45.7 %all_to_all.26.mate_ref = bf16[32,192,256]{2,1,0:T(8,128)(2,1)} all-to-all(bf16[32,192,256]{2,1,0:T(8,128)(2,1)} %get-tuple-element.24), channel_id=1, replica_groups=mesh['pair'=32,'win'=4] {'pair'}, dimensions={0} | all-to-all | bytes 6291456 | tf_op jit(solution)/shard_map/all_to_all | solution.py:528
  106.9 7.1 %all-to-all-start.2 = ((bf16[32,192,256]{2,1,0:T(8,128)(2,1)}), bf16[32,192,256]{2,1,0:T(8,128)(2,1)}, u32[]{:S(2)}, u32[]{:S(2)}) async-start(bf16[32,192,256]{2,1,0:T(8,128)(2,1)} %get-tuple-element.26), calls=%async_computation.2 | async-start | bytes 6291456 | tf_op jit(solution)/shard_map/all_to_all | solution.py:528
  114.0 0.6 pad_add_fusion.place_ref
  114.6 5.0 %turn.1.own_ref = bf16[32,256,192]{2,1,0:T(8,128)(2,1)} custom-call(bf16[32,192,256]{2,1,0:T(8,128)(2,1)} %bitcast.6), custom_call_target="tpu_custom_call" | custom-call | bytes 12000000 | tf_op jit(solution)/shard_map/turn/pallas_call | solution.py:73
  119.6 12.3 %correlate.2 = (f32[17,128,256]{2,1,0:T(8,128)}, bf16[17,128,256]{2,1,0:T(8,128)(2,1)}) custom-call(s32[3]{0:T(128)} %pad_add_fusion.place_ref, bf16[32,256,192]{2,1,0:T(8,128)(2,1)} %turn.1.own_ref, bf16[32,192,256]{2,1,0:T(8,128)(2,1)} %all_to_all.26.mate_ref), custom_call_target="tpu_custom_call" | custom-call | flops 1610612736 | bytes 20000000 | tf_op jit(solution)/shard_map/correlate/pallas_call | solution.py:305
  131.9 0.1 collective-permute-start
  132.0 3.1 %collective-permute-done.recv_ref = bf16[17,128,256]{2,1,0:T(8,128)(2,1)} collective-permute-done((bf16[17,128,256]{2,1,0:T(8,128)(2,1)}, bf16[17,128,256]{2,1,0:T(8,128)(2,1)}, u32[]{:S(2)}, u32[]{:S(2)}) %collective-permute-start) | collective-permute-done | bytes 1114144 | tf_op jit(solution)/shard_map/ppermute | solution.py:558
  135.1 3.8 %core_sum.2 = (f32[16,64,256]{2,1,0:T(8,128)}, bf16[16,64,256]{2,1,0:T(8,128)(2,1)}, bf16[64,2,64,128]{3,2,1,0:T(8,128)(2,1)}) custom-call(s32[3]{0:T(128)} %pad_add_fusion.place_ref, f32[17,128,256]{2,1,0:T(8,128)} %get-tuple-element.27.keep_ref, bf16[17,128,256]{2,1,0:T(8,128)(2,1)} %collective-permute-done.recv_ref), custom_call_target="tpu_custom_call" | custom-call | bytes 12000000 | tf_op jit(solution)/shard_map/core_sum/pallas_call | solution.py:388
  138.9 1.7 collective-permute-start.1
  140.6 12.9 %all-to-all-done.2.mate_ref = bf16[32,192,256]{2,1,0:T(8,128)(2,1)} async-done(((bf16[32,192,256]{2,1,0:T(8,128)(2,1)}), bf16[32,192,256]{2,1,0:T(8,128)(2,1)}, u32[]{:S(2)}, u32[]{:S(2)}) %all-to-all-start.2) | async-done | bytes 3145760 | tf_op jit(solution)/shard_map/all_to_all | solution.py:528
  153.5 12.3 %correlate.3 = (f32[17,128,256]{2,1,0:T(8,128)}, bf16[17,128,256]{2,1,0:T(8,128)(2,1)}) custom-call(s32[3]{0:T(128)} %pad_add_fusion.place_ref, bf16[32,256,192]{2,1,0:T(8,128)(2,1)} %turn.1.own_ref, bf16[32,192,256]{2,1,0:T(8,128)(2,1)} %all-to-all-done.2.mate_ref), custom_call_target="tpu_custom_call" | custom-call | flops 1610612736 | bytes 20000000 | tf_op jit(solution)/shard_map/correlate/pallas_call | solution.py:305
  165.8 0.0 collective-permute-done.1.recv_ref
  165.8 0.0 copy-start
  165.9 0.1 collective-permute-start.2
  166.0 3.1 %collective-permute-done.2.recv_ref = bf16[17,128,256]{2,1,0:T(8,128)(2,1)} collective-permute-done((bf16[17,128,256]{2,1,0:T(8,128)(2,1)}, bf16[17,128,256]{2,1,0:T(8,128)(2,1)}, u32[]{:S(2)}, u32[]{:S(2)}) %collective-permute-start.2) | collective-permute-done | bytes 1114144 | tf_op jit(solution)/shard_map/ppermute | solution.py:558
  169.0 3.8 %core_sum.3 = (f32[16,64,256]{2,1,0:T(8,128)}, bf16[16,64,256]{2,1,0:T(8,128)(2,1)}, bf16[64,2,64,128]{3,2,1,0:T(8,128)(2,1)}) custom-call(s32[3]{0:T(128)} %pad_add_fusion.place_ref, f32[17,128,256]{2,1,0:T(8,128)} %get-tuple-element.31.keep_ref, bf16[17,128,256]{2,1,0:T(8,128)(2,1)} %collective-permute-done.2.recv_ref, ...), custom_call_target="tpu_custom_call", output_to_operand_aliasing={{2}: (3, {})} | custom-call | bytes 12000000 | tf_op jit(solution)/shard_map/core_sum/pallas_call | solution.py:388
  172.9 39.7 %all_to_all.27.spread_ref = bf16[64,2,64,128]{3,2,1,0:T(8,128)(2,1)} all-to-all(bf16[64,2,64,128]{3,2,1,0:T(8,128)(2,1)} %get-tuple-element.38), channel_id=1, replica_groups={{0,4,8,12,16,20,24,28,32,36,40,44,48,52,56,60,64,68,72,76,80,84,88,92,9..., dimensions={0} | all-to-all | bytes 4194304 | tf_op jit(solution)/shard_map/all_to_all | solution.py:566
  212.6 0.0 copy-done
  212.6 2.6 %gather_sum.1 = bf16[32,2,64,128]{3,2,1,0:T(8,128)(2,1)} custom-call(s32[2,32]{1,0:T(2,128)} %get-tuple-element.37.index_ref, bf16[64,2,64,128]{3,2,1,0:T(8,128)(2,1)} %all_to_all.27.spread_ref), custom_call_target="tpu_custom_call" | custom-call | tf_op jit(solution)/shard_map/gather_sum/pallas_call | solution.py:431
  215.2 6.1 %all-to-all-start.4 = ((bf16[32,2,64,128]{3,2,1,0:T(8,128)(2,1)}), bf16[32,2,64,128]{3,2,1,0:T(8,128)(2,1)}, u32[]{:S(2)}, u32[]{:S(2)}) async-start(bf16[32,2,64,128]{3,2,1,0:T(8,128)(2,1)} %gather_sum.1), calls=%async_computation.4 | async-start | bytes 2097152 | tf_op jit(solution)/shard_map/all_to_all | solution.py:528
  221.3 3.3 %own_rows.1.in_ref = f32[64,4,16,256]{3,2,1,0:T(8,128)} custom-call(s32[2,32]{1,0:T(2,128)} %get-tuple-element.23.flip_ref, s32[3]{0:T(128)} %pad_add_fusion.place_ref, f32[16,64,256]{2,1,0:T(8,128)} %get-tuple-element.39.own_ref, bf16[16,64,256]{2,1,0:T(8,128)(2,1)} %copy-done), custom_call_target="tpu_custom_call" | custom-call | bytes 5000000 | tf_op jit(solution)/shard_map/own_rows/pallas_call | solution.py:455
  224.5 1.6 collective-permute-start.3
  226.1 11.4 %all-to-all-done.4.near_ref = bf16[32,2,64,128]{3,2,1,0:T(8,128)(2,1)} async-done(((bf16[32,2,64,128]{3,2,1,0:T(8,128)(2,1)}), bf16[32,2,64,128]{3,2,1,0:T(8,128)(2,1)}, u32[]{:S(2)}, u32[]{:S(2)}) %all-to-all-start.4) | async-done | bytes 1048608 | tf_op jit(solution)/shard_map/all_to_all | solution.py:528
  237.5 1.1 slice.4
  238.6 0.1 collective-permute-start.4
  238.7 6.4 %collective-permute-done.3.recv_ref = bf16[16,64,256]{2,1,0:T(8,128)(2,1)S(1)} collective-permute-done((bf16[16,64,256]{2,1,0:T(8,128)(2,1)}, bf16[16,64,256]{2,1,0:T(8,128)(2,1)S(1)}, u32[]{:S(2)}, u32[]{:S(2)}) %collective-permute-start.3) | collective-permute-done | bytes 524320 | tf_op jit(solution)/shard_map/ppermute | solution.py:569
  245.1 0.0 copy-start.1
  245.1 0.0 collective-permute-done.4.far_ref
  245.2 0.8 copy-done.1
  246.0 5.4 %last_rows.1 = f32[64,4,16,256]{3,2,1,0:T(8,128)} custom-call(s32[2,32]{1,0:T(2,128)} %get-tuple-element.23.flip_ref, s32[3]{0:T(128)} %pad_add_fusion.place_ref, f32[16,64,256]{2,1,0:T(8,128)} %get-tuple-element.35.own_ref, bf16[16,64,256]{2,1,0:T(8,128)(2,1)} %copy-done.1, ...), custom_call_target="tpu_custom_call", output_to_operand_aliasing={{}: (6, {})} | custom-call | tf_op jit(solution)/shard_map/last_rows/pallas_call | solution.py:512
Async XLA Ops:
  106.9 46.7 %all-to-all-start.2 = ((bf16[32,192,256]{2,1,0:T(8,128)(2,1)}), bf16[32,192,256]{2,1,0:T(8,128)(2,1)}, u32[]{:S(2)}, u32[]{:S(2)}) async-start(bf16[32,192,256]{2,1,0:T(8,128)(2,1)} %get-tuple-element.26), calls=%async_computation.2 | async-start | bytes 6291456 | tf_op jit(solution)/shard_map/all_to_all | solution.py:528
  131.9 3.2 %collective-permute-start = (bf16[17,128,256]{2,1,0:T(8,128)(2,1)}, bf16[17,128,256]{2,1,0:T(8,128)(2,1)}, u32[]{:S(2)}, u32[]{:S(2)}) collective-permute-start(bf16[17,128,256]{2,1,0:T(8,128)(2,1)} %get-tuple-element.28), channel_id=1, source_target_pairs={{0,1},{1,0},{2,3},{3,2},{4,5},{5,4},{6,7},{7,6},{8,9},{9,8},{10,11... | collective-permute-start | bytes 3342344 | tf_op jit(solution)/shard_map/ppermute | solution.py:558
  138.9 26.9 %collective-permute-start.1 = (bf16[16,64,256]{2,1,0:T(8,128)(2,1)}, bf16[16,64,256]{2,1,0:T(8,128)(2,1)S(1)}, u32[]{:S(2)}, u32[]{:S(2)}) collective-permute-start(bf16[16,64,256]{2,1,0:T(8,128)(2,1)} %get-tuple-element.29), channel_id=1, source_target_pairs={{0,2},{1,3},{2,0},{3,1},{4,6},{5,7},{6,4},{7,5},{8,10},{9,11},{10,... | collective-permute-start | bytes 1572872 | tf_op jit(solution)/shard_map/ppermute | solution.py:563
  165.8 46.7 %copy-start = (bf16[16,64,256]{2,1,0:T(8,128)(2,1)}, bf16[16,64,256]{2,1,0:T(8,128)(2,1)S(1)}, u32[]{:S(2)}) copy-start(bf16[16,64,256]{2,1,0:T(8,128)(2,1)S(1)} %collective-permute-done.1.recv_ref) | copy-start | bytes 1572868
  165.9 3.2 %collective-permute-start.2 = (bf16[17,128,256]{2,1,0:T(8,128)(2,1)}, bf16[17,128,256]{2,1,0:T(8,128)(2,1)}, u32[]{:S(2)}, u32[]{:S(2)}) collective-permute-start(bf16[17,128,256]{2,1,0:T(8,128)(2,1)} %get-tuple-element.33), channel_id=1, source_target_pairs={{0,1},{1,0},{2,3},{3,2},{4,5},{5,4},{6,7},{7,6},{8,9},{9,8},{10,11... | collective-permute-start | bytes 3342344 | tf_op jit(solution)/shard_map/ppermute | solution.py:558
  215.2 22.4 %all-to-all-start.4 = ((bf16[32,2,64,128]{3,2,1,0:T(8,128)(2,1)}), bf16[32,2,64,128]{3,2,1,0:T(8,128)(2,1)}, u32[]{:S(2)}, u32[]{:S(2)}) async-start(bf16[32,2,64,128]{3,2,1,0:T(8,128)(2,1)} %gather_sum.1), calls=%async_computation.4 | async-start | bytes 2097152 | tf_op jit(solution)/shard_map/all_to_all | solution.py:528
  224.5 20.6 %collective-permute-start.3 = (bf16[16,64,256]{2,1,0:T(8,128)(2,1)}, bf16[16,64,256]{2,1,0:T(8,128)(2,1)S(1)}, u32[]{:S(2)}, u32[]{:S(2)}) collective-permute-start(bf16[16,64,256]{2,1,0:T(8,128)(2,1)} %get-tuple-element.36), channel_id=1, source_target_pairs={{0,2},{1,3},{2,0},{3,1},{4,6},{5,7},{6,4},{7,5},{8,10},{9,11},{10,... | collective-permute-start | bytes 1572872 | tf_op jit(solution)/shard_map/ppermute | solution.py:569
  238.6 6.5 %collective-permute-start.4 = (bf16[16,2,64,128]{3,2,1,0:T(8,128)(2,1)S(1)}, bf16[16,2,64,128]{3,2,1,0:T(8,128)(2,1)}, u32[]{:S(2)}, u32[]{:S(2)}) collective-permute-start(bf16[16,2,64,128]{3,2,1,0:T(8,128)(2,1)S(1)} %slice.4), channel_id=1, source_target_pairs={{0,1},{1,0},{2,3},{3,2},{4,5},{5,4},{6,7},{7,6},{8,9},{9,8},{10,11... | collective-permute-start | bytes 1572872 | tf_op jit(solution)/shard_map/ppermute | solution.py:571
  245.1 0.8 copy-start.1

commit v10 on v8

--- a/solution.py
+++ b/solution.py
@@ -150,7 +150,7 @@
             pltpu.VMEM(source.shape, source.dtype),
             pltpu.VMEM((tasks,) + source.shape, source.dtype),
             pltpu.SemaphoreType.DMA((1,)),
-            pltpu.SemaphoreType.DMA((tasks, 4)),
+            pltpu.SemaphoreType.DMA((tasks, 2)),
         ],
         compiler_params=params(),
         name="gather",
@@ -400,9 +400,9 @@
             pltpu.VMEM(part, f32),
             pltpu.VMEM(part, bf16),
             pltpu.VMEM((count,) + piece, bf16),
-            pltpu.SemaphoreType.DMA((2, 4)),
-            pltpu.SemaphoreType.DMA((2, 4)),
-            pltpu.SemaphoreType.DMA((4, 4)),
+            pltpu.SemaphoreType.DMA((2, 2)),
+            pltpu.SemaphoreType.DMA((2, 2)),
+            pltpu.SemaphoreType.DMA((4, 2)),
         ],
         input_output_aliases={3: 2} if extra else {},
         compiler_params=params(),

time: 251 us -> 252 us (level)
  no operation moved by 1% of the time
where the time goes in v10:
time: 252 us; the launch traced here: 251 us
  blocking collectives  135 us (54%)
  Pallas kernels  57.8 us (23%)
  waiting for transfers between devices  37.8 us (15%)
  starting transfers between devices  16.8 us (7%)
    all_to_all x2, blocking collectives, exchange(): lax.all_to_all(array, 'pair', split_axis=0, concat_axis=0, tiled=True)  95.7 us
    all_to_all x1, blocking collectives, local(): lax.all_to_all(after(pieces, out), ('pair', 'win'), 0, 0, tiled=True, axi...  39.5 us
    all_to_all x2, waiting for transfers between devices, exchange(): lax.all_to_all(array, 'pair', split_axis=0, concat_axis=0, tiled=True)  28.3 us
    pallas_call x2, Pallas kernels, correlate(): pl.pallas_call(functools.partial(correlate_kernel, norm), out_shape=[jax....  22.2 us
    all_to_all x2, starting transfers between devices, exchange(): lax.all_to_all(array, 'pair', split_axis=0, concat_axis=0, tiled=True)  13 us
    pallas_call x2, Pallas kernels, core_sum(): pl.pallas_call(functools.partial(core_sum_kernel, task), out_shape=[jax.S...  8.07 us
    ppermute x1, waiting for transfers between devices, local(): row_recv = lax.ppermute(row_send, 'win', other_chip)  6.42 us
    pallas_call x1, Pallas kernels, gather(): pl.pallas_call(gather_kernel, out_shape=[jax.ShapeDtypeStruct(source.shap...  6.32 us
  transfers between devices with their start and end apart: 7, of which 4 were waited for; matrix products, arithmetic and copies ran while one was open for 0% of the time, Pallas kernels for 14%

profile of v10, /device:TPU:16, one launch (start us, length us, event | category | flops | bytes accessed | tf_op | source)
XLA Modules:
  0.0 250.7 jit_solution(16373170786277178219)
XLA Ops:
  0.0 5.0 %whiten.1 = bf16[32,2,96,256]{3,2,1,0:T(8,128)(2,1)} custom-call(s32[1,256]{1,0:T(1,128)} %order_ref.1, bf16[32,2,96,256]{3,2,1,0:T(8,128)(2,1)} %spectra_ref.1), custom_call_target="tpu_custom_call" | custom-call | tf_op jit(solution)/shard_map/whiten/pallas_call | solution.py:45
  5.0 49.9 %all_to_all.25.source_ref = bf16[32,192,256]{2,1,0:T(8,128)(2,1)} all-to-all(bf16[32,192,256]{2,1,0:T(8,128)(2,1)} %bitcast.5), channel_id=1, replica_groups=mesh['pair'=32,'win'=4] {'pair'}, dimensions={0} | all-to-all | bytes 6291456 | tf_op jit(solution)/shard_map/all_to_all | solution.py:528
  55.0 6.3 %gather.1 = (bf16[32,192,256]{2,1,0:T(8,128)(2,1)}, bf16[32,192,256]{2,1,0:T(8,128)(2,1)}, s32[2,32]{1,0:T(2,128)}, s32[2,32]{1,0:T(2,128)}, s32[2,32]{1,0:T(2,128)}) custom-call(s32[4,32]{1,0:T(4,128)} %partners_ref.1, bf16[32,192,256]{2,1,0:T(8,128)(2,1)} %all_to_all.25.source_ref), custom_call_target="tpu_custom_call" | custom-call | tf_op jit(solution)/shard_map/gather/pallas_call | solution.py:144
  61.3 45.7 %all_to_all.26.mate_ref = bf16[32,192,256]{2,1,0:T(8,128)(2,1)} all-to-all(bf16[32,192,256]{2,1,0:T(8,128)(2,1)} %get-tuple-element.24), channel_id=1, replica_groups=mesh['pair'=32,'win'=4] {'pair'}, dimensions={0} | all-to-all | bytes 6291456 | tf_op jit(solution)/shard_map/all_to_all | solution.py:528
  107.0 7.2 %all-to-all-start.2 = ((bf16[32,192,256]{2,1,0:T(8,128)(2,1)}), bf16[32,192,256]{2,1,0:T(8,128)(2,1)}, u32[]{:S(2)}, u32[]{:S(2)}) async-start(bf16[32,192,256]{2,1,0:T(8,128)(2,1)} %get-tuple-element.26), calls=%async_computation.2 | async-start | bytes 6291456 | tf_op jit(solution)/shard_map/all_to_all | solution.py:528
  114.2 0.7 pad_add_fusion.place_ref
  114.9 5.0 %turn.1.own_ref = bf16[32,256,192]{2,1,0:T(8,128)(2,1)} custom-call(bf16[32,192,256]{2,1,0:T(8,128)(2,1)} %bitcast.6), custom_call_target="tpu_custom_call" | custom-call | bytes 12000000 | tf_op jit(solution)/shard_map/turn/pallas_call | solution.py:73
  119.8 11.1 %correlate.2 = (f32[17,128,256]{2,1,0:T(8,128)}, bf16[17,128,256]{2,1,0:T(8,128)(2,1)}) custom-call(s32[3]{0:T(128)} %pad_add_fusion.place_ref, bf16[32,256,192]{2,1,0:T(8,128)(2,1)} %turn.1.own_ref, bf16[32,192,256]{2,1,0:T(8,128)(2,1)} %all_to_all.26.mate_ref), custom_call_target="tpu_custom_call" | custom-call | flops 1610612736 | bytes 20000000 | tf_op jit(solution)/shard_map/correlate/pallas_call | solution.py:305
  130.9 0.1 collective-permute-start
  131.0 3.1 %collective-permute-done.recv_ref = bf16[17,128,256]{2,1,0:T(8,128)(2,1)} collective-permute-done((bf16[17,128,256]{2,1,0:T(8,128)(2,1)}, bf16[17,128,256]{2,1,0:T(8,128)(2,1)}, u32[]{:S(2)}, u32[]{:S(2)}) %collective-permute-start) | collective-permute-done | bytes 1114144 | tf_op jit(solution)/shard_map/ppermute | solution.py:558
  134.1 4.1 %core_sum.2 = (f32[16,64,256]{2,1,0:T(8,128)}, bf16[16,64,256]{2,1,0:T(8,128)(2,1)}, bf16[64,2,64,128]{3,2,1,0:T(8,128)(2,1)}) custom-call(s32[3]{0:T(128)} %pad_add_fusion.place_ref, f32[17,128,256]{2,1,0:T(8,128)} %get-tuple-element.27.keep_ref, bf16[17,128,256]{2,1,0:T(8,128)(2,1)} %collective-permute-done.recv_ref), custom_call_target="tpu_custom_call" | custom-call | bytes 12000000 | tf_op jit(solution)/shard_map/core_sum/pallas_call | solution.py:388
  138.2 1.5 collective-permute-start.1
  139.7 14.0 %all-to-all-done.2.mate_ref = bf16[32,192,256]{2,1,0:T(8,128)(2,1)} async-done(((bf16[32,192,256]{2,1,0:T(8,128)(2,1)}), bf16[32,192,256]{2,1,0:T(8,128)(2,1)}, u32[]{:S(2)}, u32[]{:S(2)}) %all-to-all-start.2) | async-done | bytes 3145760 | tf_op jit(solution)/shard_map/all_to_all | solution.py:528
  153.7 11.1 %correlate.3 = (f32[17,128,256]{2,1,0:T(8,128)}, bf16[17,128,256]{2,1,0:T(8,128)(2,1)}) custom-call(s32[3]{0:T(128)} %pad_add_fusion.place_ref, bf16[32,256,192]{2,1,0:T(8,128)(2,1)} %turn.1.own_ref, bf16[32,192,256]{2,1,0:T(8,128)(2,1)} %all-to-all-done.2.mate_ref), custom_call_target="tpu_custom_call" | custom-call | flops 1610612736 | bytes 20000000 | tf_op jit(solution)/shard_map/correlate/pallas_call | solution.py:305
  164.7 0.0 collective-permute-done.1.recv_ref
  164.7 0.0 copy-start.2
  164.7 0.3 collective-permute-start.2
  165.0 0.5 copy-done.2
  165.5 3.3 %own_rows.1.in_ref = f32[64,4,16,256]{3,2,1,0:T(8,128)} custom-call(s32[2,32]{1,0:T(2,128)} %get-tuple-element.23.flip_ref, s32[3]{0:T(128)} %pad_add_fusion.place_ref, f32[16,64,256]{2,1,0:T(8,128)} %get-tuple-element.39.own_ref, bf16[16,64,256]{2,1,0:T(8,128)(2,1)} %copy-done.2), custom_call_target="tpu_custom_call" | custom-call | bytes 5000000 | tf_op jit(solution)/shard_map/own_rows/pallas_call | solution.py:455
  168.8 0.0 collective-permute-done.2.recv_ref
  168.8 4.0 %core_sum.3 = (f32[16,64,256]{2,1,0:T(8,128)}, bf16[16,64,256]{2,1,0:T(8,128)(2,1)}, bf16[64,2,64,128]{3,2,1,0:T(8,128)(2,1)}) custom-call(s32[3]{0:T(128)} %pad_add_fusion.place_ref, f32[17,128,256]{2,1,0:T(8,128)} %get-tuple-element.31.keep_ref, bf16[17,128,256]{2,1,0:T(8,128)(2,1)} %collective-permute-done.2.recv_ref, ...), custom_call_target="tpu_custom_call", output_to_operand_aliasing={{2}: (3, {})} | custom-call | bytes 12000000 | tf_op jit(solution)/shard_map/core_sum/pallas_call | solution.py:388
  172.8 39.5 %all_to_all.27.spread_ref = bf16[64,2,64,128]{3,2,1,0:T(8,128)(2,1)} all-to-all(bf16[64,2,64,128]{3,2,1,0:T(8,128)(2,1)} %get-tuple-element.40), channel_id=1, replica_groups={{0,4,8,12,16,20,24,28,32,36,40,44,48,52,56,60,64,68,72,76,80,84,88,92,9..., dimensions={0} | all-to-all | bytes 4194304 | tf_op jit(solution)/shard_map/all_to_all | solution.py:566
  212.4 2.6 %gather_sum.1 = bf16[32,2,64,128]{3,2,1,0:T(8,128)(2,1)} custom-call(s32[2,32]{1,0:T(2,128)} %get-tuple-element.37.index_ref, bf16[64,2,64,128]{3,2,1,0:T(8,128)(2,1)} %all_to_all.27.spread_ref), custom_call_target="tpu_custom_call" | custom-call | tf_op jit(solution)/shard_map/gather_sum/pallas_call | solution.py:431
  214.9 5.8 %all-to-all-start.4 = ((bf16[32,2,64,128]{3,2,1,0:T(8,128)(2,1)}), bf16[32,2,64,128]{3,2,1,0:T(8,128)(2,1)S(1)}, u32[]{:S(2)}, u32[]{:S(2)}) async-start(bf16[32,2,64,128]{3,2,1,0:T(8,128)(2,1)} %gather_sum.1), calls=%async_computation.4 | async-start | bytes 2097152 | tf_op jit(solution)/shard_map/all_to_all | solution.py:528
  220.8 1.8 collective-permute-start.3
  222.6 14.3 %all-to-all-done.4.near_ref = bf16[32,2,64,128]{3,2,1,0:T(8,128)(2,1)S(1)} async-done(((bf16[32,2,64,128]{3,2,1,0:T(8,128)(2,1)}), bf16[32,2,64,128]{3,2,1,0:T(8,128)(2,1)S(1)}, u32[]{:S(2)}, u32[]{:S(2)}) %all-to-all-start.4) | async-done | bytes 1048608 | tf_op jit(solution)/shard_map/all_to_all | solution.py:528
  236.9 0.0 copy-start
  236.9 1.0 copy-done
  237.9 0.1 collective-permute-start.4
  238.0 6.4 %collective-permute-done.3.recv_ref = bf16[16,64,256]{2,1,0:T(8,128)(2,1)S(1)} collective-permute-done((bf16[16,64,256]{2,1,0:T(8,128)(2,1)}, bf16[16,64,256]{2,1,0:T(8,128)(2,1)S(1)}, u32[]{:S(2)}, u32[]{:S(2)}) %collective-permute-start.3) | collective-permute-done | bytes 524320 | tf_op jit(solution)/shard_map/ppermute | solution.py:569
  244.4 0.0 copy-start.1
  244.4 0.0 collective-permute-done.4.far_ref
  244.4 0.8 copy-done.1
  245.2 5.4 %last_rows.1 = f32[64,4,16,256]{3,2,1,0:T(8,128)} custom-call(s32[2,32]{1,0:T(2,128)} %get-tuple-element.23.flip_ref, s32[3]{0:T(128)} %pad_add_fusion.place_ref, f32[16,64,256]{2,1,0:T(8,128)} %get-tuple-element.35.own_ref, bf16[16,64,256]{2,1,0:T(8,128)(2,1)} %copy-done.1, bf16[32,2,64,128]{3,2,1,0:T(8,128)(2,1)} %copy-done, ...), custom_call_target="tpu_custom_call", output_to_operand_aliasing={{}: (6, {})} | custom-call | tf_op jit(solution)/shard_map/last_rows/pallas_call | solution.py:512
  (1 shorter events, 0.0 us)
Async XLA Ops:
  107.0 46.7 %all-to-all-start.2 = ((bf16[32,192,256]{2,1,0:T(8,128)(2,1)}), bf16[32,192,256]{2,1,0:T(8,128)(2,1)}, u32[]{:S(2)}, u32[]{:S(2)}) async-start(bf16[32,192,256]{2,1,0:T(8,128)(2,1)} %get-tuple-element.26), calls=%async_computation.2 | async-start | bytes 6291456 | tf_op jit(solution)/shard_map/all_to_all | solution.py:528
  130.9 3.2 %collective-permute-start = (bf16[17,128,256]{2,1,0:T(8,128)(2,1)}, bf16[17,128,256]{2,1,0:T(8,128)(2,1)}, u32[]{:S(2)}, u32[]{:S(2)}) collective-permute-start(bf16[17,128,256]{2,1,0:T(8,128)(2,1)} %get-tuple-element.28), channel_id=1, source_target_pairs={{0,1},{1,0},{2,3},{3,2},{4,5},{5,4},{6,7},{7,6},{8,9},{9,8},{10,11... | collective-permute-start | bytes 3342344 | tf_op jit(solution)/shard_map/ppermute | solution.py:558
  138.2 26.6 %collective-permute-start.1 = (bf16[16,64,256]{2,1,0:T(8,128)(2,1)}, bf16[16,64,256]{2,1,0:T(8,128)(2,1)S(1)}, u32[]{:S(2)}, u32[]{:S(2)}) collective-permute-start(bf16[16,64,256]{2,1,0:T(8,128)(2,1)} %get-tuple-element.29), channel_id=1, source_target_pairs={{0,2},{1,3},{2,0},{3,1},{4,6},{5,7},{6,4},{7,5},{8,10},{9,11},{10,... | collective-permute-start | bytes 1572872 | tf_op jit(solution)/shard_map/ppermute | solution.py:563
  164.7 0.8 copy-start.2
  164.7 4.1 %collective-permute-start.2 = (bf16[17,128,256]{2,1,0:T(8,128)(2,1)}, bf16[17,128,256]{2,1,0:T(8,128)(2,1)}, u32[]{:S(2)}, u32[]{:S(2)}) collective-permute-start(bf16[17,128,256]{2,1,0:T(8,128)(2,1)} %get-tuple-element.33), channel_id=1, source_target_pairs={{0,1},{1,0},{2,3},{3,2},{4,5},{5,4},{6,7},{7,6},{8,9},{9,8},{10,11... | collective-permute-start | bytes 3342344 | tf_op jit(solution)/shard_map/ppermute | solution.py:558
  214.9 21.9 %all-to-all-start.4 = ((bf16[32,2,64,128]{3,2,1,0:T(8,128)(2,1)}), bf16[32,2,64,128]{3,2,1,0:T(8,128)(2,1)S(1)}, u32[]{:S(2)}, u32[]{:S(2)}) async-start(bf16[32,2,64,128]{3,2,1,0:T(8,128)(2,1)} %gather_sum.1), calls=%async_computation.4 | async-start | bytes 2097152 | tf_op jit(solution)/shard_map/all_to_all | solution.py:528
  220.8 23.6 %collective-permute-start.3 = (bf16[16,64,256]{2,1,0:T(8,128)(2,1)}, bf16[16,64,256]{2,1,0:T(8,128)(2,1)S(1)}, u32[]{:S(2)}, u32[]{:S(2)}) collective-permute-start(bf16[16,64,256]{2,1,0:T(8,128)(2,1)} %get-tuple-element.36), channel_id=1, source_target_pairs={{0,2},{1,3},{2,0},{3,1},{4,6},{5,7},{6,4},{7,5},{8,10},{9,11},{10,... | collective-permute-start | bytes 1572872 | tf_op jit(solution)/shard_map/ppermute | solution.py:569
  236.9 1.0 copy-start
  237.9 6.5 %collective-permute-start.4 = (bf16[16,2,64,128]{3,2,1,0:T(8,128)(2,1)S(1)}, bf16[16,2,64,128]{3,2,1,0:T(8,128)(2,1)}, u32[]{:S(2)}, u32[]{:S(2)}) collective-permute-start(bf16[16,2,64,128]{3,2,1,0:T(8,128)(2,1)S(1)} %slice.4), channel_id=1, source_target_pairs={{0,1},{1,0},{2,3},{3,2},{4,5},{5,4},{6,7},{7,6},{8,9},{9,8},{10,11... | collective-permute-start | bytes 1572872 | tf_op jit(solution)/shard_map/ppermute | solution.py:571
  244.4 0.8 copy-start.1
